TPU v7x, 32 devices: a whole 2x2x4 slice. The times are simulated.
32 devices in a mesh: ta: 2 (over core), ha: 4 (over y, x), wa: 4 (over z).
Axes of the slice: x: 2, y: 2, z: 4, core: 2. Of those that a mesh axis runs over, the one named last changes fastest.
Arguments:
- queries: bfloat16 [2, 4, 4, 24, 1536], P('ta', 'ha', 'wa'), may hold values from -6 to 6
- current_kv: bfloat16 [2, 4, 4, 2, 24, 1536], P('ta', 'ha', 'wa'), may hold values from -18 to 18
- stale_kv: bfloat16 [2, 4, 4, 2, 24, 1536], P('ta', 'ha', 'wa'), may hold values from -18 to 18
- text_kv: bfloat16 [2, 16, 1536], P(None, 'wa'), may hold values from -18 to 18
- q_gain: float32 [128], replicated, may hold values from 0.8 to 1.8
- k_gain: float32 [128], replicated, may hold values from 0.8 to 1.8
- pattern: int32 [2, 4, 4, 27], P('ta', 'ha', 'wa'), may hold values 0 or 1
Outputs:
- attended: bfloat16 [2, 4, 4, 24, 1536], P('ta', 'ha', 'wa')
Inputs may be any that keep to these rules, and one draw needn't show every extreme that they name: pattern holds 0 or 1; its entry 13 and entries pointing out of the grid are not read.
All inputs are finite; a program needn't handle non-finite values. No bound on the sum of `pattern` on one device may be relied on, other than what follows from the above.
Results may differ from a plain program's by a relative error of at most 0.0082.
Values may be sent and summed in bfloat16 or wider, within the bound.
No kernel may reach another device: no remote copies, remote signals or barrier semaphores. Data moves between devices by JAX's collectives and lax.ppermute only.
A program may use at most 64 MiB of HBM per device.

v0:
```python
import jax
import jax.numpy as jnp
import numpy as np
from jax import lax
from jax.sharding import PartitionSpec as P

offset_t = np.array([o // 9 - 1 for o in range(27)])
offset_h = np.array([o // 3 % 3 - 1 for o in range(27)])
offset_w = np.array([o % 3 - 1 for o in range(27)])


def with_halo(cells, sides, width):
    for axis, dim in sides:
        count = lax.axis_size(axis)
        ends = count - 1
        head = lax.slice_in_dim(cells, 0, width, axis=dim)
        tail = lax.slice_in_dim(cells, cells.shape[dim] - width, cells.shape[dim], axis=dim)
        cells = jnp.concatenate(
            [
                lax.ppermute(tail, axis, [(i, (i + 1) % count) for i in range(ends)]),
                cells,
                lax.ppermute(head, axis, [((i + 1) % count, i) for i in range(ends)]),
            ],
            axis=dim,
        )
    return cells


def qk_normed(values, gain, heads):
    shaped = values.astype(jnp.float32).reshape(values.shape[:-1] + (heads, gain.shape[0]))
    square = jnp.mean(shaped * shaped, axis=-1, keepdims=True)
    return (shaped * lax.rsqrt(square + 1e-06) * gain).reshape(values.shape).astype(jnp.bfloat16)


def shards(queries, current_kv, stale_kv, text_kv, q_gain, k_gain, pattern):
    tile = queries.shape[3]
    width = queries.shape[4]
    head_dim = q_gain.shape[0]
    heads = width // head_dim
    scale = head_dim ** (-0.5)
    query_rows = qk_normed(queries[0, 0, 0], q_gain, heads).reshape(tile, heads, head_dim)
    local_keys = qk_normed(current_kv[0, 0, 0, 0], k_gain, heads)
    text_send = jnp.stack([qk_normed(text_kv[0], k_gain, heads), text_kv[1]])
    piece = lax.all_gather(text_send, "wa", axis=1, tiled=True)
    keys = piece[0].reshape(-1, heads, head_dim)
    vals = piece[1].reshape(-1, heads, head_dim)
    text_scores = (
        jnp.einsum("qhd,khd->hqk", query_rows, keys, preferred_element_type=jnp.float32) * scale
    )
    text_expo = jnp.exp(text_scores)
    weight = jnp.sum(text_expo, axis=-1)
    total = jnp.einsum(
        "hqk,khd->qhd", text_expo.astype(jnp.bfloat16), vals, preferred_element_type=jnp.float32
    )
    text_total = total
    text_weight = weight
    extended = with_halo(stale_kv, (("ta", 0), ("ha", 1), ("wa", 2)), 1)
    near_keys = qk_normed(extended[:, :, :, 0], k_gain, heads)
    near_keys = near_keys.at[1, 1, 1].set(local_keys)
    near_vals = extended[:, :, :, 1].at[1, 1, 1].set(current_kv[0, 0, 0, 1])
    near_keys = near_keys.reshape(27 * tile, heads, head_dim)
    near_vals = near_vals.reshape(27 * tile, heads, head_dim)
    place_t = lax.axis_index("ta") + jnp.asarray(offset_t, jnp.int32)
    place_h = lax.axis_index("ha") + jnp.asarray(offset_h, jnp.int32)
    place_w = lax.axis_index("wa") + jnp.asarray(offset_w, jnp.int32)
    inside = (
        (place_t >= 0)
        & (place_t < lax.axis_size("ta"))
        & (place_h >= 0)
        & (place_h < lax.axis_size("ha"))
    )
    inside = inside & (place_w >= 0) & (place_w < lax.axis_size("wa"))
    chosen = inside & ((pattern[0, 0, 0] == 1) | (jnp.arange(27) == 13))
    key_mask = jnp.repeat(chosen, tile)
    totals = []
    weights = []
    for first in range(0, heads, 4):
        last = min(first + 4, heads)
        scores = (
            jnp.einsum(
                "qhd,khd->hqk",
                query_rows[:, first:last],
                near_keys[:, first:last],
                preferred_element_type=jnp.float32,
            )
            * scale
        )
        expo = jnp.where(key_mask[None, None, :], jnp.exp(scores), 0.0)
        weights.append(jnp.sum(expo, axis=-1))
        totals.append(
            jnp.einsum(
                "hqk,khd->qhd",
                expo.astype(jnp.bfloat16),
                near_vals[:, first:last],
                preferred_element_type=jnp.float32,
            )
        )
    total = jnp.concatenate(totals, axis=1) + text_total
    weight = jnp.concatenate(weights, axis=0) + text_weight
    result = total / weight.T[:, :, None]
    return result.reshape(1, 1, 1, tile, width).astype(jnp.bfloat16)


def solution(mesh):
    return jax.shard_map(
        shards,
        mesh=mesh,
        in_specs=(
            P("ta", "ha", "wa", None, None),
            P("ta", "ha", "wa", None, None, None),
            P("ta", "ha", "wa", None, None, None),
            P(None, "wa", None),
            P(),
            P(),
            P("ta", "ha", "wa", None),
        ),
        out_specs=P("ta", "ha", "wa", None, None),
        check_vma=False,
    )
```

profile of v0, /device:TPU:0, one launch (start us, length us, event | category | flops | bytes accessed | tf_op | source)
XLA Modules:
  0.0 124.1 jit_solution(8134756490613881225)
XLA Ops:
  0.0 0.0 copy-start
  0.0 2.5 %collective-permute-start = (bf16[1,1,1,2,24,1536]{5,4,2,1,0,3:T(8,128)(2,1)}, bf16[1,1,1,2,24,1536]{5,4,2,1,0,3:T(8,128)(2,1)S(1)}, u32[]{:S(2)}, u32[]{:S(2)}) collective-permute-start(bf16[1,1,1,2,24,1536]{5,4,2,1,0,3:T(8,128)(2,1)} %bitcast.83), channel_id=1, source_target_pairs={{0,16},{1,17},{2,18},{3,19},{4,20},{5,21},{6,22},{7,23},{8,24},{9,... | collective-permute-start | bytes 442376 | tf_op jit(solution)/shard_map/ppermute | solution.py:20
  2.5 1.3 %collective-permute-start.1 = (bf16[1,1,1,2,24,1536]{5,4,2,1,0,3:T(8,128)(2,1)}, bf16[1,1,1,2,24,1536]{5,4,2,1,0,3:T(8,128)(2,1)S(1)}, u32[]{:S(2)}, u32[]{:S(2)}) collective-permute-start(bf16[1,1,1,2,24,1536]{5,4,2,1,0,3:T(8,128)(2,1)} %bitcast.84), channel_id=1, source_target_pairs={{16,0},{17,1},{18,2},{19,3},{20,4},{21,5},{22,6},{23,7},{24,8},{25... | collective-permute-start | bytes 442376 | tf_op jit(solution)/shard_map/ppermute | solution.py:22
  3.8 0.9 convert_multiply_fusion.1
  4.8 0.0 copy-start.6
  4.8 0.0 slice-start
  4.8 0.1 reduce_sum.74
  4.9 0.7 convert_multiply_fusion.3
  5.7 0.0 copy-start.7
  5.7 1.0 reshape.229
  6.7 0.1 reduce_sum.75
  6.8 0.1 multiply_reduce_fusion
  6.9 0.0 copy-start.4
  6.9 0.0 collective-permute-done
  6.9 0.0 collective-permute-done.1
  6.9 1.0 pad_maximum_fusion.2
  7.9 4.3 %collective-permute-start.2 = (bf16[3,1,1,2,24,1536]{5,4,2,1,0,3:T(8,128)(2,1)S(1)}, bf16[3,1,1,2,24,1536]{5,4,2,1,0,3:T(8,128)(2,1)S(1)}, u32[]{:S(2)}, u32[]{:S(2)}) collective-permute-start(bf16[3,1,1,2,24,1536]{5,4,2,1,0,3:T(8,128)(2,1)S(1)} %pad_maximum_fusion.2), channel_id=1, source_target_pairs={{0,4},{4,8},{8,12},{1,5},{5,9},{9,13},{2,6},{6,10},{10,14},{3,7},{... | collective-permute-start | bytes 1327112 | tf_op jit(solution)/shard_map/ppermute | solution.py:20
  12.2 1.3 %collective-permute-start.3 = (bf16[3,1,1,2,24,1536]{5,4,2,1,0,3:T(8,128)(2,1)S(1)}, bf16[3,1,1,2,24,1536]{5,4,2,1,0,3:T(8,128)(2,1)S(1)}, u32[]{:S(2)}, u32[]{:S(2)}) collective-permute-start(bf16[3,1,1,2,24,1536]{5,4,2,1,0,3:T(8,128)(2,1)S(1)} %pad_maximum_fusion.2), channel_id=1, source_target_pairs={{4,0},{8,4},{12,8},{5,1},{9,5},{13,9},{6,2},{10,6},{14,10},{7,3},{... | collective-permute-start | bytes 1327112 | tf_op jit(solution)/shard_map/ppermute | solution.py:22
  13.5 9.0 %collective-permute-done.2 = bf16[3,1,1,2,24,1536]{5,4,2,1,0,3:T(8,128)(2,1)S(1)} collective-permute-done((bf16[3,1,1,2,24,1536]{5,4,2,1,0,3:T(8,128)(2,1)S(1)}, bf16[3,1,1,2,24,1536]{5,4,2,1,0,3:T(8,128)(2,1)S(1)}, u32[]{:S(2)}, u32[]{:S(2)}) %collective-permute-start.2) | collective-permute-done | bytes 442400 | tf_op jit(solution)/shard_map/ppermute | solution.py:20
  22.5 11.4 %collective-permute-done.3 = bf16[3,1,1,2,24,1536]{5,4,2,1,0,3:T(8,128)(2,1)S(1)} collective-permute-done((bf16[3,1,1,2,24,1536]{5,4,2,1,0,3:T(8,128)(2,1)S(1)}, bf16[3,1,1,2,24,1536]{5,4,2,1,0,3:T(8,128)(2,1)S(1)}, u32[]{:S(2)}, u32[]{:S(2)}) %collective-permute-start.3) | collective-permute-done | bytes 442400 | tf_op jit(solution)/shard_map/ppermute | solution.py:22
  34.0 1.1 pad_maximum_fusion.1
  35.0 4.6 %collective-permute-start.4 = (bf16[3,3,1,2,24,1536]{5,4,2,1,0,3:T(8,128)(2,1)S(1)}, bf16[3,3,1,2,24,1536]{5,4,2,1,0,3:T(8,128)(2,1)}, u32[]{:S(2)}, u32[]{:S(2)}) collective-permute-start(bf16[3,3,1,2,24,1536]{5,4,2,1,0,3:T(8,128)(2,1)S(1)} %pad_maximum_fusion.1), channel_id=1, source_target_pairs={{0,1},{1,2},{2,3},{4,5},{5,6},{6,7},{8,9},{9,10},{10,11},{12,13},{... | collective-permute-start | bytes 3981320 | tf_op jit(solution)/shard_map/ppermute | solution.py:20
  39.6 1.3 %collective-permute-start.5 = (bf16[3,3,1,2,24,1536]{5,4,2,1,0,3:T(8,128)(2,1)S(1)}, bf16[3,3,1,2,24,1536]{5,4,2,1,0,3:T(8,128)(2,1)}, u32[]{:S(2)}, u32[]{:S(2)}) collective-permute-start(bf16[3,3,1,2,24,1536]{5,4,2,1,0,3:T(8,128)(2,1)S(1)} %pad_maximum_fusion.1), channel_id=1, source_target_pairs={{1,0},{2,1},{3,2},{5,4},{6,5},{7,6},{9,8},{10,9},{11,10},{13,12},{... | collective-permute-start | bytes 3981320 | tf_op jit(solution)/shard_map/ppermute | solution.py:22
  40.9 0.0 copy-done.9
  40.9 0.0 copy-done.10
  40.9 0.0 copy-done.11
  40.9 0.0 copy-done.8
  41.0 0.1 mul.164
  41.1 0.1 broadcast_in_dim.34
  41.2 0.1 broadcast_in_dim.35
  41.3 0.1 copy.30
  41.4 0.1 mul.174
  41.6 39.5 %all_gather.3 = bf16[2,16,1536]{2,0,1:T(2,128)(2,1)S(1)} all-gather(bf16[2,4,1536]{2,0,1:T(2,128)(2,1)S(1)} %copy.37), channel_id=1, replica_groups=mesh['ta'=2,'ha'=4,'wa'=4] {'wa'}, dimensions={1}, use_global_device_ids=true | all-gather | bytes 122880 | tf_op jit(solution)/shard_map/all_gather | solution.py:44
  81.1 0.4 slice_reduce_fusion.1
  81.5 0.0 copy-done.7
  81.5 0.1 fusion.23
  81.6 0.2 fusion.39
  81.8 0.0 collective-permute-done.4
  81.8 0.0 collective-permute-done.5
  81.8 2.7 %pad_maximum_fusion = bf16[3,3,3,2,24,1536]{5,4,2,1,0,3:T(8,128)(2,1)S(1)} fusion(bf16[3,3,1,2,24,1536]{5,4,2,1,0,3:T(8,128)(2,1)} %collective-permute-done.5, bf16[3,1,1,2,24,1536]{5,4,2,1,0,3:T(8,128)(2,1)S(1)} %collective-permute-done.3, bf16[1,1,1,2,24,1536]{5,4,2,1,0,3:T(8,128)(2,1)S(1)} %collective-permute-done.1, ...), kind=kLoop, calls=%fused_computation.5 | loop fusion | flops 11943936 | bytes 7962624 | tf_op jit(solution)/shard_map/concatenate | solution.py:18
  84.5 2.8 %convert_multiply_fusion = f32[3,3,3,1,24,1536]{5,4,2,1,0,3:T(8,128)} fusion(bf16[3,3,3,2,24,1536]{5,4,2,1,0,3:T(8,128)(2,1)S(1)} %pad_maximum_fusion), kind=kLoop, calls=%fused_computation | loop fusion | flops 1990656 | bytes 5971968 | tf_op jit(solution)/shard_map/mul | solution.py:31
  87.3 0.3 copy-done.1
  87.6 0.1 slice_bitcast_fusion
  87.7 5.5 %mul.154 = f32[3,3,3,24,12,128]{5,4,3,2,1,0:T(8,128)} reshape(f32[3,3,3,1,24,1536]{5,4,2,1,0,3:T(8,128)} %convert_multiply_fusion) | data formatting | bytes 7962624 | tf_op jit(solution)/shard_map/mul | solution.py:31
  93.2 4.0 %reduce_sum.73 = f32[3,3,3,24,12]{4,3,2,1,0:T(8,128)S(1)} reduce(f32[3,3,3,24,12,128]{5,4,3,2,1,0:T(8,128)} %mul.154, f32[]{:T(128)} %constant.94.clone.1), dimensions={5}, to_apply=%region_1.0 | reduce | flops 987552 | bytes 4012420 | tf_op jit(solution)/shard_map/reduce_sum | solution.py:31
  97.1 0.1 add_rsqrt_fusion
  97.2 3.5 %mul.155 = f32[3,3,3,24,12,128]{5,4,3,2,1,0:T(8,128)} broadcast(f32[3,3,3,24,12]{4,3,2,1,0:T(8,128)S(1)} %add_rsqrt_fusion), dimensions={0,1,2,3,4} | broadcast | bytes 4012416 | tf_op jit(solution)/shard_map/mul | solution.py:32
  100.7 5.6 %mul.156 = f32[3,3,3,24,1536]{4,3,2,1,0:T(8,128)} reshape(f32[3,3,3,24,12,128]{5,4,3,2,1,0:T(8,128)} %mul.155) | data formatting | bytes 7962624 | tf_op jit(solution)/shard_map/mul | solution.py:32
  106.4 3.4 %fusion.2 = bf16[3,3,3,24,1536]{4,3,2,1,0:T(8,128)(2,1)S(1)} fusion(f32[3,3,3,24,1536]{4,3,2,1,0:T(8,128)} %mul.156, f32[1536]{0:T(1024)S(1)} %broadcast_bitcast_fusion, bf16[3,3,3,2,24,1536]{5,4,2,1,0,3:T(8,128)(2,1)} %copy-done.1), kind=kLoop, calls=%fused_computation.4 | loop fusion | flops 3981312 | bytes 7968768 | tf_op jit(solution)/shard_map/convert_element_type | solution.py:32
  109.8 0.0 copy-done.5
  109.8 1.3 %copy-done.2 = bf16[3,3,3,24,1536]{4,3,2,1,0:T(8,128)(2,1)} copy-done((bf16[3,3,3,24,1536]{4,3,2,1,0:T(8,128)(2,1)}, bf16[3,3,3,24,1536]{4,3,2,1,0:T(8,128)(2,1)S(1)}, u32[]{:S(2)}) %copy-start.2) | copy-done | bytes 1990680
  111.1 1.3 %copy-done.3 = bf16[3,3,3,24,1536]{4,3,2,1,0:T(8,128)(2,1)} copy-done((bf16[3,3,3,24,1536]{4,3,2,1,0:T(8,128)(2,1)}, bf16[3,3,3,24,1536]{4,3,2,1,0:T(8,128)(2,1)S(1)}, u32[]{:S(2)}) %copy-start.3) | copy-done | bytes 1990680
  112.4 3.8 %reshape.228 = bf16[648,12,128]{2,1,0:T(8,128)(2,1)S(1)} reshape(bf16[3,3,3,24,1536]{4,3,2,1,0:T(8,128)(2,1)} %copy-done.3) | data formatting | bytes 3981312 | tf_op jit(solution)/shard_map/reshape | solution.py:61
  116.1 0.6 fusion.37
  116.7 0.4 fusion.40
  117.2 0.4 fusion.41
  117.6 0.4 fusion.42
  118.0 3.8 %reshape.227 = bf16[648,12,128]{2,1,0:T(8,128)(2,1)S(1)} reshape(bf16[3,3,3,24,1536]{4,3,2,1,0:T(8,128)(2,1)} %copy-done.2) | data formatting | bytes 3981312 | tf_op jit(solution)/shard_map/reshape | solution.py:62
  121.8 0.6 fusion.38
  122.4 0.2 convolution_bitcast_fusion.3
  122.6 0.2 convolution_bitcast_fusion.2
  122.8 0.2 convolution_bitcast_fusion.1
  123.1 0.2 fusion.11
  123.4 0.7 convert_element_type.122
  (27 shorter events, 0.3 us)
Async XLA Ops:
  0.0 5.7 %copy-start = (f32[128]{0:T(128)S(1)}, f32[128]{0:T(128)}, u32[]{:S(2)}) copy-start(f32[128]{0:T(128)} %param.19) | copy-start | bytes 1540
  0.0 40.9 %copy-start.9 = (s32[27]{0:T(128)S(1)}, s32[27]{0:T(128)}, u32[]{:S(2)}) copy-start(s32[27]{0:T(128)} %constant.100.clone) | copy-start | bytes 328
  0.0 40.9 %copy-start.10 = (s32[27]{0:T(128)S(1)}, s32[27]{0:T(128)}, u32[]{:S(2)}) copy-start(s32[27]{0:T(128)} %constant.98.clone) | copy-start | bytes 328
  0.0 40.9 %copy-start.11 = (s32[27]{0:T(128)S(1)}, s32[27]{0:T(128)}, u32[]{:S(2)}) copy-start(s32[27]{0:T(128)} %constant.99.clone) | copy-start | bytes 328
  0.0 40.9 %copy-start.8 = (s32[1,1,1,27]{3,2,1,0:T(1,128)S(1)}, s32[1,1,1,27]{3,2,1,0:T(1,128)}, u32[]{:S(2)}) copy-start(s32[1,1,1,27]{3,2,1,0:T(1,128)} %param.20) | copy-start | bytes 328
  0.0 6.9 %collective-permute-start = (bf16[1,1,1,2,24,1536]{5,4,2,1,0,3:T(8,128)(2,1)}, bf16[1,1,1,2,24,1536]{5,4,2,1,0,3:T(8,128)(2,1)S(1)}, u32[]{:S(2)}, u32[]{:S(2)}) collective-permute-start(bf16[1,1,1,2,24,1536]{5,4,2,1,0,3:T(8,128)(2,1)} %bitcast.83), channel_id=1, source_target_pairs={{0,16},{1,17},{2,18},{3,19},{4,20},{5,21},{6,22},{7,23},{8,24},{9,... | collective-permute-start | bytes 442376 | tf_op jit(solution)/shard_map/ppermute | solution.py:20
  2.5 4.4 %collective-permute-start.1 = (bf16[1,1,1,2,24,1536]{5,4,2,1,0,3:T(8,128)(2,1)}, bf16[1,1,1,2,24,1536]{5,4,2,1,0,3:T(8,128)(2,1)S(1)}, u32[]{:S(2)}, u32[]{:S(2)}) collective-permute-start(bf16[1,1,1,2,24,1536]{5,4,2,1,0,3:T(8,128)(2,1)} %bitcast.84), channel_id=1, source_target_pairs={{16,0},{17,1},{18,2},{19,3},{20,4},{21,5},{22,6},{23,7},{24,8},{25... | collective-permute-start | bytes 442376 | tf_op jit(solution)/shard_map/ppermute | solution.py:22
  4.8 36.7 %copy-start.6 = (bf16[2,4,1536]{2,1,0:T(4,128)(2,1)S(1)}, bf16[2,4,1536]{2,1,0:T(4,128)(2,1)}, u32[]{:S(2)}) copy-start(bf16[2,4,1536]{2,1,0:T(4,128)(2,1)} %param.17) | copy-start | bytes 73732
  4.8 36.7 %slice-start = ((bf16[2,4,1536]{2,1,0:T(4,128)(2,1)}), bf16[1,4,1536]{2,1,0:T(4,128)(2,1)S(1)}, s32[]{:S(2)}) async-start(bf16[2,4,1536]{2,1,0:T(4,128)(2,1)} %param.17), calls=%async_computation | async-start | bytes 24576 | tf_op jit(solution)/shard_map/slice | solution.py:43
  5.7 75.8 %copy-start.7 = (f32[128]{0:T(128)S(1)}, f32[128]{0:T(128)}, u32[]{:S(2)}) copy-start(f32[128]{0:T(128)} %param.18) | copy-start | bytes 1540
  6.9 74.9 %copy-start.4 = (bf16[1,1,1,2,24,1536]{5,4,3,2,1,0:T(8,128)(2,1)S(1)}, bf16[1,1,1,2,24,1536]{5,4,3,2,1,0:T(8,128)(2,1)}, u32[]{:S(2)}) copy-start(bf16[1,1,1,2,24,1536]{5,4,3,2,1,0:T(8,128)(2,1)} %param.16) | copy-start | bytes 442372
  7.9 14.6 %collective-permute-start.2 = (bf16[3,1,1,2,24,1536]{5,4,2,1,0,3:T(8,128)(2,1)S(1)}, bf16[3,1,1,2,24,1536]{5,4,2,1,0,3:T(8,128)(2,1)S(1)}, u32[]{:S(2)}, u32[]{:S(2)}) collective-permute-start(bf16[3,1,1,2,24,1536]{5,4,2,1,0,3:T(8,128)(2,1)S(1)} %pad_maximum_fusion.2), channel_id=1, source_target_pairs={{0,4},{4,8},{8,12},{1,5},{5,9},{9,13},{2,6},{6,10},{10,14},{3,7},{... | collective-permute-start | bytes 1327112 | tf_op jit(solution)/shard_map/ppermute | solution.py:20
  12.2 21.8 %collective-permute-start.3 = (bf16[3,1,1,2,24,1536]{5,4,2,1,0,3:T(8,128)(2,1)S(1)}, bf16[3,1,1,2,24,1536]{5,4,2,1,0,3:T(8,128)(2,1)S(1)}, u32[]{:S(2)}, u32[]{:S(2)}) collective-permute-start(bf16[3,1,1,2,24,1536]{5,4,2,1,0,3:T(8,128)(2,1)S(1)} %pad_maximum_fusion.2), channel_id=1, source_target_pairs={{4,0},{8,4},{12,8},{5,1},{9,5},{13,9},{6,2},{10,6},{14,10},{7,3},{... | collective-permute-start | bytes 1327112 | tf_op jit(solution)/shard_map/ppermute | solution.py:22
  35.0 46.7 %collective-permute-start.4 = (bf16[3,3,1,2,24,1536]{5,4,2,1,0,3:T(8,128)(2,1)S(1)}, bf16[3,3,1,2,24,1536]{5,4,2,1,0,3:T(8,128)(2,1)}, u32[]{:S(2)}, u32[]{:S(2)}) collective-permute-start(bf16[3,3,1,2,24,1536]{5,4,2,1,0,3:T(8,128)(2,1)S(1)} %pad_maximum_fusion.1), channel_id=1, source_target_pairs={{0,1},{1,2},{2,3},{4,5},{5,6},{6,7},{8,9},{9,10},{10,11},{12,13},{... | collective-permute-start | bytes 3981320 | tf_op jit(solution)/shard_map/ppermute | solution.py:20
  39.6 42.2 %collective-permute-start.5 = (bf16[3,3,1,2,24,1536]{5,4,2,1,0,3:T(8,128)(2,1)S(1)}, bf16[3,3,1,2,24,1536]{5,4,2,1,0,3:T(8,128)(2,1)}, u32[]{:S(2)}, u32[]{:S(2)}) collective-permute-start(bf16[3,3,1,2,24,1536]{5,4,2,1,0,3:T(8,128)(2,1)S(1)} %pad_maximum_fusion.1), channel_id=1, source_target_pairs={{1,0},{2,1},{3,2},{5,4},{6,5},{7,6},{9,8},{10,9},{11,10},{13,12},{... | collective-permute-start | bytes 3981320 | tf_op jit(solution)/shard_map/ppermute | solution.py:22
  84.5 3.1 %copy-start.1 = (bf16[3,3,3,2,24,1536]{5,4,2,1,0,3:T(8,128)(2,1)}, bf16[3,3,3,2,24,1536]{5,4,2,1,0,3:T(8,128)(2,1)S(1)}, u32[]{:S(2)}) copy-start(bf16[3,3,3,2,24,1536]{5,4,2,1,0,3:T(8,128)(2,1)S(1)} %pad_maximum_fusion) | copy-start | bytes 11943940
  106.4 3.4 %copy-start.5 = (bf16[1,1,1,2,24,1536]{5,4,3,2,1,0:T(8,128)(2,1)S(1)}, bf16[1,1,1,2,24,1536]{5,4,3,2,1,0:T(8,128)(2,1)}, u32[]{:S(2)}) copy-start(bf16[1,1,1,2,24,1536]{5,4,3,2,1,0:T(8,128)(2,1)} %param.15) | copy-start | bytes 442372
  109.8 1.3 %copy-start.2 = (bf16[3,3,3,24,1536]{4,3,2,1,0:T(8,128)(2,1)}, bf16[3,3,3,24,1536]{4,3,2,1,0:T(8,128)(2,1)S(1)}, u32[]{:S(2)}) copy-start(bf16[3,3,3,24,1536]{4,3,2,1,0:T(8,128)(2,1)S(1)} %get-tuple-element.38) | copy-start | bytes 5971972
  111.1 1.3 %copy-start.3 = (bf16[3,3,3,24,1536]{4,3,2,1,0:T(8,128)(2,1)}, bf16[3,3,3,24,1536]{4,3,2,1,0:T(8,128)(2,1)S(1)}, u32[]{:S(2)}) copy-start(bf16[3,3,3,24,1536]{4,3,2,1,0:T(8,128)(2,1)S(1)} %get-tuple-element.37) | copy-start | bytes 5971972
where the time goes:
time: 125 us; the launch traced here: 124 us
  blocking collectives  39.5 us (32%)
  local copies, waits for them, and re-layouts  29 us (23%)
  waiting for transfers between devices  20.5 us (16%)
  other arithmetic  17.1 us (14%)
  starting transfers between devices  15.2 us (12%)
  matrix products  2.36 us (2%)
    all_gather x1, blocking collectives, shards(): piece = lax.all_gather(text_send, 'wa', axis=1, tiled=True)  39.5 us
    ppermute x3, waiting for transfers between devices, with_halo(): lax.ppermute(head, axis, [((i + 1) % count, i) for i in range(ends)])  11.4 us
    ppermute x3, starting transfers between devices, with_halo(): lax.ppermute(tail, axis, [(i, (i + 1) % count) for i in range(ends)])  11.3 us
    mul x7, local copies, waits for them, and re-layouts, qk_normed(): shaped * lax.rsqrt(square + 1e-06) * gain  9.37 us
    ppermute x3, waiting for transfers between devices, with_halo(): lax.ppermute(tail, axis, [(i, (i + 1) % count) for i in range(ends)])  9.03 us
    mul x3, local copies, waits for them, and re-layouts, qk_normed(): square = jnp.mean(shaped * shaped, axis=-1, keepdims=True)  5.5 us
    concatenate x3, other arithmetic, with_halo(): jnp.concatenate([lax.ppermute(tail, axis, [(i, (i + 1) % count) for i in...  4.73 us
    mul x3, other arithmetic, qk_normed(): square = jnp.mean(shaped * shaped, axis=-1, keepdims=True)  4.42 us
  transfers between devices with their start and end apart: 6, of which 2 were waited for; matrix products, arithmetic and copies ran while one was open for 3% of the time, Pallas kernels for 0%

commit v1 on v0

v1 whole, which is shorter than its diff:
```python
import jax
import jax.numpy as jnp
from jax import lax
from jax.experimental import pallas as pl
from jax.experimental.pallas import tpu as pltpu
from jax.sharding import PartitionSpec as P

EPS = 1e-06
LANES = 128
IN_VMEM = pl.BlockSpec(memory_space=pltpu.VMEM)


def parities(count):
    return [parity for parity in (0, 1) if count - parity >= 2]


def step_of(place, parity):
    return jnp.where(place % 2 == parity, 1, -1)


def matching(axis_size, ta_size, parity):
    pairs = []
    for t in range(ta_size):
        for a in range(axis_size):
            b = a + 1 if a % 2 == parity else a - 1
            if 0 <= b < axis_size:
                pairs.append((t * axis_size + a, t * axis_size + b))
            elif t ^ 1 < ta_size:
                pairs.append((t * axis_size + a, (t ^ 1) * axis_size + a))
    return pairs


def swap_along(values, axis, parity):
    pairs = matching(lax.axis_size(axis), lax.axis_size("ta"), parity)
    return lax.ppermute(values, ("ta", axis), pairs)


def swap_ta(values, parity):
    count = lax.axis_size("ta")
    pairs = []
    for t in range(count):
        u = t + 1 if t % 2 == parity else t - 1
        if 0 <= u < count:
            pairs.append((t, u))
    return lax.ppermute(values, "ta", pairs)


def resident(values):
    return pltpu.with_memory_space_constraint(values, pltpu.VMEM)


def call(body, out_shape, *operands, flops=0, exps=0):
    outs = [pltpu.VMEM(s.shape, s.dtype) for s in out_shape]
    moved = sum(x.size * x.dtype.itemsize for x in operands)
    return pl.pallas_call(
        body,
        out_shape=outs,
        in_specs=[IN_VMEM] * len(operands),
        out_specs=[IN_VMEM] * len(outs),
        cost_estimate=pl.CostEstimate(flops=flops, bytes_accessed=moved, transcendentals=exps),
    )(*[resident(x) for x in operands])


def head_normed(values, gain, heads):
    hd = gain.shape[-1]
    parts = []
    for head in range(heads):
        part = values[:, head * hd : (head + 1) * hd]
        square = jnp.mean(part * part, axis=-1, keepdims=True)
        parts.append(part * lax.rsqrt(square + EPS) * gain)
    return jnp.concatenate(parts, axis=1)


def scores_of(q, k):
    return lax.dot_general(q, k, (((1,), (1,)), ((), ())), preferred_element_type=jnp.float32)


def prepare_queries(queries, q_gain, mask_rows):
    tile, width = queries.shape
    heads = width // q_gain.shape[-1]

    def body(q_ref, gain_ref, mask_ref, out_ref):
        normed = head_normed(q_ref[...].astype(jnp.float32), gain_ref[...], heads)
        masks = mask_ref[...]
        pad = jnp.zeros((masks.shape[0], width - masks.shape[1]), jnp.float32)
        rows = jnp.concatenate([masks, pad], axis=1)
        out_ref[...] = jnp.concatenate([normed, rows], axis=0).astype(jnp.bfloat16)

    shape = jax.ShapeDtypeStruct((tile + mask_rows.shape[0], width), jnp.bfloat16)
    return call(body, [shape], queries, q_gain, mask_rows)[0]


def attend_for_partners(slots, sent, k_gain, tile):
    rows, width = sent[0].shape if sent else (tile + 8, slots[0].shape[1])
    hd = k_gain.shape[-1]
    heads = width // hd
    count = len(slots)
    keys = count * tile
    scale = hd ** (-0.5)

    def body(*refs):
        slot_refs = refs[:count]
        sent_refs = refs[count : count + len(sent)]
        gain_ref = refs[count + len(sent)]
        outs = refs[count + len(sent) + 1 :]
        keys_ref, vals_ref = outs[0], outs[1]
        back_refs = outs[2:]
        gain = gain_ref[...]
        both = [r[...].astype(jnp.float32) for r in slot_refs]
        keys_ref[...] = jnp.concatenate(
            [head_normed(b[:tile], gain, heads) for b in both], axis=0
        ).astype(jnp.bfloat16)
        vals_ref[...] = jnp.concatenate([b[tile:] for b in both], axis=0).astype(jnp.bfloat16)
        if not sent:
            return
        q_all = jnp.concatenate([r[...] for r in sent_refs], axis=0)
        masks = []
        for index, r in enumerate(sent_refs):
            row = r[...].astype(jnp.float32)[tile + index : tile + index + 1, :keys]
            masks.append(jnp.broadcast_to(row, (rows, keys)))
        mask = jnp.concatenate(masks, axis=0)
        lane = lax.broadcasted_iota(jnp.int32, (len(sent) * rows, LANES), 1)
        sums = jnp.zeros((len(sent) * rows, LANES), jnp.float32)
        for head in range(heads):
            cols = slice(head * hd, (head + 1) * hd)
            expo = jnp.exp(scores_of(q_all[:, cols], keys_ref[:, cols]) * scale) * mask
            total = jnp.dot(
                expo.astype(jnp.bfloat16), vals_ref[:, cols], preferred_element_type=jnp.float32
            )
            weight = jnp.sum(expo, axis=1, keepdims=True)
            high = weight.astype(jnp.bfloat16).astype(jnp.float32)
            sums = jnp.where(lane == head, high, sums)
            sums = jnp.where(lane == head + LANES // 2, weight - high, sums)
            for index, back in enumerate(back_refs):
                back[:, cols] = total[index * rows : index * rows + tile].astype(jnp.bfloat16)
        for index, back in enumerate(back_refs):
            back[:, width:] = sums[index * rows : index * rows + tile].astype(jnp.bfloat16)

    shapes = [jax.ShapeDtypeStruct((keys, width), jnp.bfloat16)] * 2
    shapes += [jax.ShapeDtypeStruct((tile, width + LANES), jnp.bfloat16)] * len(sent)
    outs = call(
        body,
        shapes,
        *slots,
        *sent,
        k_gain,
        flops=4 * len(sent) * rows * keys * width,
        exps=len(sent) * rows * keys * heads,
    )
    return outs[0], outs[1], outs[2:]


def attend_own(own, keys, vals, current, text_keys, text_vals, k_gain, tile, mask_row):
    rows, width = own.shape
    hd = k_gain.shape[-1]
    heads = width // hd
    count = keys.shape[0]
    scale = hd ** (-0.5)

    def body(q_ref, keys_ref, vals_ref, current_ref, text_k_ref, text_v_ref, gain_ref, total_ref, sum_ref):
        gain = gain_ref[...]
        here = current_ref[...].astype(jnp.float32)
        sure_keys = jnp.concatenate(
            [
                head_normed(here[:tile], gain, heads),
                head_normed(text_k_ref[...].astype(jnp.float32), gain, heads),
            ],
            axis=0,
        ).astype(jnp.bfloat16)
        sure_vals = jnp.concatenate(
            [here[tile:], text_v_ref[...].astype(jnp.float32)], axis=0
        ).astype(jnp.bfloat16)
        q = q_ref[...]
        mask = q.astype(jnp.float32)[tile + mask_row : tile + mask_row + 1, :count]
        lane = lax.broadcasted_iota(jnp.int32, (rows, LANES), 1)
        sums = jnp.ones((rows, LANES), jnp.float32)
        for head in range(heads):
            cols = slice(head * hd, (head + 1) * hd)
            near = jnp.exp(scores_of(q[:, cols], keys_ref[:, cols]) * scale) * mask
            sure = jnp.exp(scores_of(q[:, cols], sure_keys[:, cols]) * scale)
            total = jnp.dot(
                near.astype(jnp.bfloat16), vals_ref[:, cols], preferred_element_type=jnp.float32
            ) + jnp.dot(
                sure.astype(jnp.bfloat16), sure_vals[:, cols], preferred_element_type=jnp.float32
            )
            weight = jnp.sum(near, axis=1, keepdims=True) + jnp.sum(sure, axis=1, keepdims=True)
            sums = jnp.where(lane == head, weight, sums)
            total_ref[:, cols] = total[:tile]
        sum_ref[...] = sums[:tile]

    shapes = [
        jax.ShapeDtypeStruct((tile, width), jnp.float32),
        jax.ShapeDtypeStruct((tile, LANES), jnp.float32),
    ]
    all_keys = count + tile + text_keys.shape[0]
    return call(
        body,
        shapes,
        own,
        keys,
        vals,
        current,
        text_keys,
        text_vals,
        k_gain,
        flops=4 * rows * all_keys * width,
        exps=rows * all_keys * heads,
    )


def combine(total, weight, backs, hd):
    tile, width = total.shape
    heads = width // hd

    def body(total_ref, sum_ref, *refs):
        back_refs, out_ref = refs[:-1], refs[-1]
        sums = sum_ref[...]
        for r in back_refs:
            part = r[:, width:].astype(jnp.float32)
            sums = sums + part + pltpu.roll(part, LANES // 2, 1)
        inverse = 1.0 / sums
        for head in range(heads):
            cols = slice(head * hd, (head + 1) * hd)
            whole = total_ref[:, cols]
            for r in back_refs:
                whole = whole + r[:, cols].astype(jnp.float32)
            out_ref[:, cols] = (whole * inverse[:, head : head + 1]).astype(jnp.bfloat16)

    operands = [total, weight, *backs]
    return pl.pallas_call(
        body,
        out_shape=jax.ShapeDtypeStruct((tile, width), jnp.bfloat16),
        in_specs=[IN_VMEM] * len(operands),
        out_specs=IN_VMEM,
    )(*[resident(x) for x in operands])


def gather_text(text_kv):
    count = lax.axis_size("wa")
    if count & (count - 1):
        return lax.all_gather(text_kv, "wa", axis=1, tiled=True)
    span = 1
    while span < count:
        other = lax.ppermute(text_kv, "wa", [(i, i ^ span) for i in range(count)])
        text_kv = jnp.concatenate([text_kv, other], axis=1)
        span *= 2
    return text_kv


def mask_rows_of(pattern, tile, row_count):
    place = {a: lax.axis_index(a) for a in ("ta", "ha", "wa")}
    size = {a: lax.axis_size(a) for a in ("ta", "ha", "wa")}
    steps = {a: [step_of(place[a], p) for p in parities(size[a])] for a in size}
    steps_t = [0] + steps["ta"]
    steps_w = [0] + steps["wa"]
    steps_h = steps["ha"] + [0]
    count = len(steps_t) * len(steps_w)
    lanes = -(-count * tile // LANES) * LANES
    slot = lax.broadcasted_iota(jnp.int32, (row_count, lanes), 1) // tile
    row = lax.broadcasted_iota(jnp.int32, (row_count, lanes), 0)

    def pick(index, options):
        chosen = jnp.full((row_count, lanes), 9, jnp.int32)
        for i, option in enumerate(options):
            chosen = jnp.where(index == i, option, chosen)
        return chosen

    dt = pick(slot // len(steps_w), steps_t)
    dw = pick(slot % len(steps_w), steps_w)
    dh = pick(row, steps_h)
    inside = jnp.ones((row_count, lanes), bool)
    for axis, d in (("ta", dt), ("ha", dh), ("wa", dw)):
        inside = inside & (d < 9) & (place[axis] + d >= 0) & (place[axis] + d < size[axis])
    offset = (dt + 1) * 9 + (dh + 1) * 3 + dw + 1
    used = inside & (offset != 13)
    hits = jnp.zeros((row_count, lanes), bool)
    for o in range(27):
        hits = hits | ((offset == o) & (pattern[o] == 1))
    return jnp.where(used & hits, 1.0, 0.0).astype(jnp.float32)


def shards(queries, current_kv, stale_kv, text_kv, q_gain, k_gain, pattern):
    tile, width = queries.shape[3:]
    hd = q_gain.shape[0]
    stale = stale_kv.reshape(2 * tile, width)
    current = current_kv.reshape(2 * tile, width)
    k_gain = k_gain.reshape(1, hd)
    h_parities = parities(lax.axis_size("ha"))

    line = [stale] + [swap_along(stale, "wa", p) for p in parities(lax.axis_size("wa"))]
    mask_rows = mask_rows_of(pattern.reshape(27), tile, 8)
    own = prepare_queries(queries.reshape(tile, width), q_gain.reshape(1, hd), mask_rows)
    sent = [swap_along(own, "ha", p) for p in h_parities]
    text = gather_text(text_kv)
    slots = list(line)
    for p in parities(lax.axis_size("ta")):
        slots += [swap_ta(x, p) for x in line]
    keys, vals, answers = attend_for_partners(slots, sent, k_gain, tile)
    backs = [swap_along(x, "ha", p) for x, p in zip(answers, h_parities, strict=True)]
    total, weight = attend_own(
        own, keys, vals, current, text[0], text[1], k_gain, tile, len(h_parities)
    )
    result = combine(total, weight, backs, hd)
    return result.reshape(1, 1, 1, tile, width)


def solution(mesh):
    return jax.shard_map(
        shards,
        mesh=mesh,
        in_specs=(
            P("ta", "ha", "wa", None, None),
            P("ta", "ha", "wa", None, None, None),
            P("ta", "ha", "wa", None, None, None),
            P(None, "wa", None),
            P(),
            P(),
            P("ta", "ha", "wa", None),
        ),
        out_specs=P("ta", "ha", "wa", None, None),
        check_vma=False,
    )
```

time: 125 us -> 43.2 us (0.35)
  blocking collectives: 39.5 us -> 0 us
  local copies, waits for them, and re-layouts: 29 us -> 2.65 us
  other arithmetic: 17.1 us -> 0.26 us
  between operations: 0.45 us -> 17.1 us
  waiting for transfers between devices: 20.5 us -> 4.96 us
  Pallas kernels: 0 us -> 5.29 us
  starting transfers between devices: 15.2 us -> 12.5 us
  matrix products: 2.36 us -> 0 us
    all_gather x1 -> x0, blocking collectives: 39.5 us -> none  [shards(): piece = lax.all_gather(text_send, 'wa', axis=1, tiled=True)]
    ppermute x6 -> x11, waiting for transfers between devices: 20.5 us -> 4.96 us  [the longest x2 2.57 us: gather_text(): other = lax.ppermute(text_kv, 'wa', [(i, i ^ span) for i in range(count)])]
    mul x10 -> x0, local copies, waits for them, and re-layouts: 14.9 us -> none  [the longest x7 9.37 us: qk_normed(): shaped * lax.rsqrt(square + 1e-06) * gain]
    reshape x2 -> x0, local copies, waits for them, and re-layouts: 7.52 us -> none  [the longest x1 3.76 us: shards(): near_vals = near_vals.reshape(27 * tile, heads, head_dim)]
    pallas_call x0 -> x4, Pallas kernels: none -> 5.29 us  [the longest x3 4.45 us: call(): pl.pallas_call(body, out_shape=outs, in_specs=[IN_VMEM] * len(operands),...]
    concatenate x3 -> x2, other arithmetic: 4.73 us -> 0.07 us  [gather_text(): text_kv = jnp.concatenate([text_kv, other], axis=1)]
    mul x3 -> x0, other arithmetic: 4.42 us -> none  [qk_normed(): square = jnp.mean(shaped * shaped, axis=-1, keepdims=True)]
    reduce_sum x4 -> x0, other arithmetic: 4.29 us -> none  [qk_normed(): square = jnp.mean(shaped * shaped, axis=-1, keepdims=True)]
  transfers between devices with their start and end apart: 6 -> 11, of which waited for: 2 -> 6; matrix products, arithmetic and copies ran while one was open for 3% -> 4% of each run, Pallas kernels for 0% -> 5%
where the time goes in v1:
time: 43.2 us; the launch traced here: 42.8 us
  between operations  17.1 us (40%)
  starting transfers between devices  12.5 us (29%)
  Pallas kernels  5.29 us (12%)
  waiting for transfers between devices  4.96 us (11%)
  local copies, waits for them, and re-layouts  2.65 us (6%)
    ppermute x6, starting transfers between devices, swap_along(): return lax.ppermute(values, ('ta', axis), pairs)  8.7 us
    pallas_call x3, Pallas kernels, call(): pl.pallas_call(body, out_shape=outs, in_specs=[IN_VMEM] * len(operands),...  4.45 us
    ppermute x2, starting transfers between devices, gather_text(): other = lax.ppermute(text_kv, 'wa', [(i, i ^ span) for i in range(count)])  3.22 us
    ppermute x2, waiting for transfers between devices, gather_text(): other = lax.ppermute(text_kv, 'wa', [(i, i ^ span) for i in range(count)])  2.57 us
    ppermute x6, waiting for transfers between devices, swap_along(): return lax.ppermute(values, ('ta', axis), pairs)  1.74 us
    slice x2, local copies, waits for them, and re-layouts, mask_rows_of(): hits = hits | (offset == o) & (pattern[o] == 1)  1.4 us
    unnamed x14, local copies, waits for them, and re-layouts  1.24 us
  transfers between devices with their start and end apart: 11, of which 6 were waited for; matrix products, arithmetic and copies ran while one was open for 4% of the time, Pallas kernels for 5%

profile of v1, /device:TPU:0, one launch (start us, length us, event | category | flops | bytes accessed | tf_op | source)
XLA Modules:
  0.0 42.8 jit_solution(15795319583422443266)
XLA Ops:
  0.0 3.0 %collective-permute-start = (bf16[48,1536]{1,0:T(8,128)(2,1)}, bf16[48,1536]{1,0:T(8,128)(2,1)S(1)}, u32[]{:S(2)}, u32[]{:S(2)}) collective-permute-start(bf16[48,1536]{1,0:T(8,128)(2,1)} %bitcast.38), channel_id=1, source_target_pairs={{0,1},{1,0},{2,3},{3,2},{16,17},{17,16},{18,19},{19,18},{4,5},{5,4... | collective-permute-start | bytes 442376 | tf_op jit(solution)/shard_map/ppermute | solution.py:35
  3.0 0.0 collective-permute-start.1
  3.0 3.1 %collective-permute-start.7 = (bf16[2,4,1536]{2,1,0:T(4,128)(2,1)}, bf16[2,4,1536]{2,1,0:T(4,128)(2,1)S(1)}, u32[]{:S(2)}, u32[]{:S(2)}) collective-permute-start(bf16[2,4,1536]{2,1,0:T(4,128)(2,1)} %param.10), channel_id=1, source_target_pairs={{0,1},{1,0},{2,3},{3,2},{4,5},{5,4},{6,7},{7,6},{8,9},{9,8},{10,11... | collective-permute-start | bytes 73736 | tf_op jit(solution)/shard_map/ppermute | solution.py:244
  6.2 0.0 copy-start.5
  6.2 0.7 %copy-done.5 = s32[1,1,1,27]{3,2,1,0:T(1,128)S(1)} copy-done((s32[1,1,1,27]{3,2,1,0:T(1,128)S(1)}, s32[1,1,1,27]{3,2,1,0:T(1,128)}, u32[]{:S(2)}) %copy-start.5) | copy-done | bytes 132
  6.8 0.7 %fusion.25 = (s32[1,1,1,1]{3,2,1,0:T(1,128)}, s32[1,1,1,1]{3,2,1,0:T(1,128)}, s32[1,1,1,1]{3,2,1,0:T(1,128)}, s32[1,1,1,1]{3,2,1,0:T(1,128)}, s32[1,1,1,1]{3,2,1...) fusion(s32[1,1,1,27]{3,2,1,0:T(1,128)S(1)} %copy-done.5), kind=kLoop, calls=%fused_computation.46 | loop fusion | bytes 152 | tf_op jit(solution)/shard_map/slice | solution.py:278
  7.5 0.7 %fusion.26 = (s32[1,1,1,1]{3,2,1,0:T(1,128)}, s32[1,1,1,1]{3,2,1,0:T(1,128)}, s32[1,1,1,1]{3,2,1,0:T(1,128)}, s32[1,1,1,1]{3,2,1,0:T(1,128)}, s32[1,1,1,1]{3,2,1...) fusion(s32[1,1,1,27]{3,2,1,0:T(1,128)S(1)} %copy-done.5), kind=kLoop, calls=%fused_computation.47 | loop fusion | bytes 64 | tf_op jit(solution)/shard_map/slice | solution.py:278
  17.1 0.0 copy-start.6
  25.3 0.0 copy-start.2
  25.3 0.0 collective-permute-done.7
  25.3 0.0 copy-done.6
  25.3 0.0 copy-start.4
  25.4 0.0 copy-start.1
  25.4 0.1 collective-permute-start.8
  25.4 0.2 and_select_fusion.mask_ref
  25.6 0.6 %copy-done.2 = bf16[1,1,1,24,1536]{4,3,2,1,0:T(8,128)(2,1)S(1)} copy-done((bf16[1,1,1,24,1536]{4,3,2,1,0:T(8,128)(2,1)S(1)}, bf16[1,1,1,24,1536]{4,3,2,1,0:T(8,128)(2,1)}, u32[]{:S(2)}) %copy-start.2) | copy-done | bytes 73752
  26.2 0.0 copy-done.4
  26.2 0.1 shard_map.73.q_ref
  26.3 1.6 %collective-permute-start.5 = (bf16[32,1536]{1,0:T(8,128)(2,1)S(1)}, bf16[32,1536]{1,0:T(8,128)(2,1)S(1)}, u32[]{:S(2)}, u32[]{:S(2)}) collective-permute-start(bf16[32,1536]{1,0:T(8,128)(2,1)S(1)} %shard_map.73.q_ref), channel_id=1, source_target_pairs={{0,4},{4,0},{8,12},{12,8},{16,20},{20,16},{24,28},{28,24},{1,5},{5... | collective-permute-start | bytes 294920 | tf_op jit(solution)/shard_map/ppermute | solution.py:35
  27.9 0.0 collective-permute-start.6
  27.9 2.6 %collective-permute-done.8 = bf16[2,8,1536]{2,1,0:T(8,128)(2,1)S(1)} collective-permute-done((bf16[2,8,1536]{2,1,0:T(8,128)(2,1)S(1)}, bf16[2,8,1536]{2,1,0:T(8,128)(2,1)S(1)}, u32[]{:S(2)}, u32[]{:S(2)}) %collective-permute-start.8) | collective-permute-done | bytes 49184 | tf_op jit(solution)/shard_map/ppermute | solution.py:244
  30.4 0.0 copy-done.1
  30.4 0.0 collective-permute-start.2
  30.4 0.0 collective-permute-done.refs_1_
  30.4 0.5 %collective-permute-start.3 = (bf16[48,1536]{1,0:T(8,128)(2,1)S(1)}, bf16[48,1536]{1,0:T(8,128)(2,1)S(1)}, u32[]{:S(2)}, u32[]{:S(2)}) collective-permute-start(bf16[48,1536]{1,0:T(8,128)(2,1)S(1)} %collective-permute-done.refs_1_), channel_id=1, source_target_pairs={{0,16},{16,0},{1,17},{17,1},{2,18},{18,2},{3,19},{19,3},{4,20},{20... | collective-permute-start | bytes 442376 | tf_op jit(solution)/shard_map/ppermute | solution.py:45
  30.9 0.0 collective-permute-done.1.refs_2_
  30.9 0.1 collective-permute-start.4
  31.1 0.0 copy-start.3
  31.1 0.6 %collective-permute-done.5.refs_6_ = bf16[32,1536]{1,0:T(8,128)(2,1)S(1)} collective-permute-done((bf16[32,1536]{1,0:T(8,128)(2,1)S(1)}, bf16[32,1536]{1,0:T(8,128)(2,1)S(1)}, u32[]{:S(2)}, u32[]{:S(2)}) %collective-permute-start.5) | collective-permute-done | bytes 98336 | tf_op jit(solution)/shard_map/ppermute | solution.py:35
  31.7 0.0 collective-permute-done.6.refs_7_
  31.7 0.1 collective-permute-done.2.refs_3_
  31.8 0.2 collective-permute-done.3.refs_4_
  32.0 0.3 collective-permute-done.4.refs_5_
  32.3 0.0 copy-done.3
  32.3 2.2 %shard_map.74 = (bf16[144,1536]{1,0:T(8,128)(2,1)S(1)}, bf16[144,1536]{1,0:T(8,128)(2,1)S(1)}, bf16[24,1664]{1,0:T(8,128)(2,1)S(1)}, bf16[24,1664]{1,0:T(8,128)(2,1)S(1)}) custom-call(bf16[48,1536]{1,0:T(8,128)(2,1)S(1)} %bitcast.41, bf16[48,1536]{1,0:T(8,128)(2,1)S(1)} %collective-permute-done.refs_1_, bf16[48,1536]{1,0:T(8,128)(2,1)S(1)} %collective-permute-done.1.refs_2_, ...), custom_call_target="tpu_custom_call" | custom-call | flops 56623104 | bytes 1081856 | tf_op jit(solution)/shard_map/pallas_call | solution.py:55
  34.6 0.0 copy-start
  34.6 0.3 collective-permute-start.10
  34.8 3.8 %collective-permute-start.9 = (bf16[24,1664]{1,0:T(8,128)(2,1)S(1)}, bf16[24,1664]{1,0:T(8,128)(2,1)S(1)}, u32[]{:S(2)}, u32[]{:S(2)}) collective-permute-start(bf16[24,1664]{1,0:T(8,128)(2,1)S(1)} %get-tuple-element.15), channel_id=1, source_target_pairs={{0,4},{4,0},{8,12},{12,8},{16,20},{20,16},{24,28},{28,24},{1,5},{5... | collective-permute-start | bytes 239624 | tf_op jit(solution)/shard_map/ppermute | solution.py:35
  38.7 0.0 copy-done
  38.7 2.1 %shard_map.75 = (f32[24,1536]{1,0:T(8,128)S(1)}, f32[24,128]{1,0:T(8,128)S(1)}) custom-call(bf16[32,1536]{1,0:T(8,128)(2,1)S(1)} %shard_map.73.q_ref, bf16[144,1536]{1,0:T(8,128)(2,1)S(1)} %get-tuple-element.11.keys_ref, bf16[144,1536]{1,0:T(8,128)(2,1)S(1)} %get-tuple-element.12.vals_ref, bf16[48,1536]{1,0:T(8,128)(2,1)S(1)} %bitcast.37, ...), custom_call_target="tpu_custom_call" | custom-call | flops 36175872 | bytes 1229312 | tf_op jit(solution)/shard_map/pallas_call | solution.py:55
  40.8 0.0 collective-permute-done.10.refs_1_
  40.8 1.1 %collective-permute-done.9.refs_0_ = bf16[24,1664]{1,0:T(8,128)(2,1)S(1)} collective-permute-done((bf16[24,1664]{1,0:T(8,128)(2,1)S(1)}, bf16[24,1664]{1,0:T(8,128)(2,1)S(1)}, u32[]{:S(2)}, u32[]{:S(2)}) %collective-permute-start.9) | collective-permute-done | bytes 79904 | tf_op jit(solution)/shard_map/ppermute | solution.py:35
  41.9 0.8 %shard_map.76 = bf16[24,1536]{1,0:T(8,128)(2,1)} custom-call(f32[24,1536]{1,0:T(8,128)S(1)} %get-tuple-element.13.total_ref, f32[24,128]{1,0:T(8,128)S(1)} %get-tuple-element.14.sum_ref, bf16[24,1664]{1,0:T(8,128)(2,1)S(1)} %collective-permute-done.9.refs_0_, bf16[24,1664]{1,0:T(8,128)(2,1)S(1)} %collective-permute-done.10.refs_1_), custom_call_target="tpu_custom_call" | custom-call | tf_op jit(solution)/shard_map/pallas_call | solution.py:230
  (7 shorter events, 0.1 us)
Async XLA Ops:
  0.0 30.4 %collective-permute-start = (bf16[48,1536]{1,0:T(8,128)(2,1)}, bf16[48,1536]{1,0:T(8,128)(2,1)S(1)}, u32[]{:S(2)}, u32[]{:S(2)}) collective-permute-start(bf16[48,1536]{1,0:T(8,128)(2,1)} %bitcast.38), channel_id=1, source_target_pairs={{0,1},{1,0},{2,3},{3,2},{16,17},{17,16},{18,19},{19,18},{4,5},{5,4... | collective-permute-start | bytes 442376 | tf_op jit(solution)/shard_map/ppermute | solution.py:35
  3.0 27.9 %collective-permute-start.1 = (bf16[48,1536]{1,0:T(8,128)(2,1)}, bf16[48,1536]{1,0:T(8,128)(2,1)S(1)}, u32[]{:S(2)}, u32[]{:S(2)}) collective-permute-start(bf16[48,1536]{1,0:T(8,128)(2,1)} %bitcast.39), channel_id=1, source_target_pairs={{0,16},{1,2},{2,1},{3,19},{16,0},{17,18},{18,17},{19,3},{4,20},{5,... | collective-permute-start | bytes 442376 | tf_op jit(solution)/shard_map/ppermute | solution.py:35
  3.0 22.3 %collective-permute-start.7 = (bf16[2,4,1536]{2,1,0:T(4,128)(2,1)}, bf16[2,4,1536]{2,1,0:T(4,128)(2,1)S(1)}, u32[]{:S(2)}, u32[]{:S(2)}) collective-permute-start(bf16[2,4,1536]{2,1,0:T(4,128)(2,1)} %param.10), channel_id=1, source_target_pairs={{0,1},{1,0},{2,3},{3,2},{4,5},{5,4},{6,7},{7,6},{8,9},{9,8},{10,11... | collective-permute-start | bytes 73736 | tf_op jit(solution)/shard_map/ppermute | solution.py:244
  6.2 0.7 %copy-start.5 = (s32[1,1,1,27]{3,2,1,0:T(1,128)S(1)}, s32[1,1,1,27]{3,2,1,0:T(1,128)}, u32[]{:S(2)}) copy-start(s32[1,1,1,27]{3,2,1,0:T(1,128)} %param.13) | copy-start | bytes 328
  17.1 8.2 %copy-start.6 = (bf16[2,4,1536]{2,1,0:T(4,128)(2,1)S(1)}, bf16[2,4,1536]{2,1,0:T(4,128)(2,1)}, u32[]{:S(2)}) copy-start(bf16[2,4,1536]{2,1,0:T(4,128)(2,1)} %param.10) | copy-start | bytes 73732
  25.3 0.9 %copy-start.2 = (bf16[1,1,1,24,1536]{4,3,2,1,0:T(8,128)(2,1)S(1)}, bf16[1,1,1,24,1536]{4,3,2,1,0:T(8,128)(2,1)}, u32[]{:S(2)}) copy-start(bf16[1,1,1,24,1536]{4,3,2,1,0:T(8,128)(2,1)} %param.7) | copy-start | bytes 221188
  25.3 0.9 %copy-start.4 = (f32[128]{0:T(128)S(1)}, f32[128]{0:T(128)}, u32[]{:S(2)}) copy-start(f32[128]{0:T(128)} %param.11) | copy-start | bytes 1540
  25.4 5.1 %copy-start.1 = (bf16[1,1,1,2,24,1536]{5,4,3,2,1,0:T(8,128)(2,1)S(1)}, bf16[1,1,1,2,24,1536]{5,4,3,2,1,0:T(8,128)(2,1)}, u32[]{:S(2)}) copy-start(bf16[1,1,1,2,24,1536]{5,4,3,2,1,0:T(8,128)(2,1)} %param.9) | copy-start | bytes 442372
  25.4 5.1 %collective-permute-start.8 = (bf16[2,8,1536]{2,1,0:T(8,128)(2,1)S(1)}, bf16[2,8,1536]{2,1,0:T(8,128)(2,1)S(1)}, u32[]{:S(2)}, u32[]{:S(2)}) collective-permute-start(bf16[2,8,1536]{2,1,0:T(8,128)(2,1)S(1)} %pad_maximum_fusion.1), channel_id=1, source_target_pairs={{0,2},{1,3},{2,0},{3,1},{4,6},{5,7},{6,4},{7,5},{8,10},{9,11},{10,... | collective-permute-start | bytes 147464 | tf_op jit(solution)/shard_map/ppermute | solution.py:244
  26.3 5.4 %collective-permute-start.5 = (bf16[32,1536]{1,0:T(8,128)(2,1)S(1)}, bf16[32,1536]{1,0:T(8,128)(2,1)S(1)}, u32[]{:S(2)}, u32[]{:S(2)}) collective-permute-start(bf16[32,1536]{1,0:T(8,128)(2,1)S(1)} %shard_map.73.q_ref), channel_id=1, source_target_pairs={{0,4},{4,0},{8,12},{12,8},{16,20},{20,16},{24,28},{28,24},{1,5},{5... | collective-permute-start | bytes 294920 | tf_op jit(solution)/shard_map/ppermute | solution.py:35
  27.9 3.8 %collective-permute-start.6 = (bf16[32,1536]{1,0:T(8,128)(2,1)S(1)}, bf16[32,1536]{1,0:T(8,128)(2,1)S(1)}, u32[]{:S(2)}, u32[]{:S(2)}) collective-permute-start(bf16[32,1536]{1,0:T(8,128)(2,1)S(1)} %shard_map.73.q_ref), channel_id=1, source_target_pairs={{0,16},{4,8},{8,4},{12,28},{16,0},{20,24},{24,20},{28,12},{1,17},{... | collective-permute-start | bytes 294920 | tf_op jit(solution)/shard_map/ppermute | solution.py:35
  30.4 1.4 %collective-permute-start.2 = (bf16[48,1536]{1,0:T(8,128)(2,1)S(1)}, bf16[48,1536]{1,0:T(8,128)(2,1)S(1)}, u32[]{:S(2)}, u32[]{:S(2)}) collective-permute-start(bf16[48,1536]{1,0:T(8,128)(2,1)S(1)} %bitcast.40), channel_id=1, source_target_pairs={{0,16},{16,0},{1,17},{17,1},{2,18},{18,2},{3,19},{19,3},{4,20},{20... | collective-permute-start | bytes 442376 | tf_op jit(solution)/shard_map/ppermute | solution.py:45
  30.4 1.6 %collective-permute-start.3 = (bf16[48,1536]{1,0:T(8,128)(2,1)S(1)}, bf16[48,1536]{1,0:T(8,128)(2,1)S(1)}, u32[]{:S(2)}, u32[]{:S(2)}) collective-permute-start(bf16[48,1536]{1,0:T(8,128)(2,1)S(1)} %collective-permute-done.refs_1_), channel_id=1, source_target_pairs={{0,16},{16,0},{1,17},{17,1},{2,18},{18,2},{3,19},{19,3},{4,20},{20... | collective-permute-start | bytes 442376 | tf_op jit(solution)/shard_map/ppermute | solution.py:45
  30.9 1.4 %collective-permute-start.4 = (bf16[48,1536]{1,0:T(8,128)(2,1)S(1)}, bf16[48,1536]{1,0:T(8,128)(2,1)S(1)}, u32[]{:S(2)}, u32[]{:S(2)}) collective-permute-start(bf16[48,1536]{1,0:T(8,128)(2,1)S(1)} %collective-permute-done.1.refs_2_), channel_id=1, source_target_pairs={{0,16},{16,0},{1,17},{17,1},{2,18},{18,2},{3,19},{19,3},{4,20},{20... | collective-permute-start | bytes 442376 | tf_op jit(solution)/shard_map/ppermute | solution.py:45
  31.1 1.3 %copy-start.3 = (f32[128]{0:T(128)S(1)}, f32[128]{0:T(128)}, u32[]{:S(2)}) copy-start(f32[128]{0:T(128)} %param.12) | copy-start | bytes 1540
  34.6 4.1 %copy-start = (bf16[1,1,1,2,24,1536]{5,4,3,2,1,0:T(8,128)(2,1)S(1)}, bf16[1,1,1,2,24,1536]{5,4,3,2,1,0:T(8,128)(2,1)}, u32[]{:S(2)}) copy-start(bf16[1,1,1,2,24,1536]{5,4,3,2,1,0:T(8,128)(2,1)} %param.8) | copy-start | bytes 442372
  34.6 6.2 %collective-permute-start.10 = (bf16[24,1664]{1,0:T(8,128)(2,1)S(1)}, bf16[24,1664]{1,0:T(8,128)(2,1)S(1)}, u32[]{:S(2)}, u32[]{:S(2)}) collective-permute-start(bf16[24,1664]{1,0:T(8,128)(2,1)S(1)} %get-tuple-element.16), channel_id=1, source_target_pairs={{0,16},{4,8},{8,4},{12,28},{16,0},{20,24},{24,20},{28,12},{1,17},{... | collective-permute-start | bytes 239624 | tf_op jit(solution)/shard_map/ppermute | solution.py:35
  34.8 7.1 %collective-permute-start.9 = (bf16[24,1664]{1,0:T(8,128)(2,1)S(1)}, bf16[24,1664]{1,0:T(8,128)(2,1)S(1)}, u32[]{:S(2)}, u32[]{:S(2)}) collective-permute-start(bf16[24,1664]{1,0:T(8,128)(2,1)S(1)} %get-tuple-element.15), channel_id=1, source_target_pairs={{0,4},{4,0},{8,12},{12,8},{16,20},{20,16},{24,28},{28,24},{1,5},{5... | collective-permute-start | bytes 239624 | tf_op jit(solution)/shard_map/ppermute | solution.py:35

commit v2 on v0

v2 whole, which is shorter than its diff:
```python
import jax
import jax.numpy as jnp
from jax import lax
from jax.experimental import pallas as pl
from jax.experimental.pallas import tpu as pltpu
from jax.sharding import PartitionSpec as P

EPS = 1e-06
LANES = 128
IN_VMEM = pl.BlockSpec(memory_space=pltpu.VMEM)
IN_SMEM = pl.BlockSpec(memory_space=pltpu.SMEM)


def parities(count):
    return [parity for parity in (0, 1) if count - parity >= 2]


def matching(axis_size, ta_size, parity):
    pairs = []
    for t in range(ta_size):
        for a in range(axis_size):
            b = a + 1 if a % 2 == parity else a - 1
            if 0 <= b < axis_size:
                pairs.append((t * axis_size + a, t * axis_size + b))
            elif t ^ 1 < ta_size:
                pairs.append((t * axis_size + a, (t ^ 1) * axis_size + a))
    return pairs


def swap_along(values, axis, parity):
    pairs = matching(lax.axis_size(axis), lax.axis_size("ta"), parity)
    return lax.ppermute(values, ("ta", axis), pairs)


def swap_ta(values, parity):
    count = lax.axis_size("ta")
    pairs = []
    for t in range(count):
        u = t + 1 if t % 2 == parity else t - 1
        if 0 <= u < count:
            pairs.append((t, u))
    return lax.ppermute(values, "ta", pairs)


def resident(values):
    return pltpu.with_memory_space_constraint(values, pltpu.VMEM)


def call(body, out_shape, *operands, flops=0, exps=0):
    outs = [pltpu.VMEM(s.shape, s.dtype) for s in out_shape]
    moved = sum(x.size * x.dtype.itemsize for x in operands)
    return pl.pallas_call(
        body,
        out_shape=outs,
        in_specs=[IN_VMEM] * len(operands),
        out_specs=[IN_VMEM] * len(outs),
        cost_estimate=pl.CostEstimate(flops=flops, bytes_accessed=moved, transcendentals=exps),
    )(*[resident(x) for x in operands])


def head_normed(values, gain, heads):
    hd = gain.shape[-1]
    parts = []
    for head in range(heads):
        part = values[:, head * hd : (head + 1) * hd]
        square = jnp.mean(part * part, axis=-1, keepdims=True)
        parts.append(part * lax.rsqrt(square + EPS) * gain)
    return jnp.concatenate(parts, axis=1)


def split(values, heads):
    hd = values.shape[1] // heads
    return [values[:, head * hd : (head + 1) * hd] for head in range(heads)]


def attention(queries, groups, heads):
    scale = (queries.shape[1] // heads) ** (-0.5)
    queries = split(queries, heads)
    totals, weights = [0.0] * heads, [0.0] * heads
    for keys, vals, mask in groups:
        scores = [
            lax.dot_general(q, k, (((1,), (1,)), ((), ())), preferred_element_type=jnp.float32)
            for q, k in zip(queries, split(keys, heads), strict=True)
        ]
        expos = [jnp.exp(x * scale) for x in scores]
        if mask is not None:
            expos = [x * mask for x in expos]
        sums = [
            jnp.dot(x.astype(jnp.bfloat16), v, preferred_element_type=jnp.float32)
            for x, v in zip(expos, split(vals, heads), strict=True)
        ]
        totals = [x + y for x, y in zip(totals, sums, strict=True)]
        weights = [x + jnp.sum(y, axis=1, keepdims=True) for x, y in zip(weights, expos, strict=True)]
    return totals, weights


def in_lanes(columns):
    lane = lax.broadcasted_iota(jnp.int32, (columns[0].shape[0], LANES), 1)
    rows = jnp.zeros(lane.shape, jnp.float32)
    for h, column in enumerate(columns):
        rows = jnp.where(lane == h, column, rows)
    return rows


def normed_tiles(both, gain, heads, tile):
    both = [b.astype(jnp.float32) for b in both]
    keys = jnp.concatenate([head_normed(b[:tile], gain, heads) for b in both], axis=0)
    vals = jnp.concatenate([b[tile:] for b in both], axis=0)
    return keys.astype(jnp.bfloat16), vals.astype(jnp.bfloat16)


def slot_flags(pattern_ref, axes, sizes, rows):
    place = [lax.axis_index(a) for a in axes]
    steps_h, steps_w = (
        [jnp.where(place[i] % 2 == parity, 1, -1) for parity in parities(sizes[i])] for i in (1, 2)
    )
    lane = lax.broadcasted_iota(jnp.int32, (rows, LANES), 1)
    row = lax.broadcasted_iota(jnp.int32, (rows, LANES), 0)
    flags = jnp.zeros((rows, LANES), jnp.float32)
    for r, dh in enumerate([*steps_h, 0]):
        slot = 0
        for t in range(sizes[0]):
            dt = t - place[0]
            for dw in [0, *steps_w]:
                inside = (dt >= -1) & (dt <= 1)
                for i, d in ((1, dh), (2, dw)):
                    inside = inside & (place[i] + d >= 0) & (place[i] + d < sizes[i])
                offset = (jnp.clip(dt, -1, 1) + 1) * 9 + (dh + 1) * 3 + dw + 1
                used = jnp.where(inside & (pattern_ref[offset] == 1) & (offset != 13), 1.0, 0.0)
                flags = jnp.where((row == r) & (lane == slot), used, flags)
                slot += 1
    return flags


def key_masks(flags, places, line, tile):
    masks = []
    for t in range(places):
        lane = lax.broadcasted_iota(jnp.int32, (1, line * tile), 1) // tile
        mask = jnp.zeros(lane.shape, jnp.float32)
        for i in range(line):
            slot = t * line + i
            mask = jnp.where(lane == i, flags[:, slot : slot + 1], mask)
        masks.append(mask)
    return masks


def prepare(queries, q_gain, pattern, axes, sizes):
    tile, width = queries.shape
    heads = width // q_gain.shape[-1]

    def body(q_ref, gain_ref, pattern_ref, out_ref):
        normed = head_normed(q_ref[...].astype(jnp.float32), gain_ref[...], heads)
        flags = slot_flags(pattern_ref, axes, sizes, tile)
        out_ref[...] = jnp.concatenate([normed, flags], axis=1).astype(jnp.bfloat16)

    return pl.pallas_call(
        body,
        out_shape=pltpu.VMEM((tile, width + LANES), jnp.bfloat16),
        in_specs=[IN_VMEM, IN_VMEM, IN_SMEM],
        out_specs=IN_VMEM,
    )(queries, q_gain, pattern)


def norm_line(slots, text, k_gain, tile):
    width = slots[0].shape[1]
    heads = width // k_gain.shape[-1]

    def body(*refs):
        slot_refs, (text_ref, gain_ref, line_ref, text_out_ref) = refs[:-4], refs[-4:]
        gain = gain_ref[...]
        keys, vals = normed_tiles([r[...] for r in slot_refs], gain, heads, tile)
        text_keys = head_normed(text_ref[0].astype(jnp.float32), gain, heads)
        line_ref[:, :width] = keys
        line_ref[:, width:] = vals
        text_out_ref[0] = text_keys.astype(jnp.bfloat16)
        text_out_ref[1] = text_ref[1]

    shapes = [
        jax.ShapeDtypeStruct((len(slots) * tile, 2 * width), jnp.bfloat16),
        jax.ShapeDtypeStruct(text.shape, text.dtype),
    ]
    return call(body, shapes, *slots, text, k_gain)


def attend_partners(around, sent, tile, hd):
    places, rows, width = around.shape
    width //= 2
    line = rows // tile
    heads = width // hd

    def body(around_ref, *refs):
        sent_refs, back_refs = refs[: len(sent)], refs[len(sent) :]
        blocks = [r[...].astype(jnp.float32) for r in sent_refs]
        masks = [
            key_masks(block[i : i + 1, width:], places, line, tile) for i, block in enumerate(blocks)
        ]
        groups = []
        for t in range(places):
            mask = [jnp.broadcast_to(m[t], (tile, rows)) for m in masks]
            groups.append(
                (around_ref[t, :, :width], around_ref[t, :, width:], jnp.concatenate(mask, axis=0))
            )
        queries = jnp.concatenate([b[:, :width] for b in blocks], axis=0).astype(jnp.bfloat16)
        totals, weights = attention(queries, groups, heads)
        sums = in_lanes(weights)
        high = sums.astype(jnp.bfloat16).astype(jnp.float32)
        packed = high + pltpu.roll(sums - high, LANES // 2, 1)
        whole = jnp.concatenate([*totals, packed], axis=1)
        for i, back in enumerate(back_refs):
            back[...] = whole[i * tile : (i + 1) * tile].astype(jnp.bfloat16)

    shapes = [jax.ShapeDtypeStruct((tile, width + LANES), jnp.bfloat16)] * len(sent)
    return call(body, shapes, around, *sent)


def attend_own(own, around, current, text, k_gain, tile, reader):
    places, rows, width = around.shape
    width //= 2
    line = rows // tile
    heads = width // k_gain.shape[-1]

    def body(own_ref, around_ref, current_ref, gain_ref, *refs):
        text_refs, (total_ref, sum_ref) = refs[:-2], refs[-2:]
        here = current_ref[...].astype(jnp.float32)
        sure_keys = [head_normed(here[:tile], gain_ref[...], heads)]
        sure_vals = [here[tile:]]
        for r in text_refs:
            sure_keys.append(r[0].astype(jnp.float32))
            sure_vals.append(r[1].astype(jnp.float32))
        sure_keys, sure_vals = (
            jnp.concatenate(x, axis=0).astype(jnp.bfloat16) for x in (sure_keys, sure_vals)
        )
        flags = own_ref[:, width:].astype(jnp.float32)[reader : reader + 1]
        masks = key_masks(flags, places, line, tile)
        groups = [(sure_keys, sure_vals, None)]
        for t in range(places):
            groups.append((around_ref[t, :, :width], around_ref[t, :, width:], masks[t]))
        totals, weights = attention(own_ref[:, :width], groups, heads)
        total_ref[...] = jnp.concatenate(totals, axis=1)
        sum_ref[...] = in_lanes(weights)

    shapes = [
        jax.ShapeDtypeStruct((tile, width), jnp.float32),
        jax.ShapeDtypeStruct((tile, LANES), jnp.float32),
    ]
    return call(body, shapes, own, around, current, k_gain, *text)


def combine(total, weight, backs, hd):
    tile, width = total.shape
    heads = width // hd

    def body(total_ref, sum_ref, *refs):
        back_refs, out_ref = refs[:-1], refs[-1]
        parts = [r[...].astype(jnp.float32) for r in back_refs]
        whole, sums = total_ref[...], sum_ref[...]
        for part in parts:
            tail = part[:, width:]
            whole = whole + part[:, :width]
            sums = sums + tail + pltpu.roll(tail, LANES // 2, 1)
        inverse = 1.0 / jnp.where(lax.broadcasted_iota(jnp.int32, sums.shape, 1) < heads, sums, 1.0)
        scaled = [x * inverse[:, h : h + 1] for h, x in enumerate(split(whole, heads))]
        out_ref[...] = jnp.concatenate(scaled, axis=1).astype(jnp.bfloat16)

    operands = [total, weight, *backs]
    return pl.pallas_call(
        body,
        out_shape=jax.ShapeDtypeStruct((tile, width), jnp.bfloat16),
        in_specs=[IN_VMEM] * len(operands),
        out_specs=IN_VMEM,
    )(*[resident(x) for x in operands])


def gather_text(text):
    count, cores = lax.axis_size("wa"), lax.axis_size("ta")
    if count & (count - 1):
        return [lax.all_gather(text, "wa", axis=1, tiled=True)]
    near = lax.ppermute(text, "wa", [(i, i ^ 1) for i in range(count)]) if count > 1 else None
    if count == 4 and cores % 2 == 0:
        pairs = [(t * 4 + i, t * 4 + (i ^ (2 + t % 2))) for t in range(cores) for i in range(4)]
        far = lax.ppermute(text, ("ta", "wa"), pairs)
        return [text, near, far, swap_ta(far, 0)]
    if count > 1:
        text = jnp.concatenate([text, near], axis=1)
    span = 2
    while span < count:
        other = lax.ppermute(text, "wa", [(i, i ^ span) for i in range(count)])
        text = jnp.concatenate([text, other], axis=1)
        span *= 2
    return [text]


def shards(queries, current_kv, stale_kv, text_kv, q_gain, k_gain, pattern):
    tile, width = queries.shape[3:]
    hd = q_gain.shape[0]
    stale = stale_kv.reshape(2 * tile, width)
    current = current_kv.reshape(2 * tile, width)
    k_gain = k_gain.reshape(1, hd)
    axes = ("ta", "ha", "wa")
    sizes = [lax.axis_size(a) for a in axes]
    parities_h, parities_w = parities(sizes[1]), parities(sizes[2])

    line = [stale] + [swap_along(stale, "wa", p) for p in parities_w]
    own = prepare(
        queries.reshape(tile, width), q_gain.reshape(1, hd), pattern.reshape(27), axes, sizes
    )
    sent = [swap_along(own, "ha", p) for p in parities_h]
    line_kv, text = norm_line(line, text_kv, k_gain, tile)
    around = lax.all_gather(line_kv, "ta")
    text = gather_text(text)
    answers = attend_partners(around, sent, tile, hd)
    backs = [swap_along(x, "ha", p) for x, p in zip(answers, parities_h, strict=True)]
    total, weight = attend_own(own, around, current, text, k_gain, tile, len(parities_h))
    result = combine(total, weight, backs, hd)
    return result.reshape(1, 1, 1, tile, width)


def solution(mesh):
    return jax.shard_map(
        shards,
        mesh=mesh,
        in_specs=(
            P("ta", "ha", "wa", None, None),
            P("ta", "ha", "wa", None, None, None),
            P("ta", "ha", "wa", None, None, None),
            P(None, "wa", None),
            P(),
            P(),
            P("ta", "ha", "wa", None),
        ),
        out_specs=P("ta", "ha", "wa", None, None),
        check_vma=False,
    )
```

time: 125 us -> 22.5 us (0.18)
  blocking collectives: 39.5 us -> 2.44 us
  local copies, waits for them, and re-layouts: 29 us -> 0.75 us
  other arithmetic: 17.1 us -> 0 us
  waiting for transfers between devices: 20.5 us -> 4.6 us
  starting transfers between devices: 15.2 us -> 10.9 us
  Pallas kernels: 0 us -> 3.54 us
  matrix products: 2.36 us -> 0 us
    all_gather x1, blocking collectives: 39.5 us -> 2.44 us  [shards(): around = lax.all_gather(line_kv, 'ta')]
    ppermute x6 -> x9, waiting for transfers between devices: 20.5 us -> 4.6 us  [the longest x1 1.68 us: gather_text(): lax.ppermute(text, 'wa', [(i, i ^ 1) for i in range(count)])]
    mul x10 -> x0, local copies, waits for them, and re-layouts: 14.9 us -> none  [the longest x7 9.37 us: qk_normed(): shaped * lax.rsqrt(square + 1e-06) * gain]
    reshape x2 -> x0, local copies, waits for them, and re-layouts: 7.52 us -> none  [the longest x1 3.76 us: shards(): near_vals = near_vals.reshape(27 * tile, heads, head_dim)]
    concatenate x3 -> x0, other arithmetic: 4.73 us -> none  [with_halo(): jnp.concatenate([lax.ppermute(tail, axis, [(i, (i + 1) % count) for i in...]
    mul x3 -> x0, other arithmetic: 4.42 us -> none  [qk_normed(): square = jnp.mean(shaped * shaped, axis=-1, keepdims=True)]
    ppermute x6 -> x9, starting transfers between devices: 15.2 us -> 10.9 us  [the longest x6 7.4 us: swap_along(): return lax.ppermute(values, ('ta', axis), pairs)]
    reduce_sum x4 -> x0, other arithmetic: 4.29 us -> none  [qk_normed(): square = jnp.mean(shaped * shaped, axis=-1, keepdims=True)]
  transfers between devices with their start and end apart: 6 -> 9, of which waited for: 2 -> 3; matrix products, arithmetic and copies ran while one was open for 3% -> 0% of each run, Pallas kernels for 0% -> 9%
where the time goes in v2:
time: 22.5 us; the launch traced here: 22.2 us
  starting transfers between devices  10.9 us (48%)
  waiting for transfers between devices  4.6 us (20%)
  Pallas kernels  3.54 us (16%)
  blocking collectives  2.44 us (11%)
  local copies, waits for them, and re-layouts  0.75 us (3%)
    ppermute x6, starting transfers between devices, swap_along(): return lax.ppermute(values, ('ta', axis), pairs)  7.4 us
    ppermute x1, starting transfers between devices, gather_text(): far = lax.ppermute(text, ('ta', 'wa'), pairs)  2.94 us
    all_gather x1, blocking collectives, shards(): around = lax.all_gather(line_kv, 'ta')  2.44 us
    ppermute x1, waiting for transfers between devices, gather_text(): lax.ppermute(text, 'wa', [(i, i ^ 1) for i in range(count)])  1.68 us
    pallas_call x3, Pallas kernels, call(): pl.pallas_call(body, out_shape=outs, in_specs=[IN_VMEM] * len(operands),...  1.67 us
    ppermute x1, waiting for transfers between devices, gather_text(): far = lax.ppermute(text, ('ta', 'wa'), pairs)  1.61 us
    ppermute x6, waiting for transfers between devices, swap_along(): return lax.ppermute(values, ('ta', axis), pairs)  1.31 us
    pallas_call x1, Pallas kernels, prepare(): pl.pallas_call(body, out_shape=pltpu.VMEM((tile, width + LANES), jnp.bflo...  1.02 us
  transfers between devices with their start and end apart: 9, of which 3 were waited for; matrix products, arithmetic and copies ran while one was open for 0% of the time, Pallas kernels for 9%

profile of v2, /device:TPU:0, one launch (start us, length us, event | category | flops | bytes accessed | tf_op | source)
XLA Modules:
  0.0 22.2 jit_solution(5146684092777161397)
XLA Ops:
  0.0 0.0 copy-start.1
  0.0 3.0 %collective-permute-start = (bf16[48,1536]{1,0:T(8,128)(2,1)}, bf16[48,1536]{1,0:T(8,128)(2,1)S(1)}, u32[]{:S(2)}, u32[]{:S(2)}) collective-permute-start(bf16[48,1536]{1,0:T(8,128)(2,1)} %bitcast.11), channel_id=1, source_target_pairs={{0,1},{1,0},{2,3},{3,2},{16,17},{17,16},{18,19},{19,18},{4,5},{5,4... | collective-permute-start | bytes 442376 | tf_op jit(solution)/shard_map/ppermute | solution.py:32
  3.0 0.0 collective-permute-start.1
  3.0 1.0 %shard_map.73.own_ref = bf16[24,1664]{1,0:T(8,128)(2,1)S(1)} custom-call(bf16[24,1536]{1,0:T(8,128)(2,1)} %bitcast.16, f32[1,128]{1,0:T(1,128)} %bitcast.17, s32[27]{0:T(128)} %bitcast.18), custom_call_target="tpu_custom_call" | custom-call | tf_op jit(solution)/shard_map/pallas_call | solution.py:156
  4.1 0.0 copy-start.3
  4.1 1.6 %collective-permute-start.5 = (bf16[24,1664]{1,0:T(8,128)(2,1)S(1)}, bf16[24,1664]{1,0:T(8,128)(2,1)S(1)}, u32[]{:S(2)}, u32[]{:S(2)}) collective-permute-start(bf16[24,1664]{1,0:T(8,128)(2,1)S(1)} %shard_map.73.own_ref), channel_id=1, source_target_pairs={{0,4},{4,0},{8,12},{12,8},{16,20},{20,16},{24,28},{28,24},{1,5},{5... | collective-permute-start | bytes 239624 | tf_op jit(solution)/shard_map/ppermute | solution.py:32
  5.6 0.2 %collective-permute-start.6 = (bf16[24,1664]{1,0:T(8,128)(2,1)S(1)}, bf16[24,1664]{1,0:T(8,128)(2,1)S(1)}, u32[]{:S(2)}, u32[]{:S(2)}) collective-permute-start(bf16[24,1664]{1,0:T(8,128)(2,1)S(1)} %shard_map.73.own_ref), channel_id=1, source_target_pairs={{0,16},{4,8},{8,4},{12,28},{16,0},{20,24},{24,20},{28,12},{1,17},{... | collective-permute-start | bytes 239624 | tf_op jit(solution)/shard_map/ppermute | solution.py:32
  5.9 1.3 %collective-permute-done.refs_1_ = bf16[48,1536]{1,0:T(8,128)(2,1)S(1)} collective-permute-done((bf16[48,1536]{1,0:T(8,128)(2,1)}, bf16[48,1536]{1,0:T(8,128)(2,1)S(1)}, u32[]{:S(2)}, u32[]{:S(2)}) %collective-permute-start) | collective-permute-done | bytes 147488 | tf_op jit(solution)/shard_map/ppermute | solution.py:32
  7.2 0.0 collective-permute-done.1.refs_2_
  7.2 0.0 copy-done.1
  7.2 0.0 copy-done.3
  7.2 0.0 copy-start.2
  7.2 0.7 %copy-done.2 = bf16[2,4,1536]{2,1,0:T(4,128)(2,1)S(1)} copy-done((bf16[2,4,1536]{2,1,0:T(4,128)(2,1)S(1)}, bf16[2,4,1536]{2,1,0:T(4,128)(2,1)}, u32[]{:S(2)}) %copy-start.2) | copy-done | bytes 24600
  7.9 0.2 shard_map.74
  8.1 2.4 %all-gather = bf16[144,3072]{1,0:T(8,128)(2,1)S(1)} all-gather(bf16[72,3072]{1,0:T(8,128)(2,1)S(1)} %get-tuple-element.11), channel_id=2, replica_groups=mesh['ta'=2,'ha'=4,'wa'=4] {'ta'}, dimensions={0}, use_global_device_ids=true | all-gather | bytes 1327104 | tf_op jit(solution)/shard_map/all_gather | solution.py:309
  10.6 0.0 collective-permute-done.5.refs_0_
  10.6 0.0 collective-permute-done.6.refs_1_
  10.6 0.0 copy-start
  10.6 0.6 %shard_map.76 = (bf16[24,1664]{1,0:T(8,128)(2,1)S(1)}, bf16[24,1664]{1,0:T(8,128)(2,1)S(1)}) custom-call(bf16[2,72,3072]{2,1,0:T(8,128)(2,1)S(1)} %bitcast.8, bf16[24,1664]{1,0:T(8,128)(2,1)S(1)} %collective-permute-done.5.refs_0_, bf16[24,1664]{1,0:T(8,128)(2,1)S(1)} %collective-permute-done.6.refs_1_), custom_call_target="tpu_custom_call" | custom-call | bytes 1044480 | tf_op jit(solution)/shard_map/pallas_call | solution.py:52
  11.2 2.6 %collective-permute-start.7 = (bf16[24,1664]{1,0:T(8,128)(2,1)S(1)}, bf16[24,1664]{1,0:T(8,128)(2,1)S(1)}, u32[]{:S(2)}, u32[]{:S(2)}) collective-permute-start(bf16[24,1664]{1,0:T(8,128)(2,1)S(1)} %get-tuple-element.15), channel_id=1, source_target_pairs={{0,4},{4,0},{8,12},{12,8},{16,20},{20,16},{24,28},{28,24},{1,5},{5... | collective-permute-start | bytes 239624 | tf_op jit(solution)/shard_map/ppermute | solution.py:32
  13.8 0.0 collective-permute-start.8
  13.8 2.9 %collective-permute-start.3 = (bf16[2,4,1536]{2,1,0:T(4,128)(2,1)S(1)}, bf16[2,4,1536]{2,1,0:T(4,128)(2,1)S(1)}, u32[]{:S(2)}, u32[]{:S(2)}) collective-permute-start(bf16[2,4,1536]{2,1,0:T(4,128)(2,1)S(1)} %get-tuple-element.12.refs_0_), channel_id=1, source_target_pairs={{0,2},{1,3},{2,0},{3,1},{16,19},{17,18},{18,17},{19,16},{4,6},{5,7... | collective-permute-start | bytes 73736 | tf_op jit(solution)/shard_map/ppermute | solution.py:281
  16.7 0.3 %collective-permute-start.2 = (bf16[2,4,1536]{2,1,0:T(4,128)(2,1)S(1)}, bf16[2,4,1536]{2,1,0:T(4,128)(2,1)S(1)}, u32[]{:S(2)}, u32[]{:S(2)}) collective-permute-start(bf16[2,4,1536]{2,1,0:T(4,128)(2,1)S(1)} %get-tuple-element.12.refs_0_), channel_id=1, source_target_pairs={{0,1},{1,0},{2,3},{3,2},{4,5},{5,4},{6,7},{7,6},{8,9},{9,8},{10,11... | collective-permute-start | bytes 73736 | tf_op jit(solution)/shard_map/ppermute | solution.py:278
  17.0 1.6 %collective-permute-done.3.refs_2_ = bf16[2,4,1536]{2,1,0:T(4,128)(2,1)S(1)} collective-permute-done((bf16[2,4,1536]{2,1,0:T(4,128)(2,1)S(1)}, bf16[2,4,1536]{2,1,0:T(4,128)(2,1)S(1)}, u32[]{:S(2)}, u32[]{:S(2)}) %collective-permute-start.3) | collective-permute-done | bytes 24608 | tf_op jit(solution)/shard_map/ppermute | solution.py:281
  18.6 0.2 %collective-permute-start.4 = (bf16[2,4,1536]{2,1,0:T(4,128)(2,1)S(1)}, bf16[2,4,1536]{2,1,0:T(4,128)(2,1)S(1)}, u32[]{:S(2)}, u32[]{:S(2)}) collective-permute-start(bf16[2,4,1536]{2,1,0:T(4,128)(2,1)S(1)} %collective-permute-done.3.refs_2_), channel_id=1, source_target_pairs={{0,16},{16,0},{1,17},{17,1},{2,18},{18,2},{3,19},{19,3},{4,20},{20... | collective-permute-start | bytes 73736 | tf_op jit(solution)/shard_map/ppermute | solution.py:42
  18.9 1.7 %collective-permute-done.2.refs_1_ = bf16[2,4,1536]{2,1,0:T(4,128)(2,1)S(1)} collective-permute-done((bf16[2,4,1536]{2,1,0:T(4,128)(2,1)S(1)}, bf16[2,4,1536]{2,1,0:T(4,128)(2,1)S(1)}, u32[]{:S(2)}, u32[]{:S(2)}) %collective-permute-start.2) | collective-permute-done | bytes 24608 | tf_op jit(solution)/shard_map/ppermute | solution.py:278
  20.6 0.0 collective-permute-done.4.refs_3_
  20.6 0.0 copy-done
  20.6 0.8 %shard_map.75 = (f32[24,1536]{1,0:T(8,128)S(1)}, f32[24,128]{1,0:T(8,128)S(1)}) custom-call(bf16[24,1664]{1,0:T(8,128)(2,1)S(1)} %shard_map.73.own_ref, bf16[2,72,3072]{2,1,0:T(8,128)(2,1)S(1)} %bitcast.9, bf16[48,1536]{1,0:T(8,128)(2,1)S(1)} %bitcast.10, f32[1,128]{1,0:T(1,128)S(1)} %bitcast.15, bf16[2,4,1536]{2,1,0:T(4,128)(2,1)S(1)} %get-tuple-element.12.refs_0_, ...), custom_call_target="tpu_custom_call" | custom-call | bytes 1210880 | tf_op jit(solution)/shard_map/pallas_call | solution.py:52
  21.4 0.0 collective-permute-done.7.refs_0_
  21.4 0.0 collective-permute-done.8.refs_1_
  21.4 0.8 %shard_map.77 = bf16[24,1536]{1,0:T(8,128)(2,1)} custom-call(f32[24,1536]{1,0:T(8,128)S(1)} %get-tuple-element.13.total_ref, f32[24,128]{1,0:T(8,128)S(1)} %get-tuple-element.14.sum_ref, bf16[24,1664]{1,0:T(8,128)(2,1)S(1)} %collective-permute-done.7.refs_0_, bf16[24,1664]{1,0:T(8,128)(2,1)S(1)} %collective-permute-done.8.refs_1_), custom_call_target="tpu_custom_call" | custom-call | tf_op jit(solution)/shard_map/pallas_call | solution.py:266
Async XLA Ops:
  0.0 7.2 %copy-start.1 = (bf16[1,1,1,2,24,1536]{5,4,3,2,1,0:T(8,128)(2,1)S(1)}, bf16[1,1,1,2,24,1536]{5,4,3,2,1,0:T(8,128)(2,1)}, u32[]{:S(2)}) copy-start(bf16[1,1,1,2,24,1536]{5,4,3,2,1,0:T(8,128)(2,1)} %param.9) | copy-start | bytes 442372
  0.0 7.2 %collective-permute-start = (bf16[48,1536]{1,0:T(8,128)(2,1)}, bf16[48,1536]{1,0:T(8,128)(2,1)S(1)}, u32[]{:S(2)}, u32[]{:S(2)}) collective-permute-start(bf16[48,1536]{1,0:T(8,128)(2,1)} %bitcast.11), channel_id=1, source_target_pairs={{0,1},{1,0},{2,3},{3,2},{16,17},{17,16},{18,19},{19,18},{4,5},{5,4... | collective-permute-start | bytes 442376 | tf_op jit(solution)/shard_map/ppermute | solution.py:32
  3.0 4.1 %collective-permute-start.1 = (bf16[48,1536]{1,0:T(8,128)(2,1)}, bf16[48,1536]{1,0:T(8,128)(2,1)S(1)}, u32[]{:S(2)}, u32[]{:S(2)}) collective-permute-start(bf16[48,1536]{1,0:T(8,128)(2,1)} %bitcast.12), channel_id=1, source_target_pairs={{0,16},{1,2},{2,1},{3,19},{16,0},{17,18},{18,17},{19,3},{4,20},{5,... | collective-permute-start | bytes 442376 | tf_op jit(solution)/shard_map/ppermute | solution.py:32
  4.1 3.1 %copy-start.3 = (f32[128]{0:T(128)S(1)}, f32[128]{0:T(128)}, u32[]{:S(2)}) copy-start(f32[128]{0:T(128)} %param.12) | copy-start | bytes 1540
  4.1 6.5 %collective-permute-start.5 = (bf16[24,1664]{1,0:T(8,128)(2,1)S(1)}, bf16[24,1664]{1,0:T(8,128)(2,1)S(1)}, u32[]{:S(2)}, u32[]{:S(2)}) collective-permute-start(bf16[24,1664]{1,0:T(8,128)(2,1)S(1)} %shard_map.73.own_ref), channel_id=1, source_target_pairs={{0,4},{4,0},{8,12},{12,8},{16,20},{20,16},{24,28},{28,24},{1,5},{5... | collective-permute-start | bytes 239624 | tf_op jit(solution)/shard_map/ppermute | solution.py:32
  5.6 4.9 %collective-permute-start.6 = (bf16[24,1664]{1,0:T(8,128)(2,1)S(1)}, bf16[24,1664]{1,0:T(8,128)(2,1)S(1)}, u32[]{:S(2)}, u32[]{:S(2)}) collective-permute-start(bf16[24,1664]{1,0:T(8,128)(2,1)S(1)} %shard_map.73.own_ref), channel_id=1, source_target_pairs={{0,16},{4,8},{8,4},{12,28},{16,0},{20,24},{24,20},{28,12},{1,17},{... | collective-permute-start | bytes 239624 | tf_op jit(solution)/shard_map/ppermute | solution.py:32
  7.2 0.7 %copy-start.2 = (bf16[2,4,1536]{2,1,0:T(4,128)(2,1)S(1)}, bf16[2,4,1536]{2,1,0:T(4,128)(2,1)}, u32[]{:S(2)}) copy-start(bf16[2,4,1536]{2,1,0:T(4,128)(2,1)} %refs_3_.1) | copy-start | bytes 73732
  10.6 10.0 %copy-start = (bf16[1,1,1,2,24,1536]{5,4,3,2,1,0:T(8,128)(2,1)S(1)}, bf16[1,1,1,2,24,1536]{5,4,3,2,1,0:T(8,128)(2,1)}, u32[]{:S(2)}) copy-start(bf16[1,1,1,2,24,1536]{5,4,3,2,1,0:T(8,128)(2,1)} %param.8) | copy-start | bytes 442372
  11.2 10.2 %collective-permute-start.7 = (bf16[24,1664]{1,0:T(8,128)(2,1)S(1)}, bf16[24,1664]{1,0:T(8,128)(2,1)S(1)}, u32[]{:S(2)}, u32[]{:S(2)}) collective-permute-start(bf16[24,1664]{1,0:T(8,128)(2,1)S(1)} %get-tuple-element.15), channel_id=1, source_target_pairs={{0,4},{4,0},{8,12},{12,8},{16,20},{20,16},{24,28},{28,24},{1,5},{5... | collective-permute-start | bytes 239624 | tf_op jit(solution)/shard_map/ppermute | solution.py:32
  13.8 7.6 %collective-permute-start.8 = (bf16[24,1664]{1,0:T(8,128)(2,1)S(1)}, bf16[24,1664]{1,0:T(8,128)(2,1)S(1)}, u32[]{:S(2)}, u32[]{:S(2)}) collective-permute-start(bf16[24,1664]{1,0:T(8,128)(2,1)S(1)} %get-tuple-element.16), channel_id=1, source_target_pairs={{0,16},{4,8},{8,4},{12,28},{16,0},{20,24},{24,20},{28,12},{1,17},{... | collective-permute-start | bytes 239624 | tf_op jit(solution)/shard_map/ppermute | solution.py:32
  13.8 4.8 %collective-permute-start.3 = (bf16[2,4,1536]{2,1,0:T(4,128)(2,1)S(1)}, bf16[2,4,1536]{2,1,0:T(4,128)(2,1)S(1)}, u32[]{:S(2)}, u32[]{:S(2)}) collective-permute-start(bf16[2,4,1536]{2,1,0:T(4,128)(2,1)S(1)} %get-tuple-element.12.refs_0_), channel_id=1, source_target_pairs={{0,2},{1,3},{2,0},{3,1},{16,19},{17,18},{18,17},{19,16},{4,6},{5,7... | collective-permute-start | bytes 73736 | tf_op jit(solution)/shard_map/ppermute | solution.py:281
  16.7 3.8 %collective-permute-start.2 = (bf16[2,4,1536]{2,1,0:T(4,128)(2,1)S(1)}, bf16[2,4,1536]{2,1,0:T(4,128)(2,1)S(1)}, u32[]{:S(2)}, u32[]{:S(2)}) collective-permute-start(bf16[2,4,1536]{2,1,0:T(4,128)(2,1)S(1)} %get-tuple-element.12.refs_0_), channel_id=1, source_target_pairs={{0,1},{1,0},{2,3},{3,2},{4,5},{5,4},{6,7},{7,6},{8,9},{9,8},{10,11... | collective-permute-start | bytes 73736 | tf_op jit(solution)/shard_map/ppermute | solution.py:278
  18.6 1.9 %collective-permute-start.4 = (bf16[2,4,1536]{2,1,0:T(4,128)(2,1)S(1)}, bf16[2,4,1536]{2,1,0:T(4,128)(2,1)S(1)}, u32[]{:S(2)}, u32[]{:S(2)}) collective-permute-start(bf16[2,4,1536]{2,1,0:T(4,128)(2,1)S(1)} %collective-permute-done.3.refs_2_), channel_id=1, source_target_pairs={{0,16},{16,0},{1,17},{17,1},{2,18},{18,2},{3,19},{19,3},{4,20},{20... | collective-permute-start | bytes 73736 | tf_op jit(solution)/shard_map/ppermute | solution.py:42

commit v3 on v2

--- a/solution.py
+++ b/solution.py
@@ -46,7 +46,7 @@
     return pltpu.with_memory_space_constraint(values, pltpu.VMEM)
 
 
-def call(body, out_shape, *operands, flops=0, exps=0):
+def call(body, out_shape, *operands, flops=0):
     outs = [pltpu.VMEM(s.shape, s.dtype) for s in out_shape]
     moved = sum(x.size * x.dtype.itemsize for x in operands)
     return pl.pallas_call(
@@ -54,7 +54,7 @@
         out_shape=outs,
         in_specs=[IN_VMEM] * len(operands),
         out_specs=[IN_VMEM] * len(outs),
-        cost_estimate=pl.CostEstimate(flops=flops, bytes_accessed=moved, transcendentals=exps),
+        cost_estimate=pl.CostEstimate(flops=flops, bytes_accessed=moved, transcendentals=0),
     )(*[resident(x) for x in operands])
 
 
@@ -121,7 +121,7 @@
         slot = 0
         for t in range(sizes[0]):
             dt = t - place[0]
-            for dw in [0, *steps_w]:
+            for dw in [*steps_w[1:], 0, *steps_w[:1]]:
                 inside = (dt >= -1) & (dt <= 1)
                 for i, d in ((1, dh), (2, dw)):
                     inside = inside & (place[i] + d >= 0) & (place[i] + d < sizes[i])
@@ -132,67 +132,84 @@
     return flags
 
 
-def key_masks(flags, places, line, tile):
+def key_masks(flags, places, line, tile, rows):
+    lane = lax.broadcasted_iota(jnp.int32, (1, rows), 1)
     masks = []
     for t in range(places):
-        lane = lax.broadcasted_iota(jnp.int32, (1, line * tile), 1) // tile
-        mask = jnp.zeros(lane.shape, jnp.float32)
+        mask = jnp.zeros((1, rows), jnp.float32)
         for i in range(line):
             slot = t * line + i
-            mask = jnp.where(lane == i, flags[:, slot : slot + 1], mask)
+            mask = jnp.where(lane // tile == i, flags[:, slot : slot + 1], mask)
         masks.append(mask)
     return masks
 
 
-def prepare(queries, q_gain, pattern, axes, sizes):
+def prepare(queries, stale, text, q_gain, k_gain, pattern, axes, sizes):
     tile, width = queries.shape
+    tokens = text.shape[1]
     heads = width // q_gain.shape[-1]
-
-    def body(q_ref, gain_ref, pattern_ref, out_ref):
-        normed = head_normed(q_ref[...].astype(jnp.float32), gain_ref[...], heads)
+    folds = tile // tokens
+    chunk = 2 * width // folds
+
+    def body(q_ref, stale_ref, text_ref, q_gain_ref, k_gain_ref, pattern_ref, own_ref, pack_ref, text_out_ref):
+        k_gain = k_gain_ref[...]
+        normed = head_normed(q_ref[...].astype(jnp.float32), q_gain_ref[...], heads)
         flags = slot_flags(pattern_ref, axes, sizes, tile)
-        out_ref[...] = jnp.concatenate([normed, flags], axis=1).astype(jnp.bfloat16)
-
+        own_ref[...] = jnp.concatenate([normed, flags], axis=1).astype(jnp.bfloat16)
+        both = stale_ref[...].astype(jnp.float32)
+        text_keys = head_normed(text_ref[0].astype(jnp.float32), k_gain, heads)
+        words = jnp.concatenate([text_keys, text_ref[1].astype(jnp.float32)], axis=1)
+        folded = [words[:, i * chunk : (i + 1) * chunk] for i in range(folds)]
+        pack = [head_normed(both[:tile], k_gain, heads), both[tile:], jnp.concatenate(folded, axis=0)]
+        pack_ref[...] = jnp.concatenate(pack, axis=1).astype(jnp.bfloat16)
+        text_out_ref[...] = words.astype(jnp.bfloat16)
+
+    shapes = [(tile, width + LANES), (tile, 2 * width + chunk), (tokens, 2 * width)]
     return pl.pallas_call(
         body,
-        out_shape=pltpu.VMEM((tile, width + LANES), jnp.bfloat16),
-        in_specs=[IN_VMEM, IN_VMEM, IN_SMEM],
-        out_specs=IN_VMEM,
-    )(queries, q_gain, pattern)
-
-
-def norm_line(slots, text, k_gain, tile):
-    width = slots[0].shape[1]
+        out_shape=[pltpu.VMEM(shape, jnp.bfloat16) for shape in shapes],
+        in_specs=[IN_VMEM] * 5 + [IN_SMEM],
+        out_specs=[IN_VMEM] * 3,
+    )(queries, stale, text, q_gain, k_gain, pattern)
+
+
+def norm_raw(both, k_gain, tile):
+    width = both.shape[1]
     heads = width // k_gain.shape[-1]
 
+    def body(both_ref, gain_ref, out_ref):
+        both = both_ref[...].astype(jnp.float32)
+        keys = head_normed(both[:tile], gain_ref[...], heads)
+        out_ref[...] = jnp.concatenate([keys, both[tile:]], axis=1).astype(jnp.bfloat16)
+
+    shape = jax.ShapeDtypeStruct((tile, 2 * width), jnp.bfloat16)
+    return call(body, [shape], both, k_gain, flops=int(3e8))[0]
+
+
+def join_line(packs, width):
     def body(*refs):
-        slot_refs, (text_ref, gain_ref, line_ref, text_out_ref) = refs[:-4], refs[-4:]
-        gain = gain_ref[...]
-        keys, vals = normed_tiles([r[...] for r in slot_refs], gain, heads, tile)
-        text_keys = head_normed(text_ref[0].astype(jnp.float32), gain, heads)
-        line_ref[:, :width] = keys
-        line_ref[:, width:] = vals
-        text_out_ref[0] = text_keys.astype(jnp.bfloat16)
-        text_out_ref[1] = text_ref[1]
-
-    shapes = [
-        jax.ShapeDtypeStruct((len(slots) * tile, 2 * width), jnp.bfloat16),
-        jax.ShapeDtypeStruct(text.shape, text.dtype),
-    ]
-    return call(body, shapes, *slots, text, k_gain)
-
-
-def attend_partners(around, sent, tile, hd):
+        parts = [r[:, : 2 * width].astype(jnp.float32) for r in refs[:-1]]
+        refs[-1][...] = jnp.concatenate(parts, axis=0).astype(jnp.bfloat16)
+
+    shape = jax.ShapeDtypeStruct((sum(x.shape[0] for x in packs), 2 * width), jnp.bfloat16)
+    return call(body, [shape], *packs)[0]
+
+
+def attend_partners(around, sent, far, tile, line, hd):
     places, rows, width = around.shape
     width //= 2
-    line = rows // tile
     heads = width // hd
 
     def body(around_ref, *refs):
-        sent_refs, back_refs = refs[: len(sent)], refs[len(sent) :]
+        sent_refs, refs = refs[: len(sent)], refs[len(sent) :]
+        far_refs, refs = refs[: len(far)], refs[len(far) :]
+        back_refs, on_refs = refs[: len(sent)], refs[len(sent) :]
+        for r, on in zip(far_refs, on_refs, strict=True):
+            on[...] = r[...]
         blocks = [r[...].astype(jnp.float32) for r in sent_refs]
         masks = [
-            key_masks(block[i : i + 1, width:], places, line, tile) for i, block in enumerate(blocks)
+            key_masks(block[i : i + 1, width:], places, line, tile, rows)
+            for i, block in enumerate(blocks)
         ]
         groups = []
         for t in range(places):
@@ -210,29 +227,31 @@
             back[...] = whole[i * tile : (i + 1) * tile].astype(jnp.bfloat16)
 
     shapes = [jax.ShapeDtypeStruct((tile, width + LANES), jnp.bfloat16)] * len(sent)
-    return call(body, shapes, around, *sent)
-
-
-def attend_own(own, around, current, text, k_gain, tile, reader):
+    shapes += [jax.ShapeDtypeStruct(x.shape, x.dtype) for x in far]
+    outs = call(body, shapes, around, *sent, *far)
+    return outs[: len(sent)], outs[len(sent) :]
+
+
+def attend_own(own, around, current, words, near, k_gain, tile, line, reader):
     places, rows, width = around.shape
     width //= 2
-    line = rows // tile
     heads = width // k_gain.shape[-1]
 
     def body(own_ref, around_ref, current_ref, gain_ref, *refs):
-        text_refs, (total_ref, sum_ref) = refs[:-2], refs[-2:]
+        total_ref, sum_ref = refs[-2:]
         here = current_ref[...].astype(jnp.float32)
-        sure_keys = [head_normed(here[:tile], gain_ref[...], heads)]
-        sure_vals = [here[tile:]]
-        for r in text_refs:
-            sure_keys.append(r[0].astype(jnp.float32))
-            sure_vals.append(r[1].astype(jnp.float32))
-        sure_keys, sure_vals = (
-            jnp.concatenate(x, axis=0).astype(jnp.bfloat16) for x in (sure_keys, sure_vals)
-        )
+        keys = head_normed(here[:tile], gain_ref[...], heads)
+        sure = [jnp.concatenate([keys, here[tile:]], axis=1)]
+        sure += [r[...].astype(jnp.float32) for r in refs[: len(words)]]
+        tokens = words[0].shape[0]
+        for r in refs[len(words) : -2]:
+            folded = r[:, 2 * width :].astype(jnp.float32)
+            folds = [folded[i * tokens : (i + 1) * tokens] for i in range(tile // tokens)]
+            sure.append(jnp.concatenate(folds, axis=1))
+        sure = jnp.concatenate(sure, axis=0).astype(jnp.bfloat16)
         flags = own_ref[:, width:].astype(jnp.float32)[reader : reader + 1]
-        masks = key_masks(flags, places, line, tile)
-        groups = [(sure_keys, sure_vals, None)]
+        masks = key_masks(flags, places, line, tile, rows)
+        groups = [(sure[:, :width], sure[:, width:], None)]
         for t in range(places):
             groups.append((around_ref[t, :, :width], around_ref[t, :, width:], masks[t]))
         totals, weights = attention(own_ref[:, :width], groups, heads)
@@ -243,7 +262,7 @@
         jax.ShapeDtypeStruct((tile, width), jnp.float32),
         jax.ShapeDtypeStruct((tile, LANES), jnp.float32),
     ]
-    return call(body, shapes, own, around, current, k_gain, *text)
+    return call(body, shapes, own, around, current, k_gain, *words, *near)
 
 
 def combine(total, weight, backs, hd):
@@ -271,25 +290,6 @@
     )(*[resident(x) for x in operands])
 
 
-def gather_text(text):
-    count, cores = lax.axis_size("wa"), lax.axis_size("ta")
-    if count & (count - 1):
-        return [lax.all_gather(text, "wa", axis=1, tiled=True)]
-    near = lax.ppermute(text, "wa", [(i, i ^ 1) for i in range(count)]) if count > 1 else None
-    if count == 4 and cores % 2 == 0:
-        pairs = [(t * 4 + i, t * 4 + (i ^ (2 + t % 2))) for t in range(cores) for i in range(4)]
-        far = lax.ppermute(text, ("ta", "wa"), pairs)
-        return [text, near, far, swap_ta(far, 0)]
-    if count > 1:
-        text = jnp.concatenate([text, near], axis=1)
-    span = 2
-    while span < count:
-        other = lax.ppermute(text, "wa", [(i, i ^ span) for i in range(count)])
-        text = jnp.concatenate([text, other], axis=1)
-        span *= 2
-    return [text]
-
-
 def shards(queries, current_kv, stale_kv, text_kv, q_gain, k_gain, pattern):
     tile, width = queries.shape[3:]
     hd = q_gain.shape[0]
@@ -300,17 +300,34 @@
     sizes = [lax.axis_size(a) for a in axes]
     parities_h, parities_w = parities(sizes[1]), parities(sizes[2])
 
-    line = [stale] + [swap_along(stale, "wa", p) for p in parities_w]
-    own = prepare(
-        queries.reshape(tile, width), q_gain.reshape(1, hd), pattern.reshape(27), axes, sizes
+    raw = [norm_raw(swap_along(stale, "wa", p), k_gain, tile) for p in parities_w[1:]]
+    own, pack, words = prepare(
+        queries.reshape(tile, width),
+        stale,
+        text_kv,
+        q_gain.reshape(1, hd),
+        k_gain,
+        pattern.reshape(27),
+        axes,
+        sizes,
     )
+    packs = [pack] + [swap_along(pack, "wa", p) for p in parities_w[:1]]
     sent = [swap_along(own, "ha", p) for p in parities_h]
-    line_kv, text = norm_line(line, text_kv, k_gain, tile)
-    around = lax.all_gather(line_kv, "ta")
-    text = gather_text(text)
-    answers = attend_partners(around, sent, tile, hd)
+    near, far = [], []
+    if sizes[2] == 4 and sizes[0] % 2 == 0:
+        pairs = [(t * 4 + i, t * 4 + (i ^ (2 + t % 2))) for t in range(sizes[0]) for i in range(4)]
+        near, far = packs[1:], [lax.ppermute(words, ("ta", "wa"), pairs)]
+        words = [words]
+    else:
+        words = [lax.all_gather(words, "wa", axis=0, tiled=True)]
+    packs = raw + packs
+    line = len(packs)
+    around = lax.all_gather(join_line(packs, width), "ta")
+    answers, far = attend_partners(around, sent, far, tile, line, hd)
     backs = [swap_along(x, "ha", p) for x, p in zip(answers, parities_h, strict=True)]
-    total, weight = attend_own(own, around, current, text, k_gain, tile, len(parities_h))
+    for x in far:
+        words += [x, swap_ta(x, 0)]
+    total, weight = attend_own(own, around, current, words, near, k_gain, tile, line, len(parities_h))
     result = combine(total, weight, backs, hd)
     return result.reshape(1, 1, 1, tile, width)
 

time: 22.5 us -> 20.2 us (0.90)
  the two profiles are of different devices: /device:TPU:0 before, /device:TPU:10 now
where the time goes in v3:
time: 20.2 us; the launch traced here: 20 us
  starting transfers between devices  9.84 us (49%)
  waiting for transfers between devices  4.09 us (20%)
  Pallas kernels  3.6 us (18%)
  blocking collectives  2.44 us (12%)
    ppermute x6, starting transfers between devices, swap_along(): return lax.ppermute(values, ('ta', axis), pairs)  8.01 us
    ppermute x6, waiting for transfers between devices, swap_along(): return lax.ppermute(values, ('ta', axis), pairs)  2.89 us
    all_gather x1, blocking collectives, shards(): around = lax.all_gather(join_line(packs, width), 'ta')  2.44 us
    ppermute x1, starting transfers between devices, shards(): near, far = (packs[1:], [lax.ppermute(words, ('ta', 'wa'), pairs)])  1.82 us
    pallas_call x4, Pallas kernels, call(): pl.pallas_call(body, out_shape=outs, in_specs=[IN_VMEM] * len(operands),...  1.6 us
    ppermute x1, waiting for transfers between devices, swap_ta(): return lax.ppermute(values, 'ta', pairs)  1.19 us
    pallas_call x1, Pallas kernels, prepare(): pl.pallas_call(body, out_shape=[pltpu.VMEM(shape, jnp.bfloat16) for shape...  1.16 us
    pallas_call x1, Pallas kernels, combine(): pl.pallas_call(body, out_shape=jax.ShapeDtypeStruct((tile, width), jnp.bf...  0.84 us
  transfers between devices with their start and end apart: 8, of which 3 were waited for; matrix products, arithmetic and copies ran while one was open for 0% of the time, Pallas kernels for 11%

profile of v3, /device:TPU:10, one launch (start us, length us, event | category | flops | bytes accessed | tf_op | source)
XLA Modules:
  0.0 20.0 jit_solution(481731883137032681)
XLA Ops:
  0.0 1.6 %collective-permute-start = (bf16[48,1536]{1,0:T(8,128)(2,1)}, bf16[48,1536]{1,0:T(8,128)(2,1)S(1)}, u32[]{:S(2)}, u32[]{:S(2)}) collective-permute-start(bf16[48,1536]{1,0:T(8,128)(2,1)} %bitcast.14), channel_id=1, source_target_pairs={{0,16},{1,2},{2,1},{3,19},{16,0},{17,18},{18,17},{19,3},{4,20},{5,... | collective-permute-start | bytes 442376 | tf_op jit(solution)/shard_map/ppermute | solution.py:32
  1.6 1.2 %shard_map.73 = (bf16[24,1664]{1,0:T(8,128)(2,1)S(1)}, bf16[24,3584]{1,0:T(8,128)(2,1)S(1)}, bf16[4,3072]{1,0:T(4,128)(2,1)S(1)}) custom-call(bf16[24,1536]{1,0:T(8,128)(2,1)} %bitcast.16, bf16[48,1536]{1,0:T(8,128)(2,1)} %bitcast.15, bf16[2,4,1536]{2,1,0:T(4,128)(2,1)} %text_ref.1, f32[1,128]{1,0:T(1,128)} %bitcast.17, f32[1,128]{1,0:T(1,128)} %bitcast.11, ...), custom_call_target="tpu_custom_call" | custom-call | tf_op jit(solution)/shard_map/pallas_call | solution.py:168
  2.7 0.1 collective-permute-start.1
  2.8 0.0 copy-start.1
  2.8 0.6 %collective-permute-start.2 = (bf16[24,1664]{1,0:T(8,128)(2,1)S(1)}, bf16[24,1664]{1,0:T(8,128)(2,1)S(1)}, u32[]{:S(2)}, u32[]{:S(2)}) collective-permute-start(bf16[24,1664]{1,0:T(8,128)(2,1)S(1)} %get-tuple-element.13.own_ref), channel_id=1, source_target_pairs={{0,4},{4,0},{8,12},{12,8},{16,20},{20,16},{24,28},{28,24},{1,5},{5... | collective-permute-start | bytes 239624 | tf_op jit(solution)/shard_map/ppermute | solution.py:32
  3.4 2.4 %collective-permute-start.3 = (bf16[24,1664]{1,0:T(8,128)(2,1)S(1)}, bf16[24,1664]{1,0:T(8,128)(2,1)S(1)}, u32[]{:S(2)}, u32[]{:S(2)}) collective-permute-start(bf16[24,1664]{1,0:T(8,128)(2,1)S(1)} %get-tuple-element.13.own_ref), channel_id=1, source_target_pairs={{0,16},{4,8},{8,4},{12,28},{16,0},{20,24},{24,20},{28,12},{1,17},{... | collective-permute-start | bytes 239624 | tf_op jit(solution)/shard_map/ppermute | solution.py:32
  5.9 1.8 %collective-permute-start.4 = (bf16[4,3072]{1,0:T(4,128)(2,1)S(1)}, bf16[4,3072]{1,0:T(4,128)(2,1)S(1)}, u32[]{:S(2)}, u32[]{:S(2)}) collective-permute-start(bf16[4,3072]{1,0:T(4,128)(2,1)S(1)} %get-tuple-element.15.refs_0_), channel_id=1, source_target_pairs={{0,2},{1,3},{2,0},{3,1},{16,19},{17,18},{18,17},{19,16},{4,6},{5,7... | collective-permute-start | bytes 73736 | tf_op jit(solution)/shard_map/ppermute | solution.py:319
  7.7 0.0 collective-permute-done.both_ref
  7.7 0.0 copy-done.1
  7.7 0.1 shard_map.74.refs_0_
  7.8 0.8 %collective-permute-done.1.refs_2_.refs_3_ = bf16[24,3584]{1,0:T(8,128)(2,1)S(1)} collective-permute-done((bf16[24,3584]{1,0:T(8,128)(2,1)S(1)}, bf16[24,3584]{1,0:T(8,128)(2,1)S(1)}, u32[]{:S(2)}, u32[]{:S(2)}) %collective-permute-start.1) | collective-permute-done | bytes 172064 | tf_op jit(solution)/shard_map/ppermute | solution.py:32
  8.7 2.4 %all-gather = bf16[144,3072]{1,0:T(8,128)(2,1)S(1)} all-gather(bf16[72,3072]{1,0:T(8,128)(2,1)S(1)} %shard_map.75), channel_id=2, replica_groups=mesh['ta'=2,'ha'=4,'wa'=4] {'ta'}, dimensions={0}, use_global_device_ids=true | all-gather | bytes 1327104 | tf_op jit(solution)/shard_map/all_gather | solution.py:325
  11.1 0.0 collective-permute-done.4.refs_2_
  11.1 0.0 collective-permute-done.2.refs_0_
  11.1 0.0 collective-permute-done.3.refs_1_
  11.1 0.0 copy-start
  11.1 0.6 %shard_map.76 = (bf16[24,1664]{1,0:T(8,128)(2,1)S(1)}, bf16[24,1664]{1,0:T(8,128)(2,1)S(1)}, bf16[4,3072]{1,0:T(4,128)(2,1)S(1)}) custom-call(bf16[2,72,3072]{2,1,0:T(8,128)(2,1)S(1)} %bitcast.8, bf16[24,1664]{1,0:T(8,128)(2,1)S(1)} %collective-permute-done.2.refs_0_, bf16[24,1664]{1,0:T(8,128)(2,1)S(1)} %collective-permute-done.3.refs_1_, ...), custom_call_target="tpu_custom_call" | custom-call | bytes 1069056 | tf_op jit(solution)/shard_map/pallas_call | solution.py:52
  11.8 0.6 %collective-permute-start.6 = (bf16[24,1664]{1,0:T(8,128)(2,1)S(1)}, bf16[24,1664]{1,0:T(8,128)(2,1)S(1)}, u32[]{:S(2)}, u32[]{:S(2)}) collective-permute-start(bf16[24,1664]{1,0:T(8,128)(2,1)S(1)} %get-tuple-element.19), channel_id=1, source_target_pairs={{0,4},{4,0},{8,12},{12,8},{16,20},{20,16},{24,28},{28,24},{1,5},{5... | collective-permute-start | bytes 239624 | tf_op jit(solution)/shard_map/ppermute | solution.py:32
  12.4 2.7 %collective-permute-start.7 = (bf16[24,1664]{1,0:T(8,128)(2,1)S(1)}, bf16[24,1664]{1,0:T(8,128)(2,1)S(1)}, u32[]{:S(2)}, u32[]{:S(2)}) collective-permute-start(bf16[24,1664]{1,0:T(8,128)(2,1)S(1)} %get-tuple-element.20), channel_id=1, source_target_pairs={{0,16},{4,8},{8,4},{12,28},{16,0},{20,24},{24,20},{28,12},{1,17},{... | collective-permute-start | bytes 239624 | tf_op jit(solution)/shard_map/ppermute | solution.py:32
  15.1 0.0 collective-permute-start.5
  15.1 1.2 %collective-permute-done.5.refs_2_ = bf16[4,3072]{1,0:T(4,128)(2,1)S(1)} collective-permute-done((bf16[4,3072]{1,0:T(4,128)(2,1)S(1)}, bf16[4,3072]{1,0:T(4,128)(2,1)S(1)}, u32[]{:S(2)}, u32[]{:S(2)}) %collective-permute-start.5) | collective-permute-done | bytes 24608 | tf_op jit(solution)/shard_map/ppermute | solution.py:42
  16.3 0.0 copy-done
  16.3 0.8 %shard_map.77 = (f32[24,1536]{1,0:T(8,128)S(1)}, f32[24,128]{1,0:T(8,128)S(1)}) custom-call(bf16[24,1664]{1,0:T(8,128)(2,1)S(1)} %get-tuple-element.13.own_ref, bf16[2,72,3072]{2,1,0:T(8,128)(2,1)S(1)} %bitcast.9, bf16[48,1536]{1,0:T(8,128)(2,1)S(1)} %bitcast.10, f32[1,128]{1,0:T(1,128)S(1)} %bitcast.13, bf16[4,3072]{1,0:T(4,128)(2,1)S(1)} %get-tuple-element.15.refs_0_, ...), custom_call_target="tpu_custom_call" | custom-call | bytes 1358336 | tf_op jit(solution)/shard_map/pallas_call | solution.py:52
  17.1 0.0 collective-permute-done.6.refs_0_
  17.1 2.1 %collective-permute-done.7.refs_1_ = bf16[24,1664]{1,0:T(8,128)(2,1)S(1)} collective-permute-done((bf16[24,1664]{1,0:T(8,128)(2,1)S(1)}, bf16[24,1664]{1,0:T(8,128)(2,1)S(1)}, u32[]{:S(2)}, u32[]{:S(2)}) %collective-permute-start.7) | collective-permute-done | bytes 79904 | tf_op jit(solution)/shard_map/ppermute | solution.py:32
  19.2 0.8 %shard_map.78 = bf16[24,1536]{1,0:T(8,128)(2,1)} custom-call(f32[24,1536]{1,0:T(8,128)S(1)} %get-tuple-element.17.total_ref, f32[24,128]{1,0:T(8,128)S(1)} %get-tuple-element.18.sum_ref, bf16[24,1664]{1,0:T(8,128)(2,1)S(1)} %collective-permute-done.6.refs_0_, bf16[24,1664]{1,0:T(8,128)(2,1)S(1)} %collective-permute-done.7.refs_1_), custom_call_target="tpu_custom_call" | custom-call | tf_op jit(solution)/shard_map/pallas_call | solution.py:285
  (1 shorter events, 0.0 us)
Async XLA Ops:
  0.0 7.7 %collective-permute-start = (bf16[48,1536]{1,0:T(8,128)(2,1)}, bf16[48,1536]{1,0:T(8,128)(2,1)S(1)}, u32[]{:S(2)}, u32[]{:S(2)}) collective-permute-start(bf16[48,1536]{1,0:T(8,128)(2,1)} %bitcast.14), channel_id=1, source_target_pairs={{0,16},{1,2},{2,1},{3,19},{16,0},{17,18},{18,17},{19,3},{4,20},{5,... | collective-permute-start | bytes 442376 | tf_op jit(solution)/shard_map/ppermute | solution.py:32
  2.7 5.9 %collective-permute-start.1 = (bf16[24,3584]{1,0:T(8,128)(2,1)S(1)}, bf16[24,3584]{1,0:T(8,128)(2,1)S(1)}, u32[]{:S(2)}, u32[]{:S(2)}) collective-permute-start(bf16[24,3584]{1,0:T(8,128)(2,1)S(1)} %get-tuple-element.14.refs_1_), channel_id=1, source_target_pairs={{0,1},{1,0},{2,3},{3,2},{16,17},{17,16},{18,19},{19,18},{4,5},{5,4... | collective-permute-start | bytes 516104 | tf_op jit(solution)/shard_map/ppermute | solution.py:32
  2.8 4.9 %copy-start.1 = (f32[128]{0:T(128)S(1)}, f32[128]{0:T(128)}, u32[]{:S(2)}) copy-start(f32[128]{0:T(128)} %param.12) | copy-start | bytes 1540
  2.8 8.3 %collective-permute-start.2 = (bf16[24,1664]{1,0:T(8,128)(2,1)S(1)}, bf16[24,1664]{1,0:T(8,128)(2,1)S(1)}, u32[]{:S(2)}, u32[]{:S(2)}) collective-permute-start(bf16[24,1664]{1,0:T(8,128)(2,1)S(1)} %get-tuple-element.13.own_ref), channel_id=1, source_target_pairs={{0,4},{4,0},{8,12},{12,8},{16,20},{20,16},{24,28},{28,24},{1,5},{5... | collective-permute-start | bytes 239624 | tf_op jit(solution)/shard_map/ppermute | solution.py:32
  3.4 7.7 %collective-permute-start.3 = (bf16[24,1664]{1,0:T(8,128)(2,1)S(1)}, bf16[24,1664]{1,0:T(8,128)(2,1)S(1)}, u32[]{:S(2)}, u32[]{:S(2)}) collective-permute-start(bf16[24,1664]{1,0:T(8,128)(2,1)S(1)} %get-tuple-element.13.own_ref), channel_id=1, source_target_pairs={{0,16},{4,8},{8,4},{12,28},{16,0},{20,24},{24,20},{28,12},{1,17},{... | collective-permute-start | bytes 239624 | tf_op jit(solution)/shard_map/ppermute | solution.py:32
  5.9 5.2 %collective-permute-start.4 = (bf16[4,3072]{1,0:T(4,128)(2,1)S(1)}, bf16[4,3072]{1,0:T(4,128)(2,1)S(1)}, u32[]{:S(2)}, u32[]{:S(2)}) collective-permute-start(bf16[4,3072]{1,0:T(4,128)(2,1)S(1)} %get-tuple-element.15.refs_0_), channel_id=1, source_target_pairs={{0,2},{1,3},{2,0},{3,1},{16,19},{17,18},{18,17},{19,16},{4,6},{5,7... | collective-permute-start | bytes 73736 | tf_op jit(solution)/shard_map/ppermute | solution.py:319
  11.1 5.1 %copy-start = (bf16[1,1,1,2,24,1536]{5,4,3,2,1,0:T(8,128)(2,1)S(1)}, bf16[1,1,1,2,24,1536]{5,4,3,2,1,0:T(8,128)(2,1)}, u32[]{:S(2)}) copy-start(bf16[1,1,1,2,24,1536]{5,4,3,2,1,0:T(8,128)(2,1)} %param.8) | copy-start | bytes 442372
  11.8 5.4 %collective-permute-start.6 = (bf16[24,1664]{1,0:T(8,128)(2,1)S(1)}, bf16[24,1664]{1,0:T(8,128)(2,1)S(1)}, u32[]{:S(2)}, u32[]{:S(2)}) collective-permute-start(bf16[24,1664]{1,0:T(8,128)(2,1)S(1)} %get-tuple-element.19), channel_id=1, source_target_pairs={{0,4},{4,0},{8,12},{12,8},{16,20},{20,16},{24,28},{28,24},{1,5},{5... | collective-permute-start | bytes 239624 | tf_op jit(solution)/shard_map/ppermute | solution.py:32
  12.4 6.8 %collective-permute-start.7 = (bf16[24,1664]{1,0:T(8,128)(2,1)S(1)}, bf16[24,1664]{1,0:T(8,128)(2,1)S(1)}, u32[]{:S(2)}, u32[]{:S(2)}) collective-permute-start(bf16[24,1664]{1,0:T(8,128)(2,1)S(1)} %get-tuple-element.20), channel_id=1, source_target_pairs={{0,16},{4,8},{8,4},{12,28},{16,0},{20,24},{24,20},{28,12},{1,17},{... | collective-permute-start | bytes 239624 | tf_op jit(solution)/shard_map/ppermute | solution.py:32
  15.1 1.2 %collective-permute-start.5 = (bf16[4,3072]{1,0:T(4,128)(2,1)S(1)}, bf16[4,3072]{1,0:T(4,128)(2,1)S(1)}, u32[]{:S(2)}, u32[]{:S(2)}) collective-permute-start(bf16[4,3072]{1,0:T(4,128)(2,1)S(1)} %get-tuple-element.16.refs_1_), channel_id=1, source_target_pairs={{0,16},{16,0},{1,17},{17,1},{2,18},{18,2},{3,19},{19,3},{4,20},{20... | collective-permute-start | bytes 73736 | tf_op jit(solution)/shard_map/ppermute | solution.py:42

commit v4 on v3

--- a/solution.py
+++ b/solution.py
@@ -121,7 +121,7 @@
         slot = 0
         for t in range(sizes[0]):
             dt = t - place[0]
-            for dw in [*steps_w[1:], 0, *steps_w[:1]]:
+            for dw in [0, *steps_w]:
                 inside = (dt >= -1) & (dt <= 1)
                 for i, d in ((1, dh), (2, dw)):
                     inside = inside & (place[i] + d >= 0) & (place[i] + d < sizes[i])
@@ -148,23 +148,20 @@
     tile, width = queries.shape
     tokens = text.shape[1]
     heads = width // q_gain.shape[-1]
-    folds = tile // tokens
-    chunk = 2 * width // folds
-
-    def body(q_ref, stale_ref, text_ref, q_gain_ref, k_gain_ref, pattern_ref, own_ref, pack_ref, text_out_ref):
+
+    def body(q_ref, stale_ref, text_ref, q_gain_ref, k_gain_ref, pattern_ref, own_ref, tile_ref, words_ref):
         k_gain = k_gain_ref[...]
         normed = head_normed(q_ref[...].astype(jnp.float32), q_gain_ref[...], heads)
         flags = slot_flags(pattern_ref, axes, sizes, tile)
         own_ref[...] = jnp.concatenate([normed, flags], axis=1).astype(jnp.bfloat16)
         both = stale_ref[...].astype(jnp.float32)
+        both = [head_normed(both[:tile], k_gain, heads), both[tile:]]
+        tile_ref[...] = jnp.concatenate(both, axis=1).astype(jnp.bfloat16)
         text_keys = head_normed(text_ref[0].astype(jnp.float32), k_gain, heads)
-        words = jnp.concatenate([text_keys, text_ref[1].astype(jnp.float32)], axis=1)
-        folded = [words[:, i * chunk : (i + 1) * chunk] for i in range(folds)]
-        pack = [head_normed(both[:tile], k_gain, heads), both[tile:], jnp.concatenate(folded, axis=0)]
-        pack_ref[...] = jnp.concatenate(pack, axis=1).astype(jnp.bfloat16)
-        text_out_ref[...] = words.astype(jnp.bfloat16)
-
-    shapes = [(tile, width + LANES), (tile, 2 * width + chunk), (tokens, 2 * width)]
+        both = [text_keys, text_ref[1].astype(jnp.float32)]
+        words_ref[...] = jnp.concatenate(both, axis=1).astype(jnp.bfloat16)
+
+    shapes = [(tile, width + LANES), (tile, 2 * width), (tokens, 2 * width)]
     return pl.pallas_call(
         body,
         out_shape=[pltpu.VMEM(shape, jnp.bfloat16) for shape in shapes],
@@ -173,7 +170,7 @@
     )(queries, stale, text, q_gain, k_gain, pattern)
 
 
-def norm_raw(both, k_gain, tile):
+def norm_raw(both, k_gain, tile, flops):
     width = both.shape[1]
     heads = width // k_gain.shape[-1]
 
@@ -183,7 +180,7 @@
         out_ref[...] = jnp.concatenate([keys, both[tile:]], axis=1).astype(jnp.bfloat16)
 
     shape = jax.ShapeDtypeStruct((tile, 2 * width), jnp.bfloat16)
-    return call(body, [shape], both, k_gain, flops=int(3e8))[0]
+    return call(body, [shape], both, k_gain, flops=flops)[0]
 
 
 def join_line(packs, width):
@@ -232,7 +229,7 @@
     return outs[: len(sent)], outs[len(sent) :]
 
 
-def attend_own(own, around, current, words, near, k_gain, tile, line, reader):
+def attend_own(own, around, current, words, k_gain, tile, line, reader):
     places, rows, width = around.shape
     width //= 2
     heads = width // k_gain.shape[-1]
@@ -242,12 +239,7 @@
         here = current_ref[...].astype(jnp.float32)
         keys = head_normed(here[:tile], gain_ref[...], heads)
         sure = [jnp.concatenate([keys, here[tile:]], axis=1)]
-        sure += [r[...].astype(jnp.float32) for r in refs[: len(words)]]
-        tokens = words[0].shape[0]
-        for r in refs[len(words) : -2]:
-            folded = r[:, 2 * width :].astype(jnp.float32)
-            folds = [folded[i * tokens : (i + 1) * tokens] for i in range(tile // tokens)]
-            sure.append(jnp.concatenate(folds, axis=1))
+        sure += [r[...].astype(jnp.float32) for r in refs[:-2]]
         sure = jnp.concatenate(sure, axis=0).astype(jnp.bfloat16)
         flags = own_ref[:, width:].astype(jnp.float32)[reader : reader + 1]
         masks = key_masks(flags, places, line, tile, rows)
@@ -262,7 +254,7 @@
         jax.ShapeDtypeStruct((tile, width), jnp.float32),
         jax.ShapeDtypeStruct((tile, LANES), jnp.float32),
     ]
-    return call(body, shapes, own, around, current, k_gain, *words, *near)
+    return call(body, shapes, own, around, current, k_gain, *words)
 
 
 def combine(total, weight, backs, hd):
@@ -300,8 +292,8 @@
     sizes = [lax.axis_size(a) for a in axes]
     parities_h, parities_w = parities(sizes[1]), parities(sizes[2])
 
-    raw = [norm_raw(swap_along(stale, "wa", p), k_gain, tile) for p in parities_w[1:]]
-    own, pack, words = prepare(
+    raw = [norm_raw(swap_along(stale, "wa", p), k_gain, tile, (int(1e9), int(3e8))[p]) for p in parities_w]
+    own, mine, words = prepare(
         queries.reshape(tile, width),
         stale,
         text_kv,
@@ -311,23 +303,23 @@
         axes,
         sizes,
     )
-    packs = [pack] + [swap_along(pack, "wa", p) for p in parities_w[:1]]
     sent = [swap_along(own, "ha", p) for p in parities_h]
-    near, far = [], []
+    others = []
     if sizes[2] == 4 and sizes[0] % 2 == 0:
         pairs = [(t * 4 + i, t * 4 + (i ^ (2 + t % 2))) for t in range(sizes[0]) for i in range(4)]
-        near, far = packs[1:], [lax.ppermute(words, ("ta", "wa"), pairs)]
+        others.append(lax.ppermute(words, ("ta", "wa"), pairs))
+        others.append(lax.ppermute(words, "wa", [(i, i ^ 1) for i in range(4)]))
         words = [words]
     else:
         words = [lax.all_gather(words, "wa", axis=0, tiled=True)]
-    packs = raw + packs
+    packs = [mine] + raw
     line = len(packs)
     around = lax.all_gather(join_line(packs, width), "ta")
-    answers, far = attend_partners(around, sent, far, tile, line, hd)
+    answers, others = attend_partners(around, sent, others, tile, line, hd)
     backs = [swap_along(x, "ha", p) for x, p in zip(answers, parities_h, strict=True)]
-    for x in far:
-        words += [x, swap_ta(x, 0)]
-    total, weight = attend_own(own, around, current, words, near, k_gain, tile, line, len(parities_h))
+    if others:
+        words += [*others, swap_ta(others[0], 0)]
+    total, weight = attend_own(own, around, current, words, k_gain, tile, line, len(parities_h))
     result = combine(total, weight, backs, hd)
     return result.reshape(1, 1, 1, tile, width)
 

time: 20.2 us -> 19.9 us (0.985)
  the two profiles are of different devices: /device:TPU:10 before, /device:TPU:0 now
where the time goes in v4:
time: 19.9 us; the launch traced here: 19.8 us
  starting transfers between devices  11.4 us (57%)
  Pallas kernels  3.72 us (19%)
  blocking collectives  2.44 us (12%)
  waiting for transfers between devices  2.1 us (11%)
    ppermute x6, starting transfers between devices, swap_along(): return lax.ppermute(values, ('ta', axis), pairs)  7.86 us
    all_gather x1, blocking collectives, shards(): around = lax.all_gather(join_line(packs, width), 'ta')  2.44 us
    ppermute x1, starting transfers between devices, shards(): others.append(lax.ppermute(words, ('ta', 'wa'), pairs))  2.36 us
    pallas_call x5, Pallas kernels, call(): pl.pallas_call(body, out_shape=outs, in_specs=[IN_VMEM] * len(operands),...  1.72 us
    pallas_call x1, Pallas kernels, prepare(): pl.pallas_call(body, out_shape=[pltpu.VMEM(shape, jnp.bfloat16) for shape...  1.16 us
    ppermute x6, waiting for transfers between devices, swap_along(): return lax.ppermute(values, ('ta', axis), pairs)  0.89 us
    ppermute x1, waiting for transfers between devices, swap_ta(): return lax.ppermute(values, 'ta', pairs)  0.85 us
    pallas_call x1, Pallas kernels, combine(): pl.pallas_call(body, out_shape=jax.ShapeDtypeStruct((tile, width), jnp.bf...  0.84 us
  transfers between devices with their start and end apart: 9, of which 3 were waited for; matrix products, arithmetic and copies ran while one was open for 0% of the time, Pallas kernels for 11%

profile of v4, /device:TPU:0, one launch (start us, length us, event | category | flops | bytes accessed | tf_op | source)
XLA Modules:
  0.0 19.8 jit_solution(14745167870290898935)
XLA Ops:
  0.0 3.0 %collective-permute-start = (bf16[48,1536]{1,0:T(8,128)(2,1)}, bf16[48,1536]{1,0:T(8,128)(2,1)S(1)}, u32[]{:S(2)}, u32[]{:S(2)}) collective-permute-start(bf16[48,1536]{1,0:T(8,128)(2,1)} %bitcast.15), channel_id=1, source_target_pairs={{0,1},{1,0},{2,3},{3,2},{16,17},{17,16},{18,19},{19,18},{4,5},{5,4... | collective-permute-start | bytes 442376 | tf_op jit(solution)/shard_map/ppermute | solution.py:32
  3.0 0.0 collective-permute-start.1
  3.0 1.2 %shard_map.73 = (bf16[24,1664]{1,0:T(8,128)(2,1)S(1)}, bf16[24,3072]{1,0:T(8,128)(2,1)S(1)}, bf16[4,3072]{1,0:T(4,128)(2,1)S(1)}) custom-call(bf16[24,1536]{1,0:T(8,128)(2,1)} %bitcast.18, bf16[48,1536]{1,0:T(8,128)(2,1)} %bitcast.17, bf16[2,4,1536]{2,1,0:T(4,128)(2,1)} %text_ref.1, f32[1,128]{1,0:T(1,128)} %bitcast.19, f32[1,128]{1,0:T(1,128)} %bitcast.11, ...), custom_call_target="tpu_custom_call" | custom-call | tf_op jit(solution)/shard_map/pallas_call | solution.py:165
  4.2 0.0 copy-start.1
  4.2 1.6 %collective-permute-start.2 = (bf16[24,1664]{1,0:T(8,128)(2,1)S(1)}, bf16[24,1664]{1,0:T(8,128)(2,1)S(1)}, u32[]{:S(2)}, u32[]{:S(2)}) collective-permute-start(bf16[24,1664]{1,0:T(8,128)(2,1)S(1)} %get-tuple-element.14.own_ref), channel_id=1, source_target_pairs={{0,4},{4,0},{8,12},{12,8},{16,20},{20,16},{24,28},{28,24},{1,5},{5... | collective-permute-start | bytes 239624 | tf_op jit(solution)/shard_map/ppermute | solution.py:32
  5.8 0.2 %collective-permute-start.3 = (bf16[24,1664]{1,0:T(8,128)(2,1)S(1)}, bf16[24,1664]{1,0:T(8,128)(2,1)S(1)}, u32[]{:S(2)}, u32[]{:S(2)}) collective-permute-start(bf16[24,1664]{1,0:T(8,128)(2,1)S(1)} %get-tuple-element.14.own_ref), channel_id=1, source_target_pairs={{0,16},{4,8},{8,4},{12,28},{16,0},{20,24},{24,20},{28,12},{1,17},{... | collective-permute-start | bytes 239624 | tf_op jit(solution)/shard_map/ppermute | solution.py:32
  6.0 2.4 %collective-permute-start.4 = (bf16[4,3072]{1,0:T(4,128)(2,1)S(1)}, bf16[4,3072]{1,0:T(4,128)(2,1)S(1)}, u32[]{:S(2)}, u32[]{:S(2)}) collective-permute-start(bf16[4,3072]{1,0:T(4,128)(2,1)S(1)} %get-tuple-element.16.refs_0_), channel_id=1, source_target_pairs={{0,2},{1,3},{2,0},{3,1},{16,19},{17,18},{18,17},{19,16},{4,6},{5,7... | collective-permute-start | bytes 73736 | tf_op jit(solution)/shard_map/ppermute | solution.py:310
  8.4 0.0 collective-permute-done.both_ref
  8.4 0.7 %collective-permute-start.5 = (bf16[4,3072]{1,0:T(4,128)(2,1)S(1)}, bf16[4,3072]{1,0:T(4,128)(2,1)S(1)}, u32[]{:S(2)}, u32[]{:S(2)}) collective-permute-start(bf16[4,3072]{1,0:T(4,128)(2,1)S(1)} %get-tuple-element.16.refs_0_), channel_id=1, source_target_pairs={{0,1},{1,0},{2,3},{3,2},{4,5},{5,4},{6,7},{7,6},{8,9},{9,8},{10,11... | collective-permute-start | bytes 73736 | tf_op jit(solution)/shard_map/ppermute | solution.py:311
  9.1 0.0 copy-done.1
  9.1 0.1 shard_map.74.refs_1_
  9.2 0.0 collective-permute-done.1.both_ref
  9.2 0.1 shard_map.75.refs_2_
  9.4 2.4 %all-gather = bf16[144,3072]{1,0:T(8,128)(2,1)S(1)} all-gather(bf16[72,3072]{1,0:T(8,128)(2,1)S(1)} %shard_map.76), channel_id=2, replica_groups=mesh['ta'=2,'ha'=4,'wa'=4] {'ta'}, dimensions={0}, use_global_device_ids=true | all-gather | bytes 1327104 | tf_op jit(solution)/shard_map/all_gather | solution.py:317
  11.8 0.0 collective-permute-done.4.refs_2_
  11.8 0.4 %collective-permute-done.5.refs_3_ = bf16[4,3072]{1,0:T(4,128)(2,1)S(1)} collective-permute-done((bf16[4,3072]{1,0:T(4,128)(2,1)S(1)}, bf16[4,3072]{1,0:T(4,128)(2,1)S(1)}, u32[]{:S(2)}, u32[]{:S(2)}) %collective-permute-start.5) | collective-permute-done | bytes 24608 | tf_op jit(solution)/shard_map/ppermute | solution.py:311
  12.2 0.0 collective-permute-done.2.refs_0_
  12.2 0.0 collective-permute-done.3.refs_1_
  12.2 0.0 copy-start
  12.2 0.6 %shard_map.77 = (bf16[24,1664]{1,0:T(8,128)(2,1)S(1)}, bf16[24,1664]{1,0:T(8,128)(2,1)S(1)}, bf16[4,3072]{1,0:T(4,128)(2,1)S(1)}, bf16[4,3072]{1,0:T(4,128)(2,1)S(1)}) custom-call(bf16[2,72,3072]{2,1,0:T(8,128)(2,1)S(1)} %bitcast.8, bf16[24,1664]{1,0:T(8,128)(2,1)S(1)} %collective-permute-done.2.refs_0_, ...), custom_call_target="tpu_custom_call" | custom-call | bytes 1093632 | tf_op jit(solution)/shard_map/pallas_call | solution.py:52
  12.8 3.0 %collective-permute-start.7 = (bf16[24,1664]{1,0:T(8,128)(2,1)S(1)}, bf16[24,1664]{1,0:T(8,128)(2,1)S(1)}, u32[]{:S(2)}, u32[]{:S(2)}) collective-permute-start(bf16[24,1664]{1,0:T(8,128)(2,1)S(1)} %get-tuple-element.21), channel_id=1, source_target_pairs={{0,4},{4,0},{8,12},{12,8},{16,20},{20,16},{24,28},{28,24},{1,5},{5... | collective-permute-start | bytes 239624 | tf_op jit(solution)/shard_map/ppermute | solution.py:32
  15.9 0.0 collective-permute-start.8
  15.9 0.5 %collective-permute-start.6 = (bf16[4,3072]{1,0:T(4,128)(2,1)S(1)}, bf16[4,3072]{1,0:T(4,128)(2,1)S(1)}, u32[]{:S(2)}, u32[]{:S(2)}) collective-permute-start(bf16[4,3072]{1,0:T(4,128)(2,1)S(1)} %get-tuple-element.17.refs_1_), channel_id=1, source_target_pairs={{0,16},{16,0},{1,17},{17,1},{2,18},{18,2},{3,19},{19,3},{4,20},{20... | collective-permute-start | bytes 73736 | tf_op jit(solution)/shard_map/ppermute | solution.py:42
  16.4 0.8 %collective-permute-done.6.refs_3_ = bf16[4,3072]{1,0:T(4,128)(2,1)S(1)} collective-permute-done((bf16[4,3072]{1,0:T(4,128)(2,1)S(1)}, bf16[4,3072]{1,0:T(4,128)(2,1)S(1)}, u32[]{:S(2)}, u32[]{:S(2)}) %collective-permute-start.6) | collective-permute-done | bytes 24608 | tf_op jit(solution)/shard_map/ppermute | solution.py:42
  17.2 0.0 copy-done
  17.2 0.8 %shard_map.78 = (f32[24,1536]{1,0:T(8,128)S(1)}, f32[24,128]{1,0:T(8,128)S(1)}) custom-call(bf16[24,1664]{1,0:T(8,128)(2,1)S(1)} %get-tuple-element.14.own_ref, bf16[2,72,3072]{2,1,0:T(8,128)(2,1)S(1)} %bitcast.9, bf16[48,1536]{1,0:T(8,128)(2,1)S(1)} %bitcast.10, f32[1,128]{1,0:T(1,128)S(1)} %bitcast.14, bf16[4,3072]{1,0:T(4,128)(2,1)S(1)} %get-tuple-element.16.refs_0_, ...), custom_call_target="tpu_custom_call" | custom-call | bytes 1210880 | tf_op jit(solution)/shard_map/pallas_call | solution.py:52
  18.1 0.9 %collective-permute-done.7.refs_0_ = bf16[24,1664]{1,0:T(8,128)(2,1)S(1)} collective-permute-done((bf16[24,1664]{1,0:T(8,128)(2,1)S(1)}, bf16[24,1664]{1,0:T(8,128)(2,1)S(1)}, u32[]{:S(2)}, u32[]{:S(2)}) %collective-permute-start.7) | collective-permute-done | bytes 79904 | tf_op jit(solution)/shard_map/ppermute | solution.py:32
  18.9 0.0 collective-permute-done.8.refs_1_
  18.9 0.8 %shard_map.79 = bf16[24,1536]{1,0:T(8,128)(2,1)} custom-call(f32[24,1536]{1,0:T(8,128)S(1)} %get-tuple-element.19.total_ref, f32[24,128]{1,0:T(8,128)S(1)} %get-tuple-element.20.sum_ref, bf16[24,1664]{1,0:T(8,128)(2,1)S(1)} %collective-permute-done.7.refs_0_, bf16[24,1664]{1,0:T(8,128)(2,1)S(1)} %collective-permute-done.8.refs_1_), custom_call_target="tpu_custom_call" | custom-call | tf_op jit(solution)/shard_map/pallas_call | solution.py:277
  (1 shorter events, 0.0 us)
Async XLA Ops:
  0.0 8.4 %collective-permute-start = (bf16[48,1536]{1,0:T(8,128)(2,1)}, bf16[48,1536]{1,0:T(8,128)(2,1)S(1)}, u32[]{:S(2)}, u32[]{:S(2)}) collective-permute-start(bf16[48,1536]{1,0:T(8,128)(2,1)} %bitcast.15), channel_id=1, source_target_pairs={{0,1},{1,0},{2,3},{3,2},{16,17},{17,16},{18,19},{19,18},{4,5},{5,4... | collective-permute-start | bytes 442376 | tf_op jit(solution)/shard_map/ppermute | solution.py:32
  3.0 6.2 %collective-permute-start.1 = (bf16[48,1536]{1,0:T(8,128)(2,1)}, bf16[48,1536]{1,0:T(8,128)(2,1)S(1)}, u32[]{:S(2)}, u32[]{:S(2)}) collective-permute-start(bf16[48,1536]{1,0:T(8,128)(2,1)} %bitcast.16), channel_id=1, source_target_pairs={{0,16},{1,2},{2,1},{3,19},{16,0},{17,18},{18,17},{19,3},{4,20},{5,... | collective-permute-start | bytes 442376 | tf_op jit(solution)/shard_map/ppermute | solution.py:32
  4.2 4.9 %copy-start.1 = (f32[128]{0:T(128)S(1)}, f32[128]{0:T(128)}, u32[]{:S(2)}) copy-start(f32[128]{0:T(128)} %param.12) | copy-start | bytes 1540
  4.2 8.0 %collective-permute-start.2 = (bf16[24,1664]{1,0:T(8,128)(2,1)S(1)}, bf16[24,1664]{1,0:T(8,128)(2,1)S(1)}, u32[]{:S(2)}, u32[]{:S(2)}) collective-permute-start(bf16[24,1664]{1,0:T(8,128)(2,1)S(1)} %get-tuple-element.14.own_ref), channel_id=1, source_target_pairs={{0,4},{4,0},{8,12},{12,8},{16,20},{20,16},{24,28},{28,24},{1,5},{5... | collective-permute-start | bytes 239624 | tf_op jit(solution)/shard_map/ppermute | solution.py:32
  5.8 6.4 %collective-permute-start.3 = (bf16[24,1664]{1,0:T(8,128)(2,1)S(1)}, bf16[24,1664]{1,0:T(8,128)(2,1)S(1)}, u32[]{:S(2)}, u32[]{:S(2)}) collective-permute-start(bf16[24,1664]{1,0:T(8,128)(2,1)S(1)} %get-tuple-element.14.own_ref), channel_id=1, source_target_pairs={{0,16},{4,8},{8,4},{12,28},{16,0},{20,24},{24,20},{28,12},{1,17},{... | collective-permute-start | bytes 239624 | tf_op jit(solution)/shard_map/ppermute | solution.py:32
  6.0 5.8 %collective-permute-start.4 = (bf16[4,3072]{1,0:T(4,128)(2,1)S(1)}, bf16[4,3072]{1,0:T(4,128)(2,1)S(1)}, u32[]{:S(2)}, u32[]{:S(2)}) collective-permute-start(bf16[4,3072]{1,0:T(4,128)(2,1)S(1)} %get-tuple-element.16.refs_0_), channel_id=1, source_target_pairs={{0,2},{1,3},{2,0},{3,1},{16,19},{17,18},{18,17},{19,16},{4,6},{5,7... | collective-permute-start | bytes 73736 | tf_op jit(solution)/shard_map/ppermute | solution.py:310
  8.4 3.8 %collective-permute-start.5 = (bf16[4,3072]{1,0:T(4,128)(2,1)S(1)}, bf16[4,3072]{1,0:T(4,128)(2,1)S(1)}, u32[]{:S(2)}, u32[]{:S(2)}) collective-permute-start(bf16[4,3072]{1,0:T(4,128)(2,1)S(1)} %get-tuple-element.16.refs_0_), channel_id=1, source_target_pairs={{0,1},{1,0},{2,3},{3,2},{4,5},{5,4},{6,7},{7,6},{8,9},{9,8},{10,11... | collective-permute-start | bytes 73736 | tf_op jit(solution)/shard_map/ppermute | solution.py:311
  12.2 5.0 %copy-start = (bf16[1,1,1,2,24,1536]{5,4,3,2,1,0:T(8,128)(2,1)S(1)}, bf16[1,1,1,2,24,1536]{5,4,3,2,1,0:T(8,128)(2,1)}, u32[]{:S(2)}) copy-start(bf16[1,1,1,2,24,1536]{5,4,3,2,1,0:T(8,128)(2,1)} %param.8) | copy-start | bytes 442372
  12.8 6.1 %collective-permute-start.7 = (bf16[24,1664]{1,0:T(8,128)(2,1)S(1)}, bf16[24,1664]{1,0:T(8,128)(2,1)S(1)}, u32[]{:S(2)}, u32[]{:S(2)}) collective-permute-start(bf16[24,1664]{1,0:T(8,128)(2,1)S(1)} %get-tuple-element.21), channel_id=1, source_target_pairs={{0,4},{4,0},{8,12},{12,8},{16,20},{20,16},{24,28},{28,24},{1,5},{5... | collective-permute-start | bytes 239624 | tf_op jit(solution)/shard_map/ppermute | solution.py:32
  15.9 3.1 %collective-permute-start.8 = (bf16[24,1664]{1,0:T(8,128)(2,1)S(1)}, bf16[24,1664]{1,0:T(8,128)(2,1)S(1)}, u32[]{:S(2)}, u32[]{:S(2)}) collective-permute-start(bf16[24,1664]{1,0:T(8,128)(2,1)S(1)} %get-tuple-element.22), channel_id=1, source_target_pairs={{0,16},{4,8},{8,4},{12,28},{16,0},{20,24},{24,20},{28,12},{1,17},{... | collective-permute-start | bytes 239624 | tf_op jit(solution)/shard_map/ppermute | solution.py:32
  15.9 1.4 %collective-permute-start.6 = (bf16[4,3072]{1,0:T(4,128)(2,1)S(1)}, bf16[4,3072]{1,0:T(4,128)(2,1)S(1)}, u32[]{:S(2)}, u32[]{:S(2)}) collective-permute-start(bf16[4,3072]{1,0:T(4,128)(2,1)S(1)} %get-tuple-element.17.refs_1_), channel_id=1, source_target_pairs={{0,16},{16,0},{1,17},{17,1},{2,18},{18,2},{3,19},{19,3},{4,20},{20... | collective-permute-start | bytes 73736 | tf_op jit(solution)/shard_map/ppermute | solution.py:42

commit v5 on v4

--- a/solution.py
+++ b/solution.py
@@ -306,7 +306,7 @@
     sent = [swap_along(own, "ha", p) for p in parities_h]
     others = []
     if sizes[2] == 4 and sizes[0] % 2 == 0:
-        pairs = [(t * 4 + i, t * 4 + (i ^ (2 + t % 2))) for t in range(sizes[0]) for i in range(4)]
+        pairs = [(t * 4 + i, t * 4 + (i ^ (3 - t % 2))) for t in range(sizes[0]) for i in range(4)]
         others.append(lax.ppermute(words, ("ta", "wa"), pairs))
         others.append(lax.ppermute(words, "wa", [(i, i ^ 1) for i in range(4)]))
         words = [words]

time: 19.9 us -> 19.9 us (level)
  starting transfers between devices: 11.4 us -> 11.1 us
  waiting for transfers between devices: 2.1 us -> 2.4 us
    ppermute x6, starting transfers between devices: 7.86 us -> 7.63 us  [swap_along(): return lax.ppermute(values, ('ta', axis), pairs)]
where the time goes in v5:
time: 19.9 us; the launch traced here: 19.8 us
  starting transfers between devices  11.1 us (56%)
  Pallas kernels  3.72 us (19%)
  blocking collectives  2.44 us (12%)
  waiting for transfers between devices  2.4 us (12%)
    ppermute x6, starting transfers between devices, swap_along(): return lax.ppermute(values, ('ta', axis), pairs)  7.63 us
    ppermute x1, starting transfers between devices, shards(): others.append(lax.ppermute(words, ('ta', 'wa'), pairs))  2.47 us
    all_gather x1, blocking collectives, shards(): around = lax.all_gather(join_line(packs, width), 'ta')  2.44 us
    pallas_call x5, Pallas kernels, call(): pl.pallas_call(body, out_shape=outs, in_specs=[IN_VMEM] * len(operands),...  1.73 us
    pallas_call x1, Pallas kernels, prepare(): pl.pallas_call(body, out_shape=[pltpu.VMEM(shape, jnp.bfloat16) for shape...  1.16 us
    ppermute x6, waiting for transfers between devices, swap_along(): return lax.ppermute(values, ('ta', axis), pairs)  1 us
    ppermute x1, waiting for transfers between devices, swap_ta(): return lax.ppermute(values, 'ta', pairs)  0.85 us
    pallas_call x1, Pallas kernels, combine(): pl.pallas_call(body, out_shape=jax.ShapeDtypeStruct((tile, width), jnp.bf...  0.84 us
  transfers between devices with their start and end apart: 9, of which 3 were waited for; matrix products, arithmetic and copies ran while one was open for 0% of the time, Pallas kernels for 11%

profile of v5, /device:TPU:0, one launch (start us, length us, event | category | flops | bytes accessed | tf_op | source)
XLA Modules:
  0.0 19.8 jit_solution(11142818935046948792)
XLA Ops:
  0.0 3.0 %collective-permute-start = (bf16[48,1536]{1,0:T(8,128)(2,1)}, bf16[48,1536]{1,0:T(8,128)(2,1)S(1)}, u32[]{:S(2)}, u32[]{:S(2)}) collective-permute-start(bf16[48,1536]{1,0:T(8,128)(2,1)} %bitcast.15), channel_id=1, source_target_pairs={{0,1},{1,0},{2,3},{3,2},{16,17},{17,16},{18,19},{19,18},{4,5},{5,4... | collective-permute-start | bytes 442376 | tf_op jit(solution)/shard_map/ppermute | solution.py:32
  3.0 0.0 collective-permute-start.1
  3.0 1.2 %shard_map.73 = (bf16[24,1664]{1,0:T(8,128)(2,1)S(1)}, bf16[24,3072]{1,0:T(8,128)(2,1)S(1)}, bf16[4,3072]{1,0:T(4,128)(2,1)S(1)}) custom-call(bf16[24,1536]{1,0:T(8,128)(2,1)} %bitcast.18, bf16[48,1536]{1,0:T(8,128)(2,1)} %bitcast.17, bf16[2,4,1536]{2,1,0:T(4,128)(2,1)} %text_ref.1, f32[1,128]{1,0:T(1,128)} %bitcast.19, f32[1,128]{1,0:T(1,128)} %bitcast.11, ...), custom_call_target="tpu_custom_call" | custom-call | tf_op jit(solution)/shard_map/pallas_call | solution.py:165
  4.2 0.0 copy-start.1
  4.2 1.6 %collective-permute-start.2 = (bf16[24,1664]{1,0:T(8,128)(2,1)S(1)}, bf16[24,1664]{1,0:T(8,128)(2,1)S(1)}, u32[]{:S(2)}, u32[]{:S(2)}) collective-permute-start(bf16[24,1664]{1,0:T(8,128)(2,1)S(1)} %get-tuple-element.14.own_ref), channel_id=1, source_target_pairs={{0,4},{4,0},{8,12},{12,8},{16,20},{20,16},{24,28},{28,24},{1,5},{5... | collective-permute-start | bytes 239624 | tf_op jit(solution)/shard_map/ppermute | solution.py:32
  5.8 0.2 %collective-permute-start.3 = (bf16[24,1664]{1,0:T(8,128)(2,1)S(1)}, bf16[24,1664]{1,0:T(8,128)(2,1)S(1)}, u32[]{:S(2)}, u32[]{:S(2)}) collective-permute-start(bf16[24,1664]{1,0:T(8,128)(2,1)S(1)} %get-tuple-element.14.own_ref), channel_id=1, source_target_pairs={{0,16},{4,8},{8,4},{12,28},{16,0},{20,24},{24,20},{28,12},{1,17},{... | collective-permute-start | bytes 239624 | tf_op jit(solution)/shard_map/ppermute | solution.py:32
  6.0 2.5 %collective-permute-start.4 = (bf16[4,3072]{1,0:T(4,128)(2,1)S(1)}, bf16[4,3072]{1,0:T(4,128)(2,1)S(1)}, u32[]{:S(2)}, u32[]{:S(2)}) collective-permute-start(bf16[4,3072]{1,0:T(4,128)(2,1)S(1)} %get-tuple-element.16.refs_0_), channel_id=1, source_target_pairs={{0,3},{1,2},{2,1},{3,0},{16,18},{17,19},{18,16},{19,17},{4,7},{5,6... | collective-permute-start | bytes 73736 | tf_op jit(solution)/shard_map/ppermute | solution.py:310
  8.5 0.0 collective-permute-done.both_ref
  8.5 0.5 %collective-permute-start.5 = (bf16[4,3072]{1,0:T(4,128)(2,1)S(1)}, bf16[4,3072]{1,0:T(4,128)(2,1)S(1)}, u32[]{:S(2)}, u32[]{:S(2)}) collective-permute-start(bf16[4,3072]{1,0:T(4,128)(2,1)S(1)} %get-tuple-element.16.refs_0_), channel_id=1, source_target_pairs={{0,1},{1,0},{2,3},{3,2},{4,5},{5,4},{6,7},{7,6},{8,9},{9,8},{10,11... | collective-permute-start | bytes 73736 | tf_op jit(solution)/shard_map/ppermute | solution.py:311
  9.0 0.0 copy-done.1
  9.0 0.1 shard_map.74.refs_1_
  9.1 0.0 collective-permute-done.1.both_ref
  9.1 0.1 shard_map.75.refs_2_
  9.3 2.4 %all-gather = bf16[144,3072]{1,0:T(8,128)(2,1)S(1)} all-gather(bf16[72,3072]{1,0:T(8,128)(2,1)S(1)} %shard_map.76), channel_id=2, replica_groups=mesh['ta'=2,'ha'=4,'wa'=4] {'ta'}, dimensions={0}, use_global_device_ids=true | all-gather | bytes 1327104 | tf_op jit(solution)/shard_map/all_gather | solution.py:317
  11.7 0.0 collective-permute-done.4.refs_2_
  11.7 0.6 %collective-permute-done.5.refs_3_ = bf16[4,3072]{1,0:T(4,128)(2,1)S(1)} collective-permute-done((bf16[4,3072]{1,0:T(4,128)(2,1)S(1)}, bf16[4,3072]{1,0:T(4,128)(2,1)S(1)}, u32[]{:S(2)}, u32[]{:S(2)}) %collective-permute-start.5) | collective-permute-done | bytes 24608 | tf_op jit(solution)/shard_map/ppermute | solution.py:311
  12.3 0.0 collective-permute-done.2.refs_0_
  12.3 0.0 collective-permute-done.3.refs_1_
  12.3 0.0 copy-start
  12.3 0.6 %shard_map.77 = (bf16[24,1664]{1,0:T(8,128)(2,1)S(1)}, bf16[24,1664]{1,0:T(8,128)(2,1)S(1)}, bf16[4,3072]{1,0:T(4,128)(2,1)S(1)}, bf16[4,3072]{1,0:T(4,128)(2,1)S(1)}) custom-call(bf16[2,72,3072]{2,1,0:T(8,128)(2,1)S(1)} %bitcast.8, bf16[24,1664]{1,0:T(8,128)(2,1)S(1)} %collective-permute-done.2.refs_0_, ...), custom_call_target="tpu_custom_call" | custom-call | bytes 1093632 | tf_op jit(solution)/shard_map/pallas_call | solution.py:52
  12.9 2.8 %collective-permute-start.7 = (bf16[24,1664]{1,0:T(8,128)(2,1)S(1)}, bf16[24,1664]{1,0:T(8,128)(2,1)S(1)}, u32[]{:S(2)}, u32[]{:S(2)}) collective-permute-start(bf16[24,1664]{1,0:T(8,128)(2,1)S(1)} %get-tuple-element.21), channel_id=1, source_target_pairs={{0,4},{4,0},{8,12},{12,8},{16,20},{20,16},{24,28},{28,24},{1,5},{5... | collective-permute-start | bytes 239624 | tf_op jit(solution)/shard_map/ppermute | solution.py:32
  15.7 0.0 collective-permute-start.8
  15.7 0.5 %collective-permute-start.6 = (bf16[4,3072]{1,0:T(4,128)(2,1)S(1)}, bf16[4,3072]{1,0:T(4,128)(2,1)S(1)}, u32[]{:S(2)}, u32[]{:S(2)}) collective-permute-start(bf16[4,3072]{1,0:T(4,128)(2,1)S(1)} %get-tuple-element.17.refs_1_), channel_id=1, source_target_pairs={{0,16},{16,0},{1,17},{17,1},{2,18},{18,2},{3,19},{19,3},{4,20},{20... | collective-permute-start | bytes 73736 | tf_op jit(solution)/shard_map/ppermute | solution.py:42
  16.3 0.8 %collective-permute-done.6.refs_3_ = bf16[4,3072]{1,0:T(4,128)(2,1)S(1)} collective-permute-done((bf16[4,3072]{1,0:T(4,128)(2,1)S(1)}, bf16[4,3072]{1,0:T(4,128)(2,1)S(1)}, u32[]{:S(2)}, u32[]{:S(2)}) %collective-permute-start.6) | collective-permute-done | bytes 24608 | tf_op jit(solution)/shard_map/ppermute | solution.py:42
  17.1 0.0 copy-done
  17.1 0.8 %shard_map.78 = (f32[24,1536]{1,0:T(8,128)S(1)}, f32[24,128]{1,0:T(8,128)S(1)}) custom-call(bf16[24,1664]{1,0:T(8,128)(2,1)S(1)} %get-tuple-element.14.own_ref, bf16[2,72,3072]{2,1,0:T(8,128)(2,1)S(1)} %bitcast.9, bf16[48,1536]{1,0:T(8,128)(2,1)S(1)} %bitcast.10, f32[1,128]{1,0:T(1,128)S(1)} %bitcast.14, bf16[4,3072]{1,0:T(4,128)(2,1)S(1)} %get-tuple-element.16.refs_0_, ...), custom_call_target="tpu_custom_call" | custom-call | bytes 1210880 | tf_op jit(solution)/shard_map/pallas_call | solution.py:52
  17.9 1.0 %collective-permute-done.7.refs_0_ = bf16[24,1664]{1,0:T(8,128)(2,1)S(1)} collective-permute-done((bf16[24,1664]{1,0:T(8,128)(2,1)S(1)}, bf16[24,1664]{1,0:T(8,128)(2,1)S(1)}, u32[]{:S(2)}, u32[]{:S(2)}) %collective-permute-start.7) | collective-permute-done | bytes 79904 | tf_op jit(solution)/shard_map/ppermute | solution.py:32
  18.9 0.0 collective-permute-done.8.refs_1_
  18.9 0.8 %shard_map.79 = bf16[24,1536]{1,0:T(8,128)(2,1)} custom-call(f32[24,1536]{1,0:T(8,128)S(1)} %get-tuple-element.19.total_ref, f32[24,128]{1,0:T(8,128)S(1)} %get-tuple-element.20.sum_ref, bf16[24,1664]{1,0:T(8,128)(2,1)S(1)} %collective-permute-done.7.refs_0_, bf16[24,1664]{1,0:T(8,128)(2,1)S(1)} %collective-permute-done.8.refs_1_), custom_call_target="tpu_custom_call" | custom-call | tf_op jit(solution)/shard_map/pallas_call | solution.py:277
  (1 shorter events, 0.0 us)
Async XLA Ops:
  0.0 8.5 %collective-permute-start = (bf16[48,1536]{1,0:T(8,128)(2,1)}, bf16[48,1536]{1,0:T(8,128)(2,1)S(1)}, u32[]{:S(2)}, u32[]{:S(2)}) collective-permute-start(bf16[48,1536]{1,0:T(8,128)(2,1)} %bitcast.15), channel_id=1, source_target_pairs={{0,1},{1,0},{2,3},{3,2},{16,17},{17,16},{18,19},{19,18},{4,5},{5,4... | collective-permute-start | bytes 442376 | tf_op jit(solution)/shard_map/ppermute | solution.py:32
  3.0 6.1 %collective-permute-start.1 = (bf16[48,1536]{1,0:T(8,128)(2,1)}, bf16[48,1536]{1,0:T(8,128)(2,1)S(1)}, u32[]{:S(2)}, u32[]{:S(2)}) collective-permute-start(bf16[48,1536]{1,0:T(8,128)(2,1)} %bitcast.16), channel_id=1, source_target_pairs={{0,16},{1,2},{2,1},{3,19},{16,0},{17,18},{18,17},{19,3},{4,20},{5,... | collective-permute-start | bytes 442376 | tf_op jit(solution)/shard_map/ppermute | solution.py:32
  4.2 4.8 %copy-start.1 = (f32[128]{0:T(128)S(1)}, f32[128]{0:T(128)}, u32[]{:S(2)}) copy-start(f32[128]{0:T(128)} %param.12) | copy-start | bytes 1540
  4.2 8.1 %collective-permute-start.2 = (bf16[24,1664]{1,0:T(8,128)(2,1)S(1)}, bf16[24,1664]{1,0:T(8,128)(2,1)S(1)}, u32[]{:S(2)}, u32[]{:S(2)}) collective-permute-start(bf16[24,1664]{1,0:T(8,128)(2,1)S(1)} %get-tuple-element.14.own_ref), channel_id=1, source_target_pairs={{0,4},{4,0},{8,12},{12,8},{16,20},{20,16},{24,28},{28,24},{1,5},{5... | collective-permute-start | bytes 239624 | tf_op jit(solution)/shard_map/ppermute | solution.py:32
  5.8 6.5 %collective-permute-start.3 = (bf16[24,1664]{1,0:T(8,128)(2,1)S(1)}, bf16[24,1664]{1,0:T(8,128)(2,1)S(1)}, u32[]{:S(2)}, u32[]{:S(2)}) collective-permute-start(bf16[24,1664]{1,0:T(8,128)(2,1)S(1)} %get-tuple-element.14.own_ref), channel_id=1, source_target_pairs={{0,16},{4,8},{8,4},{12,28},{16,0},{20,24},{24,20},{28,12},{1,17},{... | collective-permute-start | bytes 239624 | tf_op jit(solution)/shard_map/ppermute | solution.py:32
  6.0 5.8 %collective-permute-start.4 = (bf16[4,3072]{1,0:T(4,128)(2,1)S(1)}, bf16[4,3072]{1,0:T(4,128)(2,1)S(1)}, u32[]{:S(2)}, u32[]{:S(2)}) collective-permute-start(bf16[4,3072]{1,0:T(4,128)(2,1)S(1)} %get-tuple-element.16.refs_0_), channel_id=1, source_target_pairs={{0,3},{1,2},{2,1},{3,0},{16,18},{17,19},{18,16},{19,17},{4,7},{5,6... | collective-permute-start | bytes 73736 | tf_op jit(solution)/shard_map/ppermute | solution.py:310
  8.5 3.8 %collective-permute-start.5 = (bf16[4,3072]{1,0:T(4,128)(2,1)S(1)}, bf16[4,3072]{1,0:T(4,128)(2,1)S(1)}, u32[]{:S(2)}, u32[]{:S(2)}) collective-permute-start(bf16[4,3072]{1,0:T(4,128)(2,1)S(1)} %get-tuple-element.16.refs_0_), channel_id=1, source_target_pairs={{0,1},{1,0},{2,3},{3,2},{4,5},{5,4},{6,7},{7,6},{8,9},{9,8},{10,11... | collective-permute-start | bytes 73736 | tf_op jit(solution)/shard_map/ppermute | solution.py:311
  12.3 4.8 %copy-start = (bf16[1,1,1,2,24,1536]{5,4,3,2,1,0:T(8,128)(2,1)S(1)}, bf16[1,1,1,2,24,1536]{5,4,3,2,1,0:T(8,128)(2,1)}, u32[]{:S(2)}) copy-start(bf16[1,1,1,2,24,1536]{5,4,3,2,1,0:T(8,128)(2,1)} %param.8) | copy-start | bytes 442372
  12.9 6.0 %collective-permute-start.7 = (bf16[24,1664]{1,0:T(8,128)(2,1)S(1)}, bf16[24,1664]{1,0:T(8,128)(2,1)S(1)}, u32[]{:S(2)}, u32[]{:S(2)}) collective-permute-start(bf16[24,1664]{1,0:T(8,128)(2,1)S(1)} %get-tuple-element.21), channel_id=1, source_target_pairs={{0,4},{4,0},{8,12},{12,8},{16,20},{20,16},{24,28},{28,24},{1,5},{5... | collective-permute-start | bytes 239624 | tf_op jit(solution)/shard_map/ppermute | solution.py:32
  15.7 3.2 %collective-permute-start.8 = (bf16[24,1664]{1,0:T(8,128)(2,1)S(1)}, bf16[24,1664]{1,0:T(8,128)(2,1)S(1)}, u32[]{:S(2)}, u32[]{:S(2)}) collective-permute-start(bf16[24,1664]{1,0:T(8,128)(2,1)S(1)} %get-tuple-element.22), channel_id=1, source_target_pairs={{0,16},{4,8},{8,4},{12,28},{16,0},{20,24},{24,20},{28,12},{1,17},{... | collective-permute-start | bytes 239624 | tf_op jit(solution)/shard_map/ppermute | solution.py:32
  15.7 1.4 %collective-permute-start.6 = (bf16[4,3072]{1,0:T(4,128)(2,1)S(1)}, bf16[4,3072]{1,0:T(4,128)(2,1)S(1)}, u32[]{:S(2)}, u32[]{:S(2)}) collective-permute-start(bf16[4,3072]{1,0:T(4,128)(2,1)S(1)} %get-tuple-element.17.refs_1_), channel_id=1, source_target_pairs={{0,16},{16,0},{1,17},{17,1},{2,18},{18,2},{3,19},{19,3},{4,20},{20... | collective-permute-start | bytes 73736 | tf_op jit(solution)/shard_map/ppermute | solution.py:42

commit v6 on v4

--- a/solution.py
+++ b/solution.py
@@ -7,6 +7,7 @@
 
 EPS = 1e-06
 LANES = 128
+WORD_ROWS = 8
 IN_VMEM = pl.BlockSpec(memory_space=pltpu.VMEM)
 IN_SMEM = pl.BlockSpec(memory_space=pltpu.SMEM)
 
@@ -158,10 +159,11 @@
         both = [head_normed(both[:tile], k_gain, heads), both[tile:]]
         tile_ref[...] = jnp.concatenate(both, axis=1).astype(jnp.bfloat16)
         text_keys = head_normed(text_ref[0].astype(jnp.float32), k_gain, heads)
-        both = [text_keys, text_ref[1].astype(jnp.float32)]
-        words_ref[...] = jnp.concatenate(both, axis=1).astype(jnp.bfloat16)
-
-    shapes = [(tile, width + LANES), (tile, 2 * width), (tokens, 2 * width)]
+        both = jnp.concatenate([text_keys, text_ref[1].astype(jnp.float32)], axis=1)
+        blank = jnp.zeros((WORD_ROWS - tokens, 2 * width), jnp.float32)
+        words_ref[...] = jnp.concatenate([both, blank], axis=0).astype(jnp.bfloat16)
+
+    shapes = [(tile, width + LANES), (tile, 2 * width), (WORD_ROWS, 2 * width)]
     return pl.pallas_call(
         body,
         out_shape=[pltpu.VMEM(shape, jnp.bfloat16) for shape in shapes],
@@ -170,17 +172,24 @@
     )(queries, stale, text, q_gain, k_gain, pattern)
 
 
-def norm_raw(both, k_gain, tile, flops):
+def norm_raw(both, k_gain, tile):
     width = both.shape[1]
     heads = width // k_gain.shape[-1]
-
-    def body(both_ref, gain_ref, out_ref):
+    tokens = both.shape[0] // 2 - tile
+
+    def body(both_ref, gain_ref, out_ref, *words_refs):
         both = both_ref[...].astype(jnp.float32)
         keys = head_normed(both[:tile], gain_ref[...], heads)
-        out_ref[...] = jnp.concatenate([keys, both[tile:]], axis=1).astype(jnp.bfloat16)
-
-    shape = jax.ShapeDtypeStruct((tile, 2 * width), jnp.bfloat16)
-    return call(body, [shape], both, k_gain, flops=flops)[0]
+        out_ref[...] = jnp.concatenate([keys, both[tile : 2 * tile]], axis=1).astype(jnp.bfloat16)
+        for r in words_refs:
+            text = both[2 * tile :]
+            keys = head_normed(text[:tokens], gain_ref[...], heads)
+            r[...] = jnp.concatenate([keys, text[tokens:]], axis=1).astype(jnp.bfloat16)
+
+    shapes = [jax.ShapeDtypeStruct((tile, 2 * width), jnp.bfloat16)]
+    if tokens:
+        shapes.append(jax.ShapeDtypeStruct((tokens, 2 * width), jnp.bfloat16))
+    return call(body, shapes, both, k_gain)
 
 
 def join_line(packs, width):
@@ -192,17 +201,13 @@
     return call(body, [shape], *packs)[0]
 
 
-def attend_partners(around, sent, far, tile, line, hd):
+def attend_partners(around, sent, tile, line, hd):
     places, rows, width = around.shape
     width //= 2
     heads = width // hd
 
     def body(around_ref, *refs):
-        sent_refs, refs = refs[: len(sent)], refs[len(sent) :]
-        far_refs, refs = refs[: len(far)], refs[len(far) :]
-        back_refs, on_refs = refs[: len(sent)], refs[len(sent) :]
-        for r, on in zip(far_refs, on_refs, strict=True):
-            on[...] = r[...]
+        sent_refs, back_refs = refs[: len(sent)], refs[len(sent) :]
         blocks = [r[...].astype(jnp.float32) for r in sent_refs]
         masks = [
             key_masks(block[i : i + 1, width:], places, line, tile, rows)
@@ -224,22 +229,24 @@
             back[...] = whole[i * tile : (i + 1) * tile].astype(jnp.bfloat16)
 
     shapes = [jax.ShapeDtypeStruct((tile, width + LANES), jnp.bfloat16)] * len(sent)
-    shapes += [jax.ShapeDtypeStruct(x.shape, x.dtype) for x in far]
-    outs = call(body, shapes, around, *sent, *far)
-    return outs[: len(sent)], outs[len(sent) :]
-
-
-def attend_own(own, around, current, words, k_gain, tile, line, reader):
+    return call(body, shapes, around, *sent)
+
+
+def attend_own(own, around, current, words, near, far, tokens, k_gain, tile, line, reader):
     places, rows, width = around.shape
     width //= 2
     heads = width // k_gain.shape[-1]
 
-    def body(own_ref, around_ref, current_ref, gain_ref, *refs):
-        total_ref, sum_ref = refs[-2:]
+    def body(own_ref, around_ref, current_ref, gain_ref, words_ref, *refs):
+        near_refs, refs = refs[: len(near)], refs[len(near) :]
+        far_refs, (total_ref, sum_ref, *on_refs) = refs[: len(far)], refs[len(far) :]
+        for r, on in zip(far_refs, on_refs, strict=True):
+            on[...] = r[...].astype(jnp.float32)[:tokens].astype(jnp.bfloat16)
         here = current_ref[...].astype(jnp.float32)
         keys = head_normed(here[:tile], gain_ref[...], heads)
         sure = [jnp.concatenate([keys, here[tile:]], axis=1)]
-        sure += [r[...].astype(jnp.float32) for r in refs[:-2]]
+        sure.append(words_ref[...].astype(jnp.float32)[:tokens])
+        sure += [r[...].astype(jnp.float32) for r in near_refs]
         sure = jnp.concatenate(sure, axis=0).astype(jnp.bfloat16)
         flags = own_ref[:, width:].astype(jnp.float32)[reader : reader + 1]
         masks = key_masks(flags, places, line, tile, rows)
@@ -254,7 +261,27 @@
         jax.ShapeDtypeStruct((tile, width), jnp.float32),
         jax.ShapeDtypeStruct((tile, LANES), jnp.float32),
     ]
-    return call(body, shapes, own, around, current, k_gain, *words)
+    shapes += [jax.ShapeDtypeStruct((tokens, x.shape[1]), x.dtype) for x in far]
+    outs = call(body, shapes, own, around, current, k_gain, words, *near, *far)
+    return outs[0], outs[1], outs[2:]
+
+
+def attend_words(own, words, total, weight, hd):
+    tile, width = total.shape
+    heads = width // hd
+
+    def body(own_ref, total_ref, sum_ref, *refs):
+        total_out, sum_out = refs[-2:]
+        both = jnp.concatenate([r[...].astype(jnp.float32) for r in refs[:-2]], axis=0)
+        both = both.astype(jnp.bfloat16)
+        totals, weights = attention(
+            own_ref[:, :width], [(both[:, :width], both[:, width:], None)], heads
+        )
+        total_out[...] = total_ref[...] + jnp.concatenate(totals, axis=1)
+        sum_out[...] = sum_ref[...] + in_lanes(weights)
+
+    shapes = [jax.ShapeDtypeStruct(x.shape, x.dtype) for x in (total, weight)]
+    return call(body, shapes, own, total, weight, *words, flops=int(3e8))
 
 
 def combine(total, weight, backs, hd):
@@ -292,7 +319,8 @@
     sizes = [lax.axis_size(a) for a in axes]
     parities_h, parities_w = parities(sizes[1]), parities(sizes[2])
 
-    raw = [norm_raw(swap_along(stale, "wa", p), k_gain, tile, (int(1e9), int(3e8))[p]) for p in parities_w]
+    tokens = text_kv.shape[1]
+    raw = [norm_raw(swap_along(stale, "wa", p), k_gain, tile)[0] for p in parities_w]
     own, mine, words = prepare(
         queries.reshape(tile, width),
         stale,
@@ -304,22 +332,24 @@
         sizes,
     )
     sent = [swap_along(own, "ha", p) for p in parities_h]
-    others = []
+    near, far = [], []
     if sizes[2] == 4 and sizes[0] % 2 == 0:
         pairs = [(t * 4 + i, t * 4 + (i ^ (2 + t % 2))) for t in range(sizes[0]) for i in range(4)]
-        others.append(lax.ppermute(words, ("ta", "wa"), pairs))
-        others.append(lax.ppermute(words, "wa", [(i, i ^ 1) for i in range(4)]))
-        words = [words]
+        far.append(lax.ppermute(words, ("ta", "wa"), pairs))
+        near.append(lax.ppermute(words[:tokens], "wa", [(i, i ^ 1) for i in range(4)]))
     else:
-        words = [lax.all_gather(words, "wa", axis=0, tiled=True)]
+        words = lax.all_gather(words[:tokens], "wa", axis=0, tiled=True)
+        tokens = words.shape[0]
     packs = [mine] + raw
     line = len(packs)
     around = lax.all_gather(join_line(packs, width), "ta")
-    answers, others = attend_partners(around, sent, others, tile, line, hd)
+    answers = attend_partners(around, sent, tile, line, hd)
     backs = [swap_along(x, "ha", p) for x, p in zip(answers, parities_h, strict=True)]
-    if others:
-        words += [*others, swap_ta(others[0], 0)]
-    total, weight = attend_own(own, around, current, words, k_gain, tile, line, len(parities_h))
+    total, weight, far = attend_own(
+        own, around, current, words, [], far, tokens, k_gain, tile, line, len(parities_h)
+    )
+    for there in far:
+        total, weight = attend_words(own, [there, swap_ta(there, 0), *near], total, weight, hd)
     result = combine(total, weight, backs, hd)
     return result.reshape(1, 1, 1, tile, width)
 

time: 19.9 us -> 20 us (level)
  waiting for transfers between devices: 2.1 us -> 1.71 us
  Pallas kernels: 3.72 us -> 4 us
    ppermute x2, waiting for transfers between devices: 0.37 us -> 1.69 us  [the longest x1 1.69 us: shards(): lax.ppermute(words[:tokens], 'wa', [(i, i ^ 1) for i in range(4)])]
    ppermute x6, waiting for transfers between devices: 0.89 us -> 0.02 us  [swap_along(): return lax.ppermute(values, ('ta', axis), pairs)]
    ppermute x1, waiting for transfers between devices: 0.85 us -> 0.01 us  [swap_ta(): return lax.ppermute(values, 'ta', pairs)]
    ppermute x2, starting transfers between devices: 3.07 us -> 3.48 us  [the longest x1 2.36 us: shards(): far.append(lax.ppermute(words, ('ta', 'wa'), pairs))]
    pallas_call x5 -> x6, Pallas kernels: 1.72 us -> 2 us  [call(): pl.pallas_call(body, out_shape=outs, in_specs=[IN_VMEM] * len(operands),...]
    ppermute x1, starting transfers between devices: 0.51 us -> 0.27 us  [swap_ta(): return lax.ppermute(values, 'ta', pairs)]
  transfers between devices with their start and end apart: 9 -> 9, of which waited for: 3 -> 1; matrix products, arithmetic and copies ran while one was open for 0% -> 0% of each run, Pallas kernels for 11% -> 16%
where the time goes in v6:
time: 20 us; the launch traced here: 19.9 us
  starting transfers between devices  11.6 us (58%)
  Pallas kernels  4 us (20%)
  blocking collectives  2.44 us (12%)
  waiting for transfers between devices  1.71 us (9%)
    ppermute x6, starting transfers between devices, swap_along(): return lax.ppermute(values, ('ta', axis), pairs)  7.86 us
    all_gather x1, blocking collectives, shards(): around = lax.all_gather(join_line(packs, width), 'ta')  2.44 us
    ppermute x1, starting transfers between devices, shards(): far.append(lax.ppermute(words, ('ta', 'wa'), pairs))  2.36 us
    pallas_call x6, Pallas kernels, call(): pl.pallas_call(body, out_shape=outs, in_specs=[IN_VMEM] * len(operands),...  2 us
    ppermute x1, waiting for transfers between devices, shards(): lax.ppermute(words[:tokens], 'wa', [(i, i ^ 1) for i in range(4)])  1.69 us
    pallas_call x1, Pallas kernels, prepare(): pl.pallas_call(body, out_shape=[pltpu.VMEM(shape, jnp.bfloat16) for shape...  1.16 us
    ppermute x1, starting transfers between devices, shards(): lax.ppermute(words[:tokens], 'wa', [(i, i ^ 1) for i in range(4)])  1.12 us
    pallas_call x1, Pallas kernels, combine(): pl.pallas_call(body, out_shape=jax.ShapeDtypeStruct((tile, width), jnp.bf...  0.84 us
  transfers between devices with their start and end apart: 9, of which 1 were waited for; matrix products, arithmetic and copies ran while one was open for 0% of the time, Pallas kernels for 16%

profile of v6, /device:TPU:0, one launch (start us, length us, event | category | flops | bytes accessed | tf_op | source)
XLA Modules:
  0.0 19.9 jit_solution(17029985041451013625)
XLA Ops:
  0.0 3.0 %collective-permute-start = (bf16[48,1536]{1,0:T(8,128)(2,1)}, bf16[48,1536]{1,0:T(8,128)(2,1)S(1)}, u32[]{:S(2)}, u32[]{:S(2)}) collective-permute-start(bf16[48,1536]{1,0:T(8,128)(2,1)} %bitcast.15), channel_id=1, source_target_pairs={{0,1},{1,0},{2,3},{3,2},{16,17},{17,16},{18,19},{19,18},{4,5},{5,4... | collective-permute-start | bytes 442376 | tf_op jit(solution)/shard_map/ppermute | solution.py:33
  3.0 0.0 collective-permute-start.1
  3.0 1.2 %shard_map.73 = (bf16[24,1664]{1,0:T(8,128)(2,1)S(1)}, bf16[24,3072]{1,0:T(8,128)(2,1)S(1)}, bf16[8,3072]{1,0:T(8,128)(2,1)S(1)}) custom-call(bf16[24,1536]{1,0:T(8,128)(2,1)} %bitcast.18, bf16[48,1536]{1,0:T(8,128)(2,1)} %bitcast.17, bf16[2,4,1536]{2,1,0:T(4,128)(2,1)} %text_ref.1, f32[1,128]{1,0:T(1,128)} %bitcast.19, f32[1,128]{1,0:T(1,128)} %bitcast.11, ...), custom_call_target="tpu_custom_call" | custom-call | tf_op jit(solution)/shard_map/pallas_call | solution.py:167
  4.2 0.0 copy-start.1
  4.2 1.6 %collective-permute-start.5 = (bf16[24,1664]{1,0:T(8,128)(2,1)S(1)}, bf16[24,1664]{1,0:T(8,128)(2,1)S(1)}, u32[]{:S(2)}, u32[]{:S(2)}) collective-permute-start(bf16[24,1664]{1,0:T(8,128)(2,1)S(1)} %get-tuple-element.15.own_ref), channel_id=1, source_target_pairs={{0,4},{4,0},{8,12},{12,8},{16,20},{20,16},{24,28},{28,24},{1,5},{5... | collective-permute-start | bytes 239624 | tf_op jit(solution)/shard_map/ppermute | solution.py:33
  5.8 0.2 %collective-permute-start.6 = (bf16[24,1664]{1,0:T(8,128)(2,1)S(1)}, bf16[24,1664]{1,0:T(8,128)(2,1)S(1)}, u32[]{:S(2)}, u32[]{:S(2)}) collective-permute-start(bf16[24,1664]{1,0:T(8,128)(2,1)S(1)} %get-tuple-element.15.own_ref), channel_id=1, source_target_pairs={{0,16},{4,8},{8,4},{12,28},{16,0},{20,24},{24,20},{28,12},{1,17},{... | collective-permute-start | bytes 239624 | tf_op jit(solution)/shard_map/ppermute | solution.py:33
  6.0 2.4 %collective-permute-start.2 = (bf16[8,3072]{1,0:T(8,128)(2,1)S(1)}, bf16[8,3072]{1,0:T(8,128)(2,1)S(1)}, u32[]{:S(2)}, u32[]{:S(2)}) collective-permute-start(bf16[8,3072]{1,0:T(8,128)(2,1)S(1)} %get-tuple-element.17.words_ref), channel_id=1, source_target_pairs={{0,2},{1,3},{2,0},{3,1},{16,19},{17,18},{18,17},{19,16},{4,6},{5,7... | collective-permute-start | bytes 147464 | tf_op jit(solution)/shard_map/ppermute | solution.py:338
  8.4 0.0 collective-permute-done.both_ref
  8.4 0.0 copy-done.1
  8.4 0.1 shard_map.74.refs_1_
  8.5 0.0 collective-permute-done.1.both_ref
  8.5 0.1 shard_map.75.refs_2_
  8.7 2.4 %all-gather = bf16[144,3072]{1,0:T(8,128)(2,1)S(1)} all-gather(bf16[72,3072]{1,0:T(8,128)(2,1)S(1)} %shard_map.76), channel_id=2, replica_groups=mesh['ta'=2,'ha'=4,'wa'=4] {'ta'}, dimensions={0}, use_global_device_ids=true | all-gather | bytes 1327104 | tf_op jit(solution)/shard_map/all_gather | solution.py:345
  11.1 0.0 collective-permute-done.5.refs_0_
  11.1 0.0 collective-permute-done.6.refs_1_
  11.1 0.0 copy-start
  11.1 0.6 %shard_map.79 = (bf16[24,1664]{1,0:T(8,128)(2,1)S(1)}, bf16[24,1664]{1,0:T(8,128)(2,1)S(1)}) custom-call(bf16[2,72,3072]{2,1,0:T(8,128)(2,1)S(1)} %bitcast.8, bf16[24,1664]{1,0:T(8,128)(2,1)S(1)} %collective-permute-done.5.refs_0_, bf16[24,1664]{1,0:T(8,128)(2,1)S(1)} %collective-permute-done.6.refs_1_), custom_call_target="tpu_custom_call" | custom-call | bytes 1044480 | tf_op jit(solution)/shard_map/pallas_call | solution.py:53
  11.8 3.0 %collective-permute-start.7 = (bf16[24,1664]{1,0:T(8,128)(2,1)S(1)}, bf16[24,1664]{1,0:T(8,128)(2,1)S(1)}, u32[]{:S(2)}, u32[]{:S(2)}) collective-permute-start(bf16[24,1664]{1,0:T(8,128)(2,1)S(1)} %get-tuple-element.23), channel_id=1, source_target_pairs={{0,4},{4,0},{8,12},{12,8},{16,20},{20,16},{24,28},{28,24},{1,5},{5... | collective-permute-start | bytes 239624 | tf_op jit(solution)/shard_map/ppermute | solution.py:33
  14.8 0.0 collective-permute-start.8
  14.8 1.1 %collective-permute-start.4 = (bf16[4,3072]{1,0:T(4,128)(2,1)S(1)}, bf16[4,3072]{1,0:T(4,128)(2,1)S(1)}, u32[]{:S(2)}, u32[]{:S(2)}) collective-permute-start(bf16[4,3072]{1,0:T(4,128)(2,1)S(1)} %slice.3), channel_id=1, source_target_pairs={{0,1},{1,0},{2,3},{3,2},{4,5},{5,4},{6,7},{7,6},{8,9},{9,8},{10,11... | collective-permute-start | bytes 73736 | tf_op jit(solution)/shard_map/ppermute | solution.py:339
  15.9 0.0 collective-permute-done.2.refs_0_
  15.9 0.0 copy-done
  15.9 0.8 %shard_map.77 = (f32[24,1536]{1,0:T(8,128)S(1)}, f32[24,128]{1,0:T(8,128)S(1)}, bf16[4,3072]{1,0:T(4,128)(2,1)S(1)}) custom-call(bf16[24,1664]{1,0:T(8,128)(2,1)S(1)} %get-tuple-element.15.own_ref, bf16[2,72,3072]{2,1,0:T(8,128)(2,1)S(1)} %bitcast.9, bf16[48,1536]{1,0:T(8,128)(2,1)S(1)} %bitcast.10, f32[1,128]{1,0:T(1,128)S(1)} %bitcast.14, ...), custom_call_target="tpu_custom_call" | custom-call | bytes 1210880 | tf_op jit(solution)/shard_map/pallas_call | solution.py:53
  16.7 0.3 %collective-permute-start.3 = (bf16[4,3072]{1,0:T(4,128)(2,1)S(1)}, bf16[4,3072]{1,0:T(4,128)(2,1)S(1)}, u32[]{:S(2)}, u32[]{:S(2)}) collective-permute-start(bf16[4,3072]{1,0:T(4,128)(2,1)S(1)} %get-tuple-element.20.refs_0_), channel_id=1, source_target_pairs={{0,16},{16,0},{1,17},{17,1},{2,18},{18,2},{3,19},{19,3},{4,20},{20... | collective-permute-start | bytes 73736 | tf_op jit(solution)/shard_map/ppermute | solution.py:43
  17.0 1.7 %collective-permute-done.4.refs_2_ = bf16[4,3072]{1,0:T(4,128)(2,1)S(1)} collective-permute-done((bf16[4,3072]{1,0:T(4,128)(2,1)S(1)}, bf16[4,3072]{1,0:T(4,128)(2,1)S(1)}, u32[]{:S(2)}, u32[]{:S(2)}) %collective-permute-start.4) | collective-permute-done | bytes 24608 | tf_op jit(solution)/shard_map/ppermute | solution.py:339
  18.7 0.0 collective-permute-done.3.refs_1_
  18.7 0.3 %shard_map.78 = (f32[24,1536]{1,0:T(8,128)S(1)}, f32[24,128]{1,0:T(8,128)S(1)}) custom-call(bf16[24,1664]{1,0:T(8,128)(2,1)S(1)} %get-tuple-element.15.own_ref, f32[24,1536]{1,0:T(8,128)S(1)} %get-tuple-element.18.total_ref, f32[24,128]{1,0:T(8,128)S(1)} %get-tuple-element.19.sum_ref, bf16[4,3072]{1,0:T(4,128)(2,1)S(1)} %get-tuple-element.20.refs_0_, ...), custom_call_target="tpu_custom_call" | custom-call | flops 300000000 | bytes 313344 | tf_op jit(solution)/shard_map/pallas_call | solution.py:53
  19.0 0.0 collective-permute-done.7.refs_0_
  19.0 0.0 collective-permute-done.8.refs_1_
  19.0 0.8 %shard_map.80 = bf16[24,1536]{1,0:T(8,128)(2,1)} custom-call(f32[24,1536]{1,0:T(8,128)S(1)} %get-tuple-element.21.total_ref, f32[24,128]{1,0:T(8,128)S(1)} %get-tuple-element.22.sum_ref, bf16[24,1664]{1,0:T(8,128)(2,1)S(1)} %collective-permute-done.7.refs_0_, bf16[24,1664]{1,0:T(8,128)(2,1)S(1)} %collective-permute-done.8.refs_1_), custom_call_target="tpu_custom_call" | custom-call | tf_op jit(solution)/shard_map/pallas_call | solution.py:304
  (2 shorter events, 0.0 us)
Async XLA Ops:
  0.0 8.4 %collective-permute-start = (bf16[48,1536]{1,0:T(8,128)(2,1)}, bf16[48,1536]{1,0:T(8,128)(2,1)S(1)}, u32[]{:S(2)}, u32[]{:S(2)}) collective-permute-start(bf16[48,1536]{1,0:T(8,128)(2,1)} %bitcast.15), channel_id=1, source_target_pairs={{0,1},{1,0},{2,3},{3,2},{16,17},{17,16},{18,19},{19,18},{4,5},{5,4... | collective-permute-start | bytes 442376 | tf_op jit(solution)/shard_map/ppermute | solution.py:33
  3.0 5.5 %collective-permute-start.1 = (bf16[48,1536]{1,0:T(8,128)(2,1)}, bf16[48,1536]{1,0:T(8,128)(2,1)S(1)}, u32[]{:S(2)}, u32[]{:S(2)}) collective-permute-start(bf16[48,1536]{1,0:T(8,128)(2,1)} %bitcast.16), channel_id=1, source_target_pairs={{0,16},{1,2},{2,1},{3,19},{16,0},{17,18},{18,17},{19,3},{4,20},{5,... | collective-permute-start | bytes 442376 | tf_op jit(solution)/shard_map/ppermute | solution.py:33
  4.2 4.2 %copy-start.1 = (f32[128]{0:T(128)S(1)}, f32[128]{0:T(128)}, u32[]{:S(2)}) copy-start(f32[128]{0:T(128)} %param.12) | copy-start | bytes 1540
  4.2 6.9 %collective-permute-start.5 = (bf16[24,1664]{1,0:T(8,128)(2,1)S(1)}, bf16[24,1664]{1,0:T(8,128)(2,1)S(1)}, u32[]{:S(2)}, u32[]{:S(2)}) collective-permute-start(bf16[24,1664]{1,0:T(8,128)(2,1)S(1)} %get-tuple-element.15.own_ref), channel_id=1, source_target_pairs={{0,4},{4,0},{8,12},{12,8},{16,20},{20,16},{24,28},{28,24},{1,5},{5... | collective-permute-start | bytes 239624 | tf_op jit(solution)/shard_map/ppermute | solution.py:33
  5.8 5.4 %collective-permute-start.6 = (bf16[24,1664]{1,0:T(8,128)(2,1)S(1)}, bf16[24,1664]{1,0:T(8,128)(2,1)S(1)}, u32[]{:S(2)}, u32[]{:S(2)}) collective-permute-start(bf16[24,1664]{1,0:T(8,128)(2,1)S(1)} %get-tuple-element.15.own_ref), channel_id=1, source_target_pairs={{0,16},{4,8},{8,4},{12,28},{16,0},{20,24},{24,20},{28,12},{1,17},{... | collective-permute-start | bytes 239624 | tf_op jit(solution)/shard_map/ppermute | solution.py:33
  6.0 9.9 %collective-permute-start.2 = (bf16[8,3072]{1,0:T(8,128)(2,1)S(1)}, bf16[8,3072]{1,0:T(8,128)(2,1)S(1)}, u32[]{:S(2)}, u32[]{:S(2)}) collective-permute-start(bf16[8,3072]{1,0:T(8,128)(2,1)S(1)} %get-tuple-element.17.words_ref), channel_id=1, source_target_pairs={{0,2},{1,3},{2,0},{3,1},{16,19},{17,18},{18,17},{19,16},{4,6},{5,7... | collective-permute-start | bytes 147464 | tf_op jit(solution)/shard_map/ppermute | solution.py:338
  11.1 4.8 %copy-start = (bf16[1,1,1,2,24,1536]{5,4,3,2,1,0:T(8,128)(2,1)S(1)}, bf16[1,1,1,2,24,1536]{5,4,3,2,1,0:T(8,128)(2,1)}, u32[]{:S(2)}) copy-start(bf16[1,1,1,2,24,1536]{5,4,3,2,1,0:T(8,128)(2,1)} %param.8) | copy-start | bytes 442372
  11.8 7.3 %collective-permute-start.7 = (bf16[24,1664]{1,0:T(8,128)(2,1)S(1)}, bf16[24,1664]{1,0:T(8,128)(2,1)S(1)}, u32[]{:S(2)}, u32[]{:S(2)}) collective-permute-start(bf16[24,1664]{1,0:T(8,128)(2,1)S(1)} %get-tuple-element.23), channel_id=1, source_target_pairs={{0,4},{4,0},{8,12},{12,8},{16,20},{20,16},{24,28},{28,24},{1,5},{5... | collective-permute-start | bytes 239624 | tf_op jit(solution)/shard_map/ppermute | solution.py:33
  14.8 4.2 %collective-permute-start.8 = (bf16[24,1664]{1,0:T(8,128)(2,1)S(1)}, bf16[24,1664]{1,0:T(8,128)(2,1)S(1)}, u32[]{:S(2)}, u32[]{:S(2)}) collective-permute-start(bf16[24,1664]{1,0:T(8,128)(2,1)S(1)} %get-tuple-element.24), channel_id=1, source_target_pairs={{0,16},{4,8},{8,4},{12,28},{16,0},{20,24},{24,20},{28,12},{1,17},{... | collective-permute-start | bytes 239624 | tf_op jit(solution)/shard_map/ppermute | solution.py:33
  14.8 3.9 %collective-permute-start.4 = (bf16[4,3072]{1,0:T(4,128)(2,1)S(1)}, bf16[4,3072]{1,0:T(4,128)(2,1)S(1)}, u32[]{:S(2)}, u32[]{:S(2)}) collective-permute-start(bf16[4,3072]{1,0:T(4,128)(2,1)S(1)} %slice.3), channel_id=1, source_target_pairs={{0,1},{1,0},{2,3},{3,2},{4,5},{5,4},{6,7},{7,6},{8,9},{9,8},{10,11... | collective-permute-start | bytes 73736 | tf_op jit(solution)/shard_map/ppermute | solution.py:339
  16.7 2.0 %collective-permute-start.3 = (bf16[4,3072]{1,0:T(4,128)(2,1)S(1)}, bf16[4,3072]{1,0:T(4,128)(2,1)S(1)}, u32[]{:S(2)}, u32[]{:S(2)}) collective-permute-start(bf16[4,3072]{1,0:T(4,128)(2,1)S(1)} %get-tuple-element.20.refs_0_), channel_id=1, source_target_pairs={{0,16},{16,0},{1,17},{17,1},{2,18},{18,2},{3,19},{19,3},{4,20},{20... | collective-permute-start | bytes 73736 | tf_op jit(solution)/shard_map/ppermute | solution.py:43
